TPU v7x, 32 devices: a whole 2x2x4 slice. The times are simulated.
32 devices in a mesh: grid: 8 (over y, x, core), dom: 4 (over z).
Axes of the slice: x: 2, y: 2, z: 4, core: 2. Of those that a mesh axis runs over, the one named last changes fastest.
Arguments:
- concentration: float32 [8, 64, 8192], P('grid', 'dom'), may hold values from -6 to 6
- diffusion: float32 [8, 64, 8192], P('grid', 'dom'), may hold values from 0.25 to 1
- velocity: float32 [4], replicated, may hold values from -1 to 1
- levels: int32 [8, 3], P('grid'), may hold values from 3 to 7, as said below
- grid_signs: int32 [8], P('grid'), may hold values from -1 to 1, as said below
- owner_list: int32 [32, 128], P(('grid', 'dom')), may hold values from 0 to 31, as said below
- slot_list: int32 [32, 128], P(('grid', 'dom')), may hold values from 0 to 63
Outputs:
- combined: float32 [8, 64, 8192], P('grid', 'dom')
Inputs may be any that keep to these rules, and one draw needn't show every extreme that they name: Each row's three levels sum to 13. `grid_signs`: each is -1 or 1. `owner_list`: at most 8 blocks of one device name the same owner; some owner is named by 8 blocks of every device.
All inputs are finite; a program needn't handle non-finite values.
Results may differ from a plain program's by a relative error of at most 0.0003.
Values sent between devices are 32-bit elements; how exact they have to be, the bound alone decides.
No kernel may reach another device: no remote copies, remote signals or barrier semaphores. Data moves between devices by JAX's collectives and lax.ppermute only.
A program may use at most 192 MiB of HBM per device.

v0:
```python
import jax
import jax.numpy as jnp
from jax import lax
from jax.sharding import PartitionSpec as P

LR = 13
LMIN = 3
TSTEPS = 2
BLK = 1024
SLOTS = 64


def extended_2(block, sides, width):
    for axis, dim in sides:
        count = lax.axis_size(axis)
        forward = [(i, i + 1) for i in range(count - 1)]
        backward = [(target, source) for source, target in forward]
        low = lax.ppermute(
            lax.slice_in_dim(block, block.shape[dim] - width, None, axis=dim), axis, forward
        )
        high = lax.ppermute(lax.slice_in_dim(block, 0, width, axis=dim), axis, backward)
        block = jnp.concatenate([low, block, high], axis=dim)
    return block


def level_table():
    level_rows = []
    for first_level in range(LMIN, LR - 2 * LMIN + 1):
        for second_level in range(LMIN, LR - first_level - LMIN + 1):
            level_rows.append((first_level, second_level, LR - first_level - second_level))
    return level_rows


def branch_index(grid_levels):
    level_rows = jnp.array(level_table(), jnp.int32)
    matching = jnp.all(grid_levels[None, :] == level_rows, axis=1)
    return jnp.sum(jnp.where(matching, jnp.arange(level_rows.shape[0], dtype=jnp.int32), 0))


def step_ahead(values, axis_num):
    length = values.shape[axis_num]
    shifted = lax.slice_in_dim(values, 1, length, axis=axis_num)
    return jnp.concatenate(
        [shifted, jnp.zeros_like(lax.slice_in_dim(values, 0, 1, axis=axis_num))], axis=axis_num
    )


def behind(values, axis_num):
    length = values.shape[axis_num]
    shifted = lax.slice_in_dim(values, 0, length - 1, axis=axis_num)
    return jnp.concatenate(
        [jnp.zeros_like(lax.slice_in_dim(values, 0, 1, axis=axis_num)), shifted], axis=axis_num
    )


def inner_terms(level_combo):

    def branch_fn(values, velocity):
        shaped = values.reshape(
            values.shape[0], 2 ** level_combo[2], 2 ** level_combo[1], 2 ** level_combo[0]
        )
        second = jnp.zeros_like(shaped)
        drift = jnp.zeros_like(shaped)
        for direction in range(3):
            axis_num = 3 - direction
            ahead_vals = step_ahead(shaped, axis_num)
            before = behind(shaped, axis_num)
            second = second + (ahead_vals - 2.0 * shaped + before)
            drift = drift + velocity[direction] * (ahead_vals - before)
        return (second.reshape(values.shape), drift.reshape(values.shape))

    return branch_fn


def hier_axis(values, axis_num):
    length = values.shape[axis_num]
    result = values
    for level_bit in range(length.bit_length() - 1):
        stride = 2 ** (level_bit + 1)
        before = lax.slice_in_dim(values, 0, length, stride, axis=axis_num)
        ahead_vals = lax.slice_in_dim(values, stride, length, stride, axis=axis_num)
        ahead_vals = jnp.concatenate(
            [ahead_vals, jnp.zeros_like(lax.slice_in_dim(before, 0, 1, axis=axis_num))],
            axis=axis_num,
        )
        position = [slice(None)] * values.ndim
        position[axis_num] = slice(2**level_bit, None, stride)
        result = result.at[tuple(position)].add(-0.5 * (before + ahead_vals))
    return result


def inner_surplus(level_combo):

    def branch_fn(values):
        shaped = values.reshape(
            values.shape[0], 2 ** level_combo[2], 2 ** level_combo[1], 2 ** level_combo[0]
        )
        for axis_num in (3, 2, 1):
            shaped = hier_axis(shaped, axis_num)
        return shaped.reshape(values.shape)

    return branch_fn


def body(concentration, diffusion, velocity, levels, grid_signs, owner_list, slot_list):
    row_count = concentration.shape[1]
    dom_count = lax.axis_size("dom")
    grid_width = lax.axis_size("grid")
    dom_index = lax.axis_index("dom")
    level_rows = level_table()
    term_fns = [inner_terms(level_combo) for level_combo in level_rows]
    surplus_fns = [inner_surplus(level_combo) for level_combo in level_rows]
    branches = jax.vmap(branch_index)(levels)

    def inner_step(operands):
        return lax.switch(operands[1], term_fns, operands[0], velocity)

    def inner_hier(operands):
        return lax.switch(operands[1], surplus_fns, operands[0])

    values = concentration
    for step_num in range(TSTEPS):
        padded = extended_2(values, (("dom", 1),), 1)
        second, drift = lax.map(inner_step, (values, branches))
        ahead_vals = padded[:, 2:]
        before = padded[:, :-2]
        second = second + (ahead_vals - 2.0 * values + before)
        drift = drift + velocity[3] * (ahead_vals - before)
        values = values + 0.1 * diffusion * second - 0.1 * drift
    leading = values[:, 0, :]
    all_rows = lax.all_gather(leading[:, None, :], "dom", axis=1, tiled=True)
    step_size = jnp.zeros((), jnp.int32)
    distance = 1
    while distance < dom_count:
        step_size = jnp.where(dom_index % (2 * distance) == distance, distance, step_size)
        distance = 2 * distance
    lower_row = lax.dynamic_index_in_dim(all_rows, dom_index - step_size, 1, keepdims=False)
    upper_at = jnp.minimum(dom_index + step_size, dom_count - 1)
    upper_row = jnp.where(
        dom_index + step_size < dom_count,
        lax.dynamic_index_in_dim(all_rows, upper_at, 1, keepdims=False),
        0.0,
    )
    coarse_fix = jnp.where(dom_index > 0, 0.5 * (lower_row + upper_row), 0.0)
    next_at = jnp.minimum(dom_index + 1, dom_count - 1)
    next_lead = jnp.where(
        dom_index + 1 < dom_count,
        lax.dynamic_index_in_dim(all_rows, next_at, 1, keepdims=False),
        0.0,
    )
    extended = jnp.concatenate([values, next_lead[:, None, :]], axis=1)
    result = values
    for level_bit in range(row_count.bit_length() - 1):
        stride = 2 ** (level_bit + 1)
        before = lax.slice_in_dim(extended, 0, row_count, stride, axis=1)
        ahead_vals = lax.slice_in_dim(extended, stride, row_count + 1, stride, axis=1)
        result = result.at[:, 2**level_bit :: stride].add(-0.5 * (before + ahead_vals))
    result = result.at[:, 0].add(-coarse_fix)
    surplus = lax.map(inner_hier, (result, branches))
    signed = grid_signs.astype(jnp.float32)[:, None, None] * surplus
    devices = grid_width * dom_count
    block_rows = signed.reshape(-1, BLK)
    block_count = block_rows.shape[0]
    capacity = 2 * block_count // devices
    owners = owner_list[0]
    slot_ids = slot_list[0]
    matches = (owners[:, None] == jnp.arange(devices, dtype=jnp.int32)[None, :]).astype(jnp.int32)
    rank_in = jnp.sum((jnp.cumsum(matches, axis=0) - 1) * matches, axis=1)
    places = owners * capacity + rank_in
    outgoing = jnp.zeros((devices * capacity, BLK), jnp.float32).at[places].set(block_rows)
    out_slots = (
        jnp.full((devices * capacity,), -1.0, jnp.float32)
        .at[places]
        .set(slot_ids.astype(jnp.float32))
    )
    arrived, arrived_slots = (
        lax.all_to_all(
            outgoing.reshape(devices, capacity, BLK),
            ("grid", "dom"),
            split_axis=0,
            concat_axis=0,
            tiled=True,
        ),
        lax.all_to_all(
            out_slots.reshape(devices, capacity),
            ("grid", "dom"),
            split_axis=0,
            concat_axis=0,
            tiled=True,
        ),
    )
    flat_rows = arrived.reshape(devices * capacity, BLK)
    slot_onehot = (
        arrived_slots.reshape(-1)[:, None] == jnp.arange(SLOTS, dtype=jnp.float32)[None, :]
    ).astype(jnp.float32)
    pieces = jnp.dot(
        slot_onehot.T,
        flat_rows,
        precision=lax.Precision.HIGHEST,
        preferred_element_type=jnp.float32,
    )
    returned = jnp.dot(
        slot_onehot, pieces, precision=lax.Precision.HIGHEST, preferred_element_type=jnp.float32
    )
    came_back = lax.all_to_all(
        returned.reshape(devices, capacity, BLK),
        ("grid", "dom"),
        split_axis=0,
        concat_axis=0,
        tiled=True,
    )
    combined = came_back.reshape(devices * capacity, BLK)[places]
    return combined.reshape(signed.shape)


def solution(mesh):
    return jax.shard_map(
        body,
        mesh=mesh,
        in_specs=(
            P("grid", "dom", None),
            P("grid", "dom", None),
            P(),
            P("grid", None),
            P("grid"),
            P(("grid", "dom"), None),
            P(("grid", "dom"), None),
        ),
        out_specs=P("grid", "dom", None),
        check_vma=False,
    )
```

profile of v0, /device:TPU:1, one launch (start us, length us, event | category | flops | bytes accessed | tf_op | source)
XLA Modules:
  0.0 662.1 jit_solution(7001417987466700390)
XLA Ops:
  3.0 5.3 collective-permute-start.1
  13.0 6.0 all-to-all-start
  21.5 3.5 copy.1794
  26.3 53.4 %conditional.3 = (f32[1,16,8192]{2,1,0:T(8,128)S(1)}, f32[1,16,8192]{2,1,0:T(8,128)S(1)}) conditional(s32[]{:T(128)} %clamp.8, (f32[16,8192]{0,1:T(8,128)}, f32[4]{0:T(128)S(1)}) %tuple.889, (f32[16,8192]{0,1:T(8,128)}, f32[4]{0:T(128)S(1)}) %tuple.876, (f32[16,8192]{0,1:T(8,128)}, f32[4]{0:T(128)S(1)}) %tuple.877, ...), branch_computations={%region_5.6_spmd, %region_6.7_spmd, %region_7.8_spmd, %region_8.9_... | conditional | flops 2228224 | bytes 17858640 | solution.py:116
  32.8 4.5 fusion.159
  39.9 3.7 fusion.161
  44.2 10.0 %fusion.7 = (f32[16,8,128,8]{0,3,2,1:T(8,128)}, f32[16,8,128,8]{0,3,2,1:T(8,128)}) fusion(f32[16,7,128,8]{0,3,2,1:T(8,128)} %get-tuple-element.1202, f32[16,7,128,8]{0,3,2,1:T(8,128)} %get-tuple-element.1201, f32[16,8,127,8]{0,3,2,1:T(8,128)} %get-tuple-element.1200, f32[16,8,127,8]{0,3,2,1:T(8,128)S(1)} %get-tuple-element.1199, ...), kind=kLoop, calls=%fused_computation.175 | loop fusion | flops 2228224 | bytes 4448268 | tf_op jit(solution)/shard_map/while/body/eval_jaxpr/cond/branch_4_fun/add | solution.py:69
  56.9 2.8 copy.1871
  83.8 4.6 collective-permute-start.3
  89.6 54.1 %conditional.4 = (f32[1,16,8192]{2,1,0:T(8,128)S(1)}, f32[1,16,8192]{2,1,0:T(8,128)S(1)}) conditional(s32[]{:T(128)} %clamp.8, (f32[1,16,8192]{2,1,0:T(8,128)S(1)}, f32[4]{0:T(128)S(1)}) %tuple.890, (f32[1,16,8192]{2,1,0:T(8,128)S(1)}, f32[4]{0:T(128)S(1)}) %tuple.891, (f32[1,16,8192]{2,1,0:T(8,128)S(1)}, ...), branch_computations={%region_20.21_spmd, %region_21.22_spmd, %region_22.23_spmd, %regio... | conditional | flops 2228224 | bytes 17858640 | solution.py:116
  99.2 4.5 fusion.219
  103.8 3.8 fusion.220
  107.6 3.7 fusion.221
  111.9 11.0 %fusion.40 = (f32[16,8,128,8]{0,3,2,1:T(8,128)}, f32[16,8,128,8]{0,3,2,1:T(8,128)}) fusion(f32[16,7,128,8]{0,3,2,1:T(8,128)} %get-tuple-element.1367, f32[16,7,128,8]{0,3,2,1:T(8,128)} %get-tuple-element.1366, f32[16,8,127,8]{0,3,2,1:T(8,128)} %get-tuple-element.1365, f32[16,8,127,8]{0,3,2,1:T(8,128)} %get-tuple-element.1364, ...), kind=kLoop, calls=%fused_computation.249 | loop fusion | flops 2228224 | bytes 4448268 | tf_op jit(solution)/shard_map/while/body/eval_jaxpr/cond/branch_4_fun/add | solution.py:69
  146.4 10.7 %all_gather.3 = f32[1,4,8192]{2,0,1:T(1,128)S(1)} all-gather(f32[1,1,8192]{2,0,1:T(1,128)S(1)} %slice_bitcast_fusion), channel_id=1, replica_groups=mesh['grid'=8,'dom'=4] {'dom'}, dimensions={1}, use_global_device_ids=true | all-gather | bytes 163840 | tf_op jit(solution)/shard_map/all_gather | solution.py:131
  165.9 204.7 %conditional.5 = (f32[16,8192]{1,0:T(8,128)S(1)}) conditional(s32[]{:T(128)} %clamp.8, (f32[1,16,8192]{2,0,1:T(1,128)S(1)}, f32[1,8192]{1,0:T(1,128)S(1)}, s32[]{:T(128)}) %tuple.617, (f32[1,16,8192]{2,0,1:T(1,128)S(1)}, f32[1,8192]{1,0:T(1,128)S(1)}, s32[]{:T(128)}) %tuple.617, (f32[1,16,8192]{2,0,1:T(1,128)S(1)}, ...), branch_computations={%region_38.49_spmd, %region_49.60_spmd, %region_60.71_spmd, %regio... | conditional | flops 1097816 | bytes 28901860 | solution.py:119
  189.6 21.5 %slice.2945 = f32[16,8,128,4]{0,3,2,1:T(4,128)} slice(f32[16,8,128,8]{0,3,2,1:T(8,128)} %bitcast.989), slice={[0:16:1], [0:8:1], [0:128:1], [0:8:2]} | slice | bytes 524288 | tf_op jit(solution)/shard_map/while/body/eval_jaxpr/cond/branch_4_fun/slice | solution.py:80
  211.1 21.5 %slice.2946 = f32[16,8,128,3]{0,3,2,1:T(4,128)} slice(f32[16,8,128,8]{0,3,2,1:T(8,128)} %bitcast.990), slice={[0:16:1], [0:8:1], [0:128:1], [2:8:2]} | slice | bytes 393216 | tf_op jit(solution)/shard_map/while/body/eval_jaxpr/cond/branch_4_fun/slice | solution.py:81
  232.6 3.0 multiply_bitcast_fusion.41
  236.2 3.5 copy.1596
  240.6 5.3 slice_multiply_fusion.8
  245.8 19.8 %slice.2947 = f32[16,8,128,2]{0,3,2,1:T(2,128)S(1)} slice(f32[16,8,128,8]{0,3,2,1:T(8,128)} %bitcast.993), slice={[0:16:1], [0:8:1], [0:128:1], [0:8:4]} | slice | bytes 262144 | tf_op jit(solution)/shard_map/while/body/eval_jaxpr/cond/branch_4_fun/slice | solution.py:80
  268.2 3.1 copy.1600
  271.3 15.4 %scatter-add.1141 = f32[16,8,128,8]{0,3,2,1:T(8,128)} dynamic-update-slice(f32[16,8,128,8]{0,3,2,1:T(8,128)} %copy.1600, f32[16,8,128,1]{0,3,2,1:T(1,128)S(1)} %copy.1601, s32[]{:T(128)} %constant.2075.clone, s32[]{:T(128)} %constant.2075.clone, s32[]{:T(128)} %constant.2075.clone, s32[]{:T(128)} %constant.2074.clone) | dynamic-update-slice | bytes 131076 | tf_op jit(solution)/shard_map/while/body/eval_jaxpr/cond/branch_4_fun/scatter-add | solution.py:88
  294.5 9.2 %scatter_fusion.2 = f32[16,8,128,8]{0,3,2,1:T(8,128)} fusion(f32[16,8,128,8]{0,3,2,1:T(8,128)} %copy.2002, s32[64]{0:T(128)S(1)} %add_bitcast_fusion.39, f32[64,16,8,8]{1,3,2,0:T(8,128)S(1)} %copy.1602), kind=kCustom, calls=%fused_computation.43 | custom fusion | flops 65536 | bytes 786688 | tf_op jit(solution)/shard_map/while/body/eval_jaxpr/cond/branch_4_fun/scatter-add | solution.py:88
  303.7 4.9 scatter_fusion.3
  324.5 3.4 copy.1608
  327.9 10.3 %scatter-add.1152 = f32[16,8,128,8]{2,3,1,0:T(8,128)S(1)} dynamic-update-slice(f32[16,8,128,8]{2,3,1,0:T(8,128)S(1)} %copy.1608, f32[16,8,1,8]{2,3,1,0:T(8,128)S(1)} %copy.1609, s32[]{:T(128)} %constant.2075.clone, s32[]{:T(128)} %constant.2075.clone, s32[]{:T(128)} %constant.2079.clone, s32[]{:T(128)} %constant.2075.clone) | dynamic-update-slice | bytes 8196 | tf_op jit(solution)/shard_map/while/body/eval_jaxpr/cond/branch_4_fun/scatter-add | solution.py:88
  372.9 229.3 %all-to-all-start.1 = ((f32[32,8,1024]{2,1,0:T(8,128)}), f32[32,8,1024]{2,1,0:T(8,128)S(1)}, u32[]{:S(2)}, u32[]{:S(2)}) async-start(f32[32,8,1024]{2,1,0:T(8,128)} %bitcast.498), calls=%async_computation.1 | async-start | bytes 2097152 | tf_op jit(solution)/shard_map/all_to_all | solution.py:177
  604.2 24.3 %all-to-all-done.1 = f32[32,8,1024]{2,1,0:T(8,128)S(1)} async-done(((f32[32,8,1024]{2,1,0:T(8,128)}), f32[32,8,1024]{2,1,0:T(8,128)S(1)}, u32[]{:S(2)}, u32[]{:S(2)}) %all-to-all-start.1) | async-done | bytes 1048608 | tf_op jit(solution)/shard_map/all_to_all | solution.py:177
  630.7 3.2 all-to-all-start.2
  633.9 26.3 %all-to-all-done.2 = f32[32,8,1024]{2,1,0:T(8,128)S(1)} async-done(((f32[32,8,1024]{2,1,0:T(8,128)}), f32[32,8,1024]{2,1,0:T(8,128)S(1)}, u32[]{:S(2)}, u32[]{:S(2)}) %all-to-all-start.2) | async-done | bytes 1048608 | tf_op jit(solution)/shard_map/all_to_all | solution.py:205
  (134 shorter events, 87.7 us)
Async XLA Ops:
  0.0 25.0 %copy-start.52 = (f32[4]{0:T(128)S(1)}, f32[4]{0:T(128)}, u32[]{:S(2)}) copy-start(f32[4]{0:T(128)} %param.149) | copy-start | bytes 52
  1.7 78.0 %collective-permute-start = (f32[1,1,8192]{2,1,0:T(1,128)}, f32[1,1,8192]{2,1,0:T(1,128)}, u32[]{:S(2)}, u32[]{:S(2)}) collective-permute-start(f32[1,1,8192]{2,1,0:T(1,128)} %get-tuple-element.1513), channel_id=1, source_target_pairs={{1,0},{2,1},{3,2},{5,4},{6,5},{7,6},{9,8},{10,9},{11,10},{13,12},{... | collective-permute-start | bytes 98312 | tf_op jit(solution)/shard_map/ppermute | solution.py:21
  3.0 76.8 %collective-permute-start.1 = (f32[1,1,8192]{2,1,0:T(1,128)}, f32[1,1,8192]{2,1,0:T(1,128)}, u32[]{:S(2)}, u32[]{:S(2)}) collective-permute-start(f32[1,1,8192]{2,1,0:T(1,128)} %get-tuple-element.1514), channel_id=1, source_target_pairs={{0,1},{1,2},{2,3},{4,5},{5,6},{6,7},{8,9},{9,10},{10,11},{12,13},{... | collective-permute-start | bytes 98312 | tf_op jit(solution)/shard_map/ppermute | solution.py:18
  10.7 15.6 %copy-start.60 = (s32[128]{0:T(128)}, s32[128]{0:T(128)S(1)}, u32[]{:S(2)}) copy-start(s32[128]{0:T(128)S(1)} %fusion.140) | copy-start | bytes 1540
  13.0 359.9 %all-to-all-start = ((f32[32,1,8]{2,1,0:T(1,128)}), f32[32,1,8]{2,1,0:T(1,128)}, u32[]{:S(2)}, u32[]{:S(2)}) async-start(f32[32,1,8]{2,1,0:T(1,128)} %bitcast.484), calls=%async_computation | async-start | bytes 32768 | tf_op jit(solution)/shard_map/all_to_all | solution.py:184
  26.3 53.5 %copy-start.53 = (f32[1,16,8192]{2,1,0:T(8,128)S(1)}, f32[1,16,8192]{2,1,0:T(8,128)}, u32[]{:S(2)}) copy-start(f32[1,16,8192]{2,1,0:T(8,128)} %param.147) | copy-start | bytes 1572868
  32.8 4.6 copy-start.4
  82.5 61.2 %collective-permute-start.2 = (f32[1,1,8192]{2,1,0:T(1,128)}, f32[1,1,8192]{2,1,0:T(1,128)}, u32[]{:S(2)}, u32[]{:S(2)}) collective-permute-start(f32[1,1,8192]{2,1,0:T(1,128)} %get-tuple-element.1511), channel_id=1, source_target_pairs={{1,0},{2,1},{3,2},{5,4},{6,5},{7,6},{9,8},{10,9},{11,10},{13,12},{... | collective-permute-start | bytes 98312 | tf_op jit(solution)/shard_map/ppermute | solution.py:21
  83.8 60.0 %collective-permute-start.3 = (f32[1,1,8192]{2,1,0:T(1,128)}, f32[1,1,8192]{2,1,0:T(1,128)}, u32[]{:S(2)}, u32[]{:S(2)}) collective-permute-start(f32[1,1,8192]{2,1,0:T(1,128)} %get-tuple-element.1512), channel_id=1, source_target_pairs={{0,1},{1,2},{2,3},{4,5},{5,6},{6,7},{8,9},{9,10},{10,11},{12,13},{... | collective-permute-start | bytes 98312 | tf_op jit(solution)/shard_map/ppermute | solution.py:18
  89.6 54.1 %copy-start.59 = (f32[1,16,8192]{2,1,0:T(8,128)S(1)}, f32[1,16,8192]{2,1,0:T(8,128)}, u32[]{:S(2)}) copy-start(f32[1,16,8192]{2,1,0:T(8,128)} %param.148) | copy-start | bytes 1572868
  99.2 4.6 copy-start.24
  266.8 1.0 copy-start.58
  286.7 4.7 copy-start.32
  303.6 4.9 copy-start.49
  370.7 263.1 %copy-start.61 = (s32[128]{0:T(128)S(1)}, s32[128]{0:T(128)}, u32[]{:S(2)}) copy-start(s32[128]{0:T(128)} %copy-done.60) | copy-start | bytes 1540
  372.9 255.6 %all-to-all-start.1 = ((f32[32,8,1024]{2,1,0:T(8,128)}), f32[32,8,1024]{2,1,0:T(8,128)S(1)}, u32[]{:S(2)}, u32[]{:S(2)}) async-start(f32[32,8,1024]{2,1,0:T(8,128)} %bitcast.498), calls=%async_computation.1 | async-start | bytes 2097152 | tf_op jit(solution)/shard_map/all_to_all | solution.py:177
  630.7 29.5 %all-to-all-start.2 = ((f32[32,8,1024]{2,1,0:T(8,128)}), f32[32,8,1024]{2,1,0:T(8,128)S(1)}, u32[]{:S(2)}, u32[]{:S(2)}) async-start(f32[32,8,1024]{2,1,0:T(8,128)} %convolution_bitcast_fusion), calls=%async_computation.2 | async-start | bytes 2097152 | tf_op jit(solution)/shard_map/all_to_all | solution.py:205
where the time goes:
time: 673 us; the launch traced here: 662 us
  starting transfers between devices  251 us (37%)
  local copies, waits for them, and re-layouts  174 us (26%)
  loops' own time  94.7 us (14%)
  other arithmetic  76.7 us (11%)
  waiting for transfers between devices  50.7 us (8%)
  blocking collectives  10.7 us (2%)
    all_to_all x1, starting transfers between devices, body(): lax.all_to_all(outgoing.reshape(devices, capacity, BLK), ('grid', 'dom'),...  229 us
    another operation x2, loops' own time, inner_step(): return lax.switch(operands[1], term_fns, operands[0], velocity)  48.7 us
    another operation x1, loops' own time, inner_hier(): return lax.switch(operands[1], surplus_fns, operands[0])  46 us
    slice x2, local copies, waits for them, and re-layouts, hier_axis(): before = lax.slice_in_dim(values, 0, length, stride, axis=axis_num)  41.3 us
    scatter-add x5, local copies, waits for them, and re-layouts, hier_axis(): result = result.at[tuple(position)].add(-0.5 * (before + ahead_vals))  34.9 us
    slice x9, local copies, waits for them, and re-layouts, hier_axis(): ahead_vals = lax.slice_in_dim(values, stride, length, stride, axis=axis_num)  26.8 us
    all_to_all x1, waiting for transfers between devices, body(): lax.all_to_all(returned.reshape(devices, capacity, BLK), ('grid', 'dom'),...  26.3 us
    scatter-add x11, other arithmetic, hier_axis(): result = result.at[tuple(position)].add(-0.5 * (before + ahead_vals))  26.1 us
  transfers between devices with their start and end apart: 7, of which 2 were waited for; matrix products, arithmetic and copies ran while one was open for 37% of the time, Pallas kernels for 0%

commit v1 on v0

v1 whole, which is shorter than its diff:
```python
import functools

import jax
import jax.numpy as jnp
from jax import lax
from jax.experimental import pallas as pl
from jax.experimental.pallas import tpu as pltpu
from jax.sharding import PartitionSpec as P

LR = 13
BLK = 1024
SLOTS = 64
LANES = 128
TILES = 2**LR // LANES
PAD = 9
VMEM_LIMIT = 48 * 1024 * 1024


def params():
    return pltpu.CompilerParams(vmem_limit_bytes=VMEM_LIMIT)


VM = pl.BlockSpec(memory_space=pltpu.VMEM)
SM = pl.BlockSpec(memory_space=pltpu.SMEM)


def grid_step(first_bits, second_bits, weights, valid, src, dst, dif, lane_two, lane_three):
    lane = lax.broadcasted_iota(jnp.int32, (1, LANES), 1)
    first_mask = (1 << first_bits) - 1
    stride_two = 1 << first_bits
    stride_three = 1 << (first_bits + second_bits)
    two_mask = stride_three - 1
    up_one = (lane & first_mask) != first_mask
    down_one = (lane & first_mask) != 0

    def rolled(tile, stride):
        return pltpu.roll(tile, LANES - stride, 1), pltpu.roll(tile, stride, 1)

    def neighbours(j, x, nxt, stride, in_lanes, carry):
        if not in_lanes:
            step = stride // LANES
            return src[PAD + j + step], src[PAD + j - step], carry
        up_here, down_here, down_last = carry
        up_next, down_next = rolled(nxt, stride)
        ahead = jnp.where(lane < LANES - stride, up_here, up_next)
        before = jnp.where(lane >= stride, down_here, down_last)
        return ahead, before, (up_next, down_next, down_here)

    def one_tile(j, carry):
        x, carry_two, carry_three = carry
        nxt = src[PAD + j + 1]
        ahead = jnp.where(up_one, pltpu.roll(x, LANES - 1, 1), 0.0)
        before = jnp.where(down_one, pltpu.roll(x, 1, 1), 0.0)
        total = ahead + before
        drift = weights[0] * (ahead - before)
        ahead, before, carry_two = neighbours(j, x, nxt, stride_two, lane_two, carry_two)
        node = (j * LANES + lane) & two_mask
        ahead = jnp.where(node < stride_three - stride_two, ahead, 0.0)
        before = jnp.where(node >= stride_two, before, 0.0)
        total = total + (ahead + before)
        drift = drift + weights[1] * (ahead - before)
        ahead, before, carry_three = neighbours(j, x, nxt, stride_three, lane_three, carry_three)
        total = total + (ahead + before)
        drift = drift + weights[2] * (ahead - before)
        ahead = pltpu.roll(x, 23, 0)
        before = pltpu.roll(x, 1, 0)
        total = total + (ahead + before)
        drift = drift + weights[3] * (ahead - before)
        new = x + dif[j] * (total - 8.0 * x) - drift
        dst[PAD + j] = jnp.where(valid, new, 0.0)
        return nxt, carry_two, carry_three

    def start(stride, in_lanes):
        if not in_lanes:
            return ()
        up_here, down_here = rolled(src[PAD], stride)
        return up_here, down_here, jnp.zeros((24, LANES), jnp.float32)

    def several(k, carry):
        for i in range(4):
            carry = one_tile(4 * k + i, carry)
        return carry

    lax.fori_loop(
        0,
        TILES // 4,
        several,
        (src[PAD], start(stride_two, lane_two), start(stride_three, lane_three)),
    )


def steps_kernel(levels, velocity, conc, dif_in, low, high, out, lead, u_a, u_b, dif):
    place = lax.axis_index("dom")
    count = lax.axis_size("dom")
    zeros = jnp.zeros((PAD, 24, LANES), jnp.float32)
    for ref in (u_a, u_b):
        ref[pl.ds(0, PAD)] = zeros
        ref[pl.ds(PAD + TILES, PAD)] = zeros
    tail = jnp.zeros((8, LANES), jnp.float32)
    for j in range(TILES):
        cols = pl.ds(j * LANES, LANES)
        u_a[PAD + j, 0:16] = conc[:, cols]
        u_a[PAD + j, 16:24] = tail
        dif[j, 0:16] = 0.1 * dif_in[:, cols]
        dif[j, 16:24] = tail
    for i in range(3):
        u_a[PAD : PAD + TILES, 16 + i] = high[i]
    for i in range(2):
        u_a[PAD : PAD + TILES, 22 + i] = low[i]
        dif[:, 16 + i] = 0.1 * high[3 + i]
    dif[:, 23] = 0.1 * low[2]
    row = lax.broadcasted_iota(jnp.int32, (24, LANES), 0)
    valid = (row < 16) | ((row < 20) & (place < count - 1)) | ((row >= 20) & (place > 0))
    weights = [0.1 * velocity[d] for d in range(4)]
    first_bits = levels[0, 0]
    second_bits = levels[0, 1]

    def both(lane_two, lane_three):
        def run():
            for src, dst in ((u_a, u_b), (u_b, u_a)):
                grid_step(
                    first_bits, second_bits, weights, valid, src, dst, dif, lane_two, lane_three
                )

        return run

    small_two = first_bits < 7
    small_three = first_bits + second_bits < 7
    pl.when(small_three)(both(True, True))
    pl.when(small_two & jnp.logical_not(small_three))(both(True, False))
    pl.when(jnp.logical_not(small_two))(both(False, False))
    out[...] = u_a[PAD : PAD + TILES]
    lead[...] = u_a[PAD : PAD + TILES, 0]


def bit_ends(levels, q):
    one = levels[0, 0]
    two = one + levels[0, 1]
    begin = jnp.where(q < one, 0, jnp.where(q < two, one, two))
    end = jnp.where(q < one, one, jnp.where(q < two, two, LR))
    return begin, end


def lane_kernel(levels, out):
    rows = lax.broadcasted_iota(jnp.int32, (LANES, LANES), 0)
    lane = lax.broadcasted_iota(jnp.int32, (LANES, LANES), 1)
    own = (rows == lane).astype(jnp.float32)
    nxt = jnp.zeros((LANES, LANES), jnp.float32)
    for q in range(7):
        begin, end = bit_ends(levels, q)
        below = (1 << q) - (1 << begin)
        above = (1 << jnp.minimum(end, 7)) - (2 << q)
        here = ((lane & below) == 0) & ((lane & (1 << q)) != 0)
        full = (lane & above) == above
        ahead = pltpu.roll(own, LANES - (1 << q), 1)
        before = pltpu.roll(own, 1 << q, 1)
        half = jnp.where(here, -0.5, 0.0)
        nxt = nxt + jnp.where(full & (end > 7), half * ahead, 0.0)
        own = own + half * (before + jnp.where(full, 0.0, ahead))
    out[0:LANES] = own
    out[LANES : 2 * LANES] = nxt


def pack_kernel(levels, sign, places, v_in, coarse, lanes, out, x, y, stage):
    place = lax.axis_index("dom")
    row = lax.broadcasted_iota(jnp.int32, (24, LANES), 0)
    for j in range(TILES):
        tile = v_in[j]
        for p in range(4):
            s = 1 << p
            both = pltpu.roll(tile, 24 - s, 0) + pltpu.roll(tile, s, 0)
            hit = ((row & (2 * s - 1)) == s) & (row < 16)
            tile = tile - 0.5 * jnp.where(hit, both, 0.0)
        x[j] = tile[0:16]
    own_upper = jnp.where((place & 1) == 1, 0.5, 0.0)
    fix = 0.5 * coarse[...] + own_upper * v_in[:, 16]
    x[0:TILES, 0] = x[0:TILES, 0] - fix
    x[TILES] = jnp.zeros((16, LANES), jnp.float32)
    y[pl.ds(0, 32)] = jnp.zeros((32, 16, LANES), jnp.float32)
    y[pl.ds(32 + TILES, 32)] = jnp.zeros((32, 16, LANES), jnp.float32)

    _, end_six = bit_ends(levels, 6)
    mask_six = (1 << (jnp.maximum(end_six, 7) - 7)) - 1
    chunk = 8
    own_mat = lanes[0:LANES]
    next_mat = lanes[LANES : 2 * LANES]

    def lane_pass(k, carry):
        j0 = k * chunk
        own = x[pl.ds(j0, chunk)].reshape(chunk * 16, LANES)
        nxt = jnp.concatenate(
            [
                jnp.where(((j0 + i) & mask_six) == mask_six, 0.0, x[j0 + i + 1])
                for i in range(chunk)
            ],
            axis=0,
        )
        res = jnp.dot(
            own, own_mat, precision=lax.Precision.HIGHEST, preferred_element_type=jnp.float32
        ) + jnp.dot(
            nxt, next_mat, precision=lax.Precision.HIGHEST, preferred_element_type=jnp.float32
        )
        y[pl.ds(32 + j0, chunk)] = res.reshape(chunk, 16, LANES)
        return carry

    lax.fori_loop(0, TILES // chunk, lane_pass, 0)

    lane = lax.broadcasted_iota(jnp.int32, (1, LANES), 1)
    for q in range(7, LR):
        t = 1 << (q - 7)
        begin, end = bit_ends(levels, q)
        low_lane = 128 - (1 << jnp.minimum(begin, 7))
        half = jnp.where((lane & low_lane) == 0, -0.5, 0.0)
        below = t - (1 << (jnp.maximum(begin, 7) - 7))
        above = (1 << (end - 7)) - 2 * t

        def tile_pass(j):
            hit = (j & below) == 0
            mine = jnp.where(hit, half, 0.0)
            ahead_on = jnp.where((j & above) == above, 0.0, 1.0)
            y[32 + j] = y[32 + j] + mine * (y[32 + j - t] + ahead_on * y[32 + j + t])

        for j in range(TILES):
            if j & t:
                tile_pass(j)

    factor = sign[0].astype(jnp.float32)
    for j in range(TILES):
        tile = factor * y[32 + j]
        for i in range(2):
            stage[pl.ds(j + i * 8 * TILES, 8, stride=TILES), :] = tile[8 * i : 8 * i + 8]
    for b in range(16 * TILES // 8):
        out[places[b]] = stage[pl.ds(8 * b, 8), :]


def places_kernel(owners, out, seen, *, devices, capacity):
    def clear(i, carry):
        seen[i] = 0
        return carry

    lax.fori_loop(0, devices, clear, 0)

    def one(b, carry):
        owner = owners[0, b]
        rank = seen[owner]
        seen[owner] = rank + 1
        out[b] = owner * capacity + rank
        return carry

    lax.fori_loop(0, owners.shape[1], one, 0)


def sum_kernel(table, arrived, out, pieces):
    pieces[...] = jnp.zeros_like(pieces)
    devices, capacity = table.shape

    def add(d, carry):
        for i in range(capacity):
            s = table[d, i]
            pieces[s] = pieces[s] + arrived[d * capacity + i]
        return carry

    lax.fori_loop(0, devices, add, 0)

    def give(d, carry):
        for i in range(capacity):
            out[d * capacity + i] = pieces[table[d, i]]
        return carry

    lax.fori_loop(0, devices, give, 0)


def unpack_kernel(places, back, out, stage):
    for b in range(16 * TILES // 8):
        stage[pl.ds(8 * b, 8), :] = back[places[b]]
    for j in range(TILES):
        for i in range(2):
            out[8 * i : 8 * i + 8, j * LANES : (j + 1) * LANES] = stage[
                pl.ds(j + i * 8 * TILES, 8, stride=TILES), :
            ]


def f32(*shape):
    return jax.ShapeDtypeStruct(shape, jnp.float32)


def body(concentration, diffusion, velocity, levels, grid_signs, owner_list, slot_list):
    dom_count = lax.axis_size("dom")
    devices = lax.axis_size("grid") * dom_count
    rows = concentration.shape[1]
    conc = concentration[0]
    dif = diffusion[0]
    blocks = owner_list.shape[1]
    capacity = 2 * blocks // devices

    up = [(i, i + 1) for i in range(dom_count - 1)]
    down = [(i + 1, i) for i in range(dom_count - 1)]
    low_rows = jnp.concatenate([conc[rows - 2 :], dif[rows - 1 :]], axis=0)
    high_rows = jnp.concatenate([conc[:3], dif[:2]], axis=0)
    low = lax.ppermute(low_rows.reshape(3, TILES, LANES), "dom", up)
    high = lax.ppermute(high_rows.reshape(5, TILES, LANES), "dom", down)

    places = pl.pallas_call(
        functools.partial(places_kernel, devices=devices, capacity=capacity),
        out_shape=jax.ShapeDtypeStruct((blocks,), jnp.int32),
        in_specs=[SM],
        out_specs=SM,
        scratch_shapes=[pltpu.SMEM((devices,), jnp.int32)],
        compiler_params=params(),
        name="places",
    )(owner_list)
    lanes = pl.pallas_call(
        lane_kernel,
        out_shape=f32(2 * LANES, LANES),
        in_specs=[SM],
        out_specs=VM,
        compiler_params=params(),
        name="lane_matrix",
    )(levels)

    me = lax.axis_index("grid") * dom_count + lax.axis_index("dom")
    keys = lax.all_gather(owner_list * SLOTS + slot_list, ("grid", "dom"), axis=0, tiled=True)
    mine = (keys // SLOTS) == me
    rank = jnp.cumsum(mine.astype(jnp.int32), axis=1)
    at_rank = mine[:, None, :] & (
        rank[:, None, :] == jnp.arange(1, capacity + 1, dtype=jnp.int32)[None, :, None]
    )
    table = SLOTS + jnp.sum(jnp.where(at_rank, (keys % SLOTS - SLOTS)[:, None, :], 0), axis=2)

    stepped, lead = pl.pallas_call(
        steps_kernel,
        out_shape=(f32(TILES, 24, LANES), f32(TILES, LANES)),
        in_specs=[SM, SM, VM, VM, VM, VM],
        out_specs=(VM, VM),
        scratch_shapes=[
            pltpu.VMEM((TILES + 2 * PAD, 24, LANES), jnp.float32),
            pltpu.VMEM((TILES + 2 * PAD, 24, LANES), jnp.float32),
            pltpu.VMEM((TILES, 24, LANES), jnp.float32),
        ],
        compiler_params=params(),
        name="steps",
    )(levels, velocity, conc, dif, low, high)

    coarse = None
    distance = 1
    while distance < dom_count:
        targets = range(distance, dom_count, 2 * distance)
        pairs = [[(d - distance, d) for d in targets]]
        if distance > 1:
            pairs.append([(d + distance, d) for d in targets if d + distance < dom_count])
        for pair in pairs:
            if pair:
                part = lax.ppermute(lead, "dom", pair)
                coarse = part if coarse is None else coarse + part
        distance *= 2

    outgoing = pl.pallas_call(
        pack_kernel,
        out_shape=f32(devices * capacity, 8, LANES),
        in_specs=[SM, SM, SM, VM, VM, VM],
        out_specs=VM,
        scratch_shapes=[
            pltpu.VMEM((TILES + 1, 16, LANES), jnp.float32),
            pltpu.VMEM((TILES + 64, 16, LANES), jnp.float32),
            pltpu.VMEM((16 * TILES, LANES), jnp.float32),
        ],
        compiler_params=params(),
        name="pack",
    )(levels, grid_signs, places, stepped, coarse, lanes)

    def exchange(x):
        return lax.all_to_all(
            x.reshape(devices, capacity * 8, LANES),
            ("grid", "dom"),
            split_axis=0,
            concat_axis=0,
            tiled=True,
        ).reshape(devices * capacity, 8, LANES)

    arrived = exchange(outgoing)
    returned = pl.pallas_call(
        sum_kernel,
        out_shape=f32(devices * capacity, 8, LANES),
        in_specs=[SM, VM],
        out_specs=VM,
        scratch_shapes=[pltpu.VMEM((SLOTS + 8, 8, LANES), jnp.float32)],
        compiler_params=params(),
        name="sum_pieces",
    )(table, arrived)
    back = exchange(returned)
    combined = pl.pallas_call(
        unpack_kernel,
        out_shape=f32(rows, TILES * LANES),
        in_specs=[SM, VM],
        out_specs=VM,
        scratch_shapes=[pltpu.VMEM((16 * TILES, LANES), jnp.float32)],
        compiler_params=params(),
        name="unpack",
    )(places, back)
    return combined[None]


def solution(mesh):
    return jax.shard_map(
        body,
        mesh=mesh,
        in_specs=(
            P("grid", "dom", None),
            P("grid", "dom", None),
            P(),
            P("grid", None),
            P("grid"),
            P(("grid", "dom"), None),
            P(("grid", "dom"), None),
        ),
        out_specs=P("grid", "dom", None),
        check_vma=False,
    )
```

time: 673 us -> 153 us (0.23); the launches traced: 662 us -> 153 us
  starting transfers between devices: 251 us -> 17.3 us
  local copies, waits for them, and re-layouts: 174 us -> 3.48 us
  blocking collectives: 10.7 us -> 110 us
  loops' own time: 94.7 us -> 0 us
  other arithmetic: 76.7 us -> 1.03 us
  waiting for transfers between devices: 50.7 us -> 1.86 us
  Pallas kernels: 0 us -> 17.9 us
    all_to_all x3 -> x1, starting transfers between devices: 238 us -> 5.04 us  [exchange(): lax.all_to_all(x.reshape(devices, capacity * 8, LANES), ('grid', 'dom'),...]
    slice x28 -> x1, local copies, waits for them, and re-layouts: 100 us -> 0.03 us  [body(): low_rows = jnp.concatenate([conc[rows - 2:], dif[rows - 1:]], axis=0)]
    another operation x3 -> x0, loops' own time: 94.7 us -> none  [the longest x2 48.7 us: inner_step(): return lax.switch(operands[1], term_fns, operands[0], velocity)]
    all_gather x1, blocking collectives: 10.7 us -> 77.2 us  [body(): lax.all_gather(owner_list * SLOTS + slot_list, ('grid', 'dom'), axis=0, t...]
    all_to_all x3 -> x1, waiting for transfers between devices: 50.7 us -> 0.01 us  [exchange(): lax.all_to_all(x.reshape(devices, capacity * 8, LANES), ('grid', 'dom'),...]
    scatter-add x8 -> x0, local copies, waits for them, and re-layouts: 38.1 us -> none  [the longest x5 34.9 us: hier_axis(): result = result.at[tuple(position)].add(-0.5 * (before + ahead_vals))]
    all_to_all x0 -> x1, blocking collectives: none -> 33.1 us  [exchange(): lax.all_to_all(x.reshape(devices, capacity * 8, LANES), ('grid', 'dom'),...]
    scatter-add x15 -> x0, other arithmetic: 29.6 us -> none  [the longest x11 26.1 us: hier_axis(): result = result.at[tuple(position)].add(-0.5 * (before + ahead_vals))]
  transfers between devices with their start and end apart: 7 -> 5, of which waited for: 2 -> 2; matrix products, arithmetic and copies ran while one was open for 37% -> 1% of each run, Pallas kernels for 0% -> 2%
where the time goes in v1:
time: 153 us
  blocking collectives  110 us (72%)
  Pallas kernels  17.9 us (12%)
  starting transfers between devices  17.3 us (11%)
  local copies, waits for them, and re-layouts  3.48 us (2%)
  waiting for transfers between devices  1.86 us (1%)
    all_gather x1, blocking collectives, body(): lax.all_gather(owner_list * SLOTS + slot_list, ('grid', 'dom'), axis=0, t...  77.2 us
    all_to_all x1, blocking collectives, exchange(): lax.all_to_all(x.reshape(devices, capacity * 8, LANES), ('grid', 'dom'),...  33.1 us
    ppermute x2, starting transfers between devices, body(): part = lax.ppermute(lead, 'dom', pair)  6.26 us
    pallas_call x1, Pallas kernels, body(): pl.pallas_call(pack_kernel, out_shape=f32(devices * capacity, 8, LANES),...  5.27 us
    pallas_call x1, Pallas kernels, body(): pl.pallas_call(steps_kernel, out_shape=(f32(TILES, 24, LANES), f32(TILES,...  5.14 us
    all_to_all x1, starting transfers between devices, exchange(): lax.all_to_all(x.reshape(devices, capacity * 8, LANES), ('grid', 'dom'),...  5.04 us
    ppermute x1, starting transfers between devices, body(): low = lax.ppermute(low_rows.reshape(3, TILES, LANES), 'dom', up)  4.66 us
    unnamed x18, local copies, waits for them, and re-layouts  3.45 us
  transfers between devices with their start and end apart: 5, of which 2 were waited for; matrix products, arithmetic and copies ran while one was open for 1% of the time, Pallas kernels for 2%

profile of v1, /device:TPU:1, one launch (start us, length us, event | category | flops | bytes accessed | tf_op | source)
XLA Modules:
  0.0 152.7 jit_solution(2773474708629208926)
XLA Ops:
  0.0 0.0 copy-start.1
  0.0 1.0 slice_bitcast_fusion.1
  1.0 0.0 copy-start
  1.1 1.0 slice_bitcast_fusion
  2.1 1.3 collective-permute-start.1
  3.4 0.0 copy-done.1
  3.5 0.0 copy-done
  3.6 4.7 %collective-permute-start = (f32[3,64,128]{2,1,0:T(8,128)S(1)}, f32[3,64,128]{2,1,0:T(8,128)S(1)}, u32[]{:S(2)}, u32[]{:S(2)}) collective-permute-start(f32[3,64,128]{2,1,0:T(8,128)S(1)} %pad_maximum_fusion.1), channel_id=1, source_target_pairs={{0,1},{1,2},{2,3},{4,5},{5,6},{6,7},{8,9},{9,10},{10,11},{12,13},{... | collective-permute-start | bytes 294920 | tf_op jit(solution)/shard_map/ppermute | solution.py:300
  8.2 1.6 %collective-permute-done.low = f32[3,64,128]{2,1,0:T(8,128)S(1)} collective-permute-done((f32[3,64,128]{2,1,0:T(8,128)S(1)}, f32[3,64,128]{2,1,0:T(8,128)S(1)}, u32[]{:S(2)}, u32[]{:S(2)}) %collective-permute-start) | collective-permute-done | bytes 98336 | tf_op jit(solution)/shard_map/ppermute | solution.py:300
  9.9 0.2 collective-permute-done.1.high
  10.1 0.7 copy-done.2
  10.7 0.0 copy-done.3
  10.8 5.1 %steps.1 = (f32[64,24,128]{2,1,0:T(8,128)S(1)}, f32[64,128]{1,0:T(8,128)S(1)}) custom-call(s32[1,3]{1,0:T(1,128)S(1)} %copy-done.2, f32[4]{0:T(128)S(1)} %copy-done.3, f32[16,8192]{1,0:T(8,128)S(1)} %bitcast.32, f32[16,8192]{1,0:T(8,128)S(1)} %bitcast.33, f32[3,64,128]{2,1,0:T(8,128)S(1)} %collective-permute-done.low, ...), custom_call_target="tpu_custom_call" | custom-call | tf_op jit(solution)/shard_map/steps/pallas_call | solution.py:330
  15.9 5.0 %collective-permute-start.3 = (f32[64,128]{1,0:T(8,128)S(1)}, f32[64,128]{1,0:T(8,128)S(1)}, u32[]{:S(2)}, u32[]{:S(2)}) collective-permute-start(f32[64,128]{1,0:T(8,128)S(1)} %get-tuple-element.8), channel_id=1, source_target_pairs={{0,2},{4,6},{8,10},{12,14},{16,18},{20,22},{24,26},{28,30}} | collective-permute-start | bytes 98312 | tf_op jit(solution)/shard_map/ppermute | solution.py:353
  20.9 1.3 collective-permute-start.2
  22.2 1.1 lane_matrix.1.lanes
  23.3 0.0 copy-start.4
  24.0 0.0 copy-done.4
  24.0 2.3 %places.1 = s32[128]{0:T(128)S(1)} custom-call(s32[1,128]{1,0:T(1,128)S(1)} %copy-done.4), custom_call_target="tpu_custom_call" | custom-call | tf_op jit(solution)/shard_map/places/pallas_call | solution.py:303
  26.4 0.0 collective-permute-done.3
  26.4 0.0 collective-permute-done.2
  26.4 5.3 %pack.1 = f32[256,8,128]{2,1,0:T(8,128)} custom-call(s32[1,3]{1,0:T(1,128)S(1)} %copy-done.2, s32[1]{0:T(128)S(6)} %copy.17.sign, s32[128]{0:T(128)S(1)} %places.1, f32[64,24,128]{2,1,0:T(8,128)S(1)} %get-tuple-element.7.v_in, f32[64,128]{1,0:T(8,128)S(1)} %add.36.coarse, f32[256,128]{1,0:T(8,128)S(1)} %lane_matrix.1.lanes), custom_call_target="tpu_custom_call" | custom-call | tf_op jit(solution)/shard_map/pack/pallas_call | solution.py:357
  31.7 5.0 %all-to-all-start = ((f32[32,64,128]{2,1,0:T(8,128)}), f32[32,64,128]{2,1,0:T(8,128)S(1)}, u32[]{:S(2)}, u32[]{:S(2)}) async-start(f32[32,64,128]{2,1,0:T(8,128)} %bitcast.5), calls=%async_computation | async-start | bytes 2097152 | tf_op jit(solution)/shard_map/all_to_all | solution.py:372
  36.7 0.0 copy-start.5
  36.7 0.6 copy-done.5
  37.4 77.2 %all-gather = s32[32,1,128]{2,1,0:T(1,128)S(1)} all-gather(s32[1,1,128]{2,1,0:T(1,128)S(1)} %add_bitcast_fusion), channel_id=1, replica_groups=mesh['grid'=8,'dom'=4] {'grid','dom'}, dimensions={0}, use_global_device_ids=true | all-gather | bytes 16896 | tf_op jit(solution)/shard_map/all_gather | solution.py:322
  114.6 0.3 reduce_window_sum.11
  114.9 0.7 select_reduce_fusion
  115.6 0.0 all-to-all-done
  115.6 2.3 %sum_pieces.1 = f32[256,8,128]{2,1,0:T(8,128)S(1)} custom-call(s32[32,8]{1,0:T(8,128)S(1)} %broadcast_add_fusion.table, f32[256,8,128]{2,1,0:T(8,128)S(1)} %bitcast.29), custom_call_target="tpu_custom_call" | custom-call | tf_op jit(solution)/shard_map/sum_pieces/pallas_call | solution.py:381
  117.9 33.1 %all_to_all.10 = f32[32,64,128]{2,1,0:T(8,128)S(1)} all-to-all(f32[32,64,128]{2,1,0:T(8,128)S(1)} %bitcast.30), channel_id=1, replica_groups=mesh['grid'=8,'dom'=4] {'grid','dom'}, dimensions={0} | all-to-all | bytes 2097152 | tf_op jit(solution)/shard_map/all_to_all | solution.py:372
  151.0 1.7 %unpack.1 = f32[16,8192]{1,0:T(8,128)} custom-call(s32[128]{0:T(128)S(1)} %places.1, f32[256,8,128]{2,1,0:T(8,128)S(1)} %bitcast.31), custom_call_target="tpu_custom_call" | custom-call | tf_op jit(solution)/shard_map/unpack/pallas_call | solution.py:391
  (15 shorter events, 0.2 us)
Async XLA Ops:
  0.0 3.4 %copy-start.1 = (f32[1,16,8192]{2,1,0:T(8,128)S(1)}, f32[1,16,8192]{2,1,0:T(8,128)}, u32[]{:S(2)}) copy-start(f32[1,16,8192]{2,1,0:T(8,128)} %param.8) | copy-start | bytes 1572868
  1.0 2.4 %copy-start = (f32[1,16,8192]{2,1,0:T(8,128)S(1)}, f32[1,16,8192]{2,1,0:T(8,128)}, u32[]{:S(2)}) copy-start(f32[1,16,8192]{2,1,0:T(8,128)} %param.7) | copy-start | bytes 1572868
  2.1 8.0 %collective-permute-start.1 = (f32[5,64,128]{2,1,0:T(8,128)S(1)}, f32[5,64,128]{2,1,0:T(8,128)S(1)}, u32[]{:S(2)}, u32[]{:S(2)}) collective-permute-start(f32[5,64,128]{2,1,0:T(8,128)S(1)} %pad_maximum_fusion), channel_id=1, source_target_pairs={{1,0},{2,1},{3,2},{5,4},{6,5},{7,6},{9,8},{10,9},{11,10},{13,12},{... | collective-permute-start | bytes 491528 | tf_op jit(solution)/shard_map/ppermute | solution.py:301
  3.6 6.3 %collective-permute-start = (f32[3,64,128]{2,1,0:T(8,128)S(1)}, f32[3,64,128]{2,1,0:T(8,128)S(1)}, u32[]{:S(2)}, u32[]{:S(2)}) collective-permute-start(f32[3,64,128]{2,1,0:T(8,128)S(1)} %pad_maximum_fusion.1), channel_id=1, source_target_pairs={{0,1},{1,2},{2,3},{4,5},{5,6},{6,7},{8,9},{9,10},{10,11},{12,13},{... | collective-permute-start | bytes 294920 | tf_op jit(solution)/shard_map/ppermute | solution.py:300
  10.1 0.7 copy-start.2
  10.1 0.7 copy-start.3
  15.9 10.5 %collective-permute-start.3 = (f32[64,128]{1,0:T(8,128)S(1)}, f32[64,128]{1,0:T(8,128)S(1)}, u32[]{:S(2)}, u32[]{:S(2)}) collective-permute-start(f32[64,128]{1,0:T(8,128)S(1)} %get-tuple-element.8), channel_id=1, source_target_pairs={{0,2},{4,6},{8,10},{12,14},{16,18},{20,22},{24,26},{28,30}} | collective-permute-start | bytes 98312 | tf_op jit(solution)/shard_map/ppermute | solution.py:353
  20.9 5.5 %collective-permute-start.2 = (f32[64,128]{1,0:T(8,128)S(1)}, f32[64,128]{1,0:T(8,128)S(1)}, u32[]{:S(2)}, u32[]{:S(2)}) collective-permute-start(f32[64,128]{1,0:T(8,128)S(1)} %get-tuple-element.8), channel_id=1, source_target_pairs={{0,1},{2,3},{4,5},{6,7},{8,9},{10,11},{12,13},{14,15},{16,17},{18,... | collective-permute-start | bytes 98312 | tf_op jit(solution)/shard_map/ppermute | solution.py:353
  23.3 0.7 copy-start.4
  31.7 83.9 %all-to-all-start = ((f32[32,64,128]{2,1,0:T(8,128)}), f32[32,64,128]{2,1,0:T(8,128)S(1)}, u32[]{:S(2)}, u32[]{:S(2)}) async-start(f32[32,64,128]{2,1,0:T(8,128)} %bitcast.5), calls=%async_computation | async-start | bytes 2097152 | tf_op jit(solution)/shard_map/all_to_all | solution.py:372
  36.7 0.7 copy-start.5

commit v2 on v1

--- a/solution.py
+++ b/solution.py
@@ -319,7 +319,14 @@
     )(levels)
 
     me = lax.axis_index("grid") * dom_count + lax.axis_index("dom")
-    keys = lax.all_gather(owner_list * SLOTS + slot_list, ("grid", "dom"), axis=0, tiled=True)
+    own_keys = owner_list * SLOTS + slot_list
+    keys = lax.all_to_all(
+        jnp.broadcast_to(own_keys[:, None], (devices, 1, blocks)),
+        ("grid", "dom"),
+        split_axis=0,
+        concat_axis=0,
+        tiled=True,
+    )[:, 0]
     mine = (keys // SLOTS) == me
     rank = jnp.cumsum(mine.astype(jnp.int32), axis=1)
     at_rank = mine[:, None, :] & (

time: 153 us -> 103 us (0.67)
  blocking collectives: 110 us -> 29.3 us
  waiting for transfers between devices: 1.86 us -> 27.2 us
  starting transfers between devices: 17.3 us -> 23.1 us
    all_gather x1 -> x0, blocking collectives: 77.2 us -> none  [body(): lax.all_gather(owner_list * SLOTS + slot_list, ('grid', 'dom'), axis=0, t...]
    all_to_all x1, waiting for transfers between devices: 0.01 us -> 25.3 us  [exchange(): lax.all_to_all(x.reshape(devices, capacity * 8, LANES), ('grid', 'dom'),...]
    all_to_all x0 -> x1, starting transfers between devices: none -> 5.03 us  [body(): lax.all_to_all(jnp.broadcast_to(own_keys[:, None], (devices, 1, blocks)),...]
    all_to_all x1, blocking collectives: 33.1 us -> 29.3 us  [exchange(): lax.all_to_all(x.reshape(devices, capacity * 8, LANES), ('grid', 'dom'),...]
  transfers between devices with their start and end apart: 5 -> 6, of which waited for: 2 -> 3; matrix products, arithmetic and copies ran while one was open for 1% -> 2% of each run, Pallas kernels for 2% -> 9%
where the time goes in v2:
time: 103 us
  blocking collectives  29.3 us (28%)
  waiting for transfers between devices  27.2 us (26%)
  starting transfers between devices  23.1 us (22%)
  Pallas kernels  18 us (17%)
  local copies, waits for them, and re-layouts  3.45 us (3%)
  other arithmetic  1.04 us (1%)
    all_to_all x1, blocking collectives, exchange(): lax.all_to_all(x.reshape(devices, capacity * 8, LANES), ('grid', 'dom'),...  29.3 us
    all_to_all x1, waiting for transfers between devices, exchange(): lax.all_to_all(x.reshape(devices, capacity * 8, LANES), ('grid', 'dom'),...  25.3 us
    ppermute x2, starting transfers between devices, body(): part = lax.ppermute(lead, 'dom', pair)  6.26 us
    all_to_all x1, starting transfers between devices, exchange(): lax.all_to_all(x.reshape(devices, capacity * 8, LANES), ('grid', 'dom'),...  5.84 us
    pallas_call x1, Pallas kernels, body(): pl.pallas_call(pack_kernel, out_shape=f32(devices * capacity, 8, LANES),...  5.26 us
    pallas_call x1, Pallas kernels, body(): pl.pallas_call(steps_kernel, out_shape=(f32(TILES, 24, LANES), f32(TILES,...  5.17 us
    all_to_all x1, starting transfers between devices, body(): lax.all_to_all(jnp.broadcast_to(own_keys[:, None], (devices, 1, blocks)),...  5.03 us
    ppermute x1, starting transfers between devices, body(): low = lax.ppermute(low_rows.reshape(3, TILES, LANES), 'dom', up)  4.66 us
  transfers between devices with their start and end apart: 6, of which 3 were waited for; matrix products, arithmetic and copies ran while one was open for 2% of the time, Pallas kernels for 9%

profile of v2, /device:TPU:1, one launch (start us, length us, event | category | flops | bytes accessed | tf_op | source)
XLA Modules:
  0.0 102.9 jit_solution(13577000525044361935)
XLA Ops:
  0.0 1.0 %slice_bitcast_fusion.1 = f32[1,2,64,128]{3,1,2,0:T(2,128)S(1)} fusion(f32[1,16,8192]{2,1,0:T(8,128)} %param.8), kind=kLoop, calls=%fused_computation.7 | loop fusion | bytes 131072
  1.0 0.0 copy-start
  1.1 1.0 slice_bitcast_fusion
  2.1 1.3 %collective-permute-start.1 = (f32[5,64,128]{2,1,0:T(8,128)S(1)}, f32[5,64,128]{2,1,0:T(8,128)S(1)}, u32[]{:S(2)}, u32[]{:S(2)}) collective-permute-start(f32[5,64,128]{2,1,0:T(8,128)S(1)} %pad_maximum_fusion), channel_id=1, source_target_pairs={{1,0},{2,1},{3,2},{5,4},{6,5},{7,6},{9,8},{10,9},{11,10},{13,12},{... | collective-permute-start | bytes 491528 | tf_op jit(solution)/shard_map/ppermute | solution.py:301
  3.4 0.0 copy-done.1
  3.5 0.0 copy-done
  3.6 4.7 %collective-permute-start = (f32[3,64,128]{2,1,0:T(8,128)S(1)}, f32[3,64,128]{2,1,0:T(8,128)S(1)}, u32[]{:S(2)}, u32[]{:S(2)}) collective-permute-start(f32[3,64,128]{2,1,0:T(8,128)S(1)} %pad_maximum_fusion.1), channel_id=1, source_target_pairs={{0,1},{1,2},{2,3},{4,5},{5,6},{6,7},{8,9},{9,10},{10,11},{12,13},{... | collective-permute-start | bytes 294920 | tf_op jit(solution)/shard_map/ppermute | solution.py:300
  8.2 1.6 %collective-permute-done.low = f32[3,64,128]{2,1,0:T(8,128)S(1)} collective-permute-done((f32[3,64,128]{2,1,0:T(8,128)S(1)}, f32[3,64,128]{2,1,0:T(8,128)S(1)}, u32[]{:S(2)}, u32[]{:S(2)}) %collective-permute-start) | collective-permute-done | bytes 98336 | tf_op jit(solution)/shard_map/ppermute | solution.py:300
  9.9 0.2 collective-permute-done.1.high
  10.1 0.7 copy-done.2
  10.7 0.0 copy-done.3
  10.8 5.2 %steps.1 = (f32[64,24,128]{2,1,0:T(8,128)S(1)}, f32[64,128]{1,0:T(8,128)S(1)}) custom-call(s32[1,3]{1,0:T(1,128)S(1)} %copy-done.2, f32[4]{0:T(128)S(1)} %copy-done.3, f32[16,8192]{1,0:T(8,128)S(1)} %bitcast.37, f32[16,8192]{1,0:T(8,128)S(1)} %bitcast.38, f32[3,64,128]{2,1,0:T(8,128)S(1)} %collective-permute-done.low, ...), custom_call_target="tpu_custom_call" | custom-call | tf_op jit(solution)/shard_map/steps/pallas_call | solution.py:337
  15.9 0.0 copy-start.4
  15.9 0.0 copy-start.5
  16.0 5.0 %collective-permute-start.3 = (f32[64,128]{1,0:T(8,128)S(1)}, f32[64,128]{1,0:T(8,128)S(1)}, u32[]{:S(2)}, u32[]{:S(2)}) collective-permute-start(f32[64,128]{1,0:T(8,128)S(1)} %get-tuple-element.8), channel_id=1, source_target_pairs={{0,2},{4,6},{8,10},{12,14},{16,18},{20,22},{24,26},{28,30}} | collective-permute-start | bytes 98312 | tf_op jit(solution)/shard_map/ppermute | solution.py:360
  20.9 1.3 %collective-permute-start.2 = (f32[64,128]{1,0:T(8,128)S(1)}, f32[64,128]{1,0:T(8,128)S(1)}, u32[]{:S(2)}, u32[]{:S(2)}) collective-permute-start(f32[64,128]{1,0:T(8,128)S(1)} %get-tuple-element.8), channel_id=1, source_target_pairs={{0,1},{2,3},{4,5},{6,7},{8,9},{10,11},{12,13},{14,15},{16,17},{18,... | collective-permute-start | bytes 98312 | tf_op jit(solution)/shard_map/ppermute | solution.py:360
  22.2 0.0 copy-done.4
  22.3 0.6 broadcast_in_dim.30
  22.9 5.0 %all-to-all-start = ((s32[32,1,128]{2,1,0:T(1,128)}), s32[32,1,128]{2,1,0:T(1,128)S(1)}, u32[]{:S(2)}, u32[]{:S(2)}) async-start(s32[32,1,128]{2,1,0:T(1,128)} %broadcast_in_dim.30), calls=%async_computation | async-start | bytes 32768 | tf_op jit(solution)/shard_map/all_to_all | solution.py:323
  27.9 2.3 %places.1 = s32[128]{0:T(128)S(1)} custom-call(s32[1,128]{1,0:T(1,128)S(1)} %copy-done.4), custom_call_target="tpu_custom_call" | custom-call | tf_op jit(solution)/shard_map/places/pallas_call | solution.py:303
  30.3 1.1 %lane_matrix.1.lanes = f32[256,128]{1,0:T(8,128)S(1)} custom-call(s32[1,3]{1,0:T(1,128)S(1)} %copy-done.2), custom_call_target="tpu_custom_call" | custom-call | tf_op jit(solution)/shard_map/lane_matrix/pallas_call | solution.py:312
  32.1 0.0 collective-permute-done.3
  32.1 0.0 collective-permute-done.2
  32.1 5.3 %pack.1 = f32[256,8,128]{2,1,0:T(8,128)} custom-call(s32[1,3]{1,0:T(1,128)S(1)} %copy-done.2, s32[1]{0:T(128)S(6)} %copy.25.sign, s32[128]{0:T(128)S(1)} %places.1, f32[64,24,128]{2,1,0:T(8,128)S(1)} %get-tuple-element.7.v_in, f32[64,128]{1,0:T(8,128)S(1)} %add.40.coarse, f32[256,128]{1,0:T(8,128)S(1)} %lane_matrix.1.lanes), custom_call_target="tpu_custom_call" | custom-call | tf_op jit(solution)/shard_map/pack/pallas_call | solution.py:364
  37.4 0.0 all-to-all-done
  37.4 5.8 %all-to-all-start.1 = ((f32[32,64,128]{2,1,0:T(8,128)}), f32[32,64,128]{2,1,0:T(8,128)S(1)}, u32[]{:S(2)}, u32[]{:S(2)}) async-start(f32[32,64,128]{2,1,0:T(8,128)} %bitcast.7), calls=%async_computation.1 | async-start | bytes 2097152 | tf_op jit(solution)/shard_map/all_to_all | solution.py:379
  43.3 0.3 reduce_window_sum.14
  43.6 0.7 select_reduce_fusion
  44.3 25.3 %all-to-all-done.1 = f32[32,64,128]{2,1,0:T(8,128)S(1)} async-done(((f32[32,64,128]{2,1,0:T(8,128)}), f32[32,64,128]{2,1,0:T(8,128)S(1)}, u32[]{:S(2)}, u32[]{:S(2)}) %all-to-all-start.1) | async-done | bytes 1048608 | tf_op jit(solution)/shard_map/all_to_all | solution.py:379
  69.6 2.4 %sum_pieces.1 = f32[256,8,128]{2,1,0:T(8,128)S(1)} custom-call(s32[32,8]{1,0:T(8,128)S(1)} %broadcast_add_fusion.table, f32[256,8,128]{2,1,0:T(8,128)S(1)} %bitcast.34), custom_call_target="tpu_custom_call" | custom-call | tf_op jit(solution)/shard_map/sum_pieces/pallas_call | solution.py:388
  71.9 29.3 %all_to_all.15 = f32[32,64,128]{2,1,0:T(8,128)S(1)} all-to-all(f32[32,64,128]{2,1,0:T(8,128)S(1)} %bitcast.35), channel_id=1, replica_groups=mesh['grid'=8,'dom'=4] {'grid','dom'}, dimensions={0} | all-to-all | bytes 2097152 | tf_op jit(solution)/shard_map/all_to_all | solution.py:379
  101.2 1.7 %unpack.1 = f32[16,8192]{1,0:T(8,128)} custom-call(s32[128]{0:T(128)S(1)} %places.1, f32[256,8,128]{2,1,0:T(8,128)S(1)} %bitcast.36), custom_call_target="tpu_custom_call" | custom-call | tf_op jit(solution)/shard_map/unpack/pallas_call | solution.py:398
  (17 shorter events, 0.2 us)
Async XLA Ops:
  0.0 3.4 %copy-start.1 = (f32[1,16,8192]{2,1,0:T(8,128)S(1)}, f32[1,16,8192]{2,1,0:T(8,128)}, u32[]{:S(2)}) copy-start(f32[1,16,8192]{2,1,0:T(8,128)} %param.8) | copy-start | bytes 1572868
  1.0 2.4 %copy-start = (f32[1,16,8192]{2,1,0:T(8,128)S(1)}, f32[1,16,8192]{2,1,0:T(8,128)}, u32[]{:S(2)}) copy-start(f32[1,16,8192]{2,1,0:T(8,128)} %param.7) | copy-start | bytes 1572868
  2.1 8.0 %collective-permute-start.1 = (f32[5,64,128]{2,1,0:T(8,128)S(1)}, f32[5,64,128]{2,1,0:T(8,128)S(1)}, u32[]{:S(2)}, u32[]{:S(2)}) collective-permute-start(f32[5,64,128]{2,1,0:T(8,128)S(1)} %pad_maximum_fusion), channel_id=1, source_target_pairs={{1,0},{2,1},{3,2},{5,4},{6,5},{7,6},{9,8},{10,9},{11,10},{13,12},{... | collective-permute-start | bytes 491528 | tf_op jit(solution)/shard_map/ppermute | solution.py:301
  3.6 6.3 %collective-permute-start = (f32[3,64,128]{2,1,0:T(8,128)S(1)}, f32[3,64,128]{2,1,0:T(8,128)S(1)}, u32[]{:S(2)}, u32[]{:S(2)}) collective-permute-start(f32[3,64,128]{2,1,0:T(8,128)S(1)} %pad_maximum_fusion.1), channel_id=1, source_target_pairs={{0,1},{1,2},{2,3},{4,5},{5,6},{6,7},{8,9},{9,10},{10,11},{12,13},{... | collective-permute-start | bytes 294920 | tf_op jit(solution)/shard_map/ppermute | solution.py:300
  10.1 0.7 copy-start.2
  10.1 0.7 copy-start.3
  15.9 6.3 %copy-start.4 = (s32[1,128]{1,0:T(1,128)S(1)}, s32[1,128]{1,0:T(1,128)}, u32[]{:S(2)}) copy-start(s32[1,128]{1,0:T(1,128)} %owners.1) | copy-start | bytes 1540
  15.9 6.3 %copy-start.5 = (s32[1,128]{1,0:T(1,128)S(1)}, s32[1,128]{1,0:T(1,128)}, u32[]{:S(2)}) copy-start(s32[1,128]{1,0:T(1,128)} %param.13) | copy-start | bytes 1540
  16.0 16.1 %collective-permute-start.3 = (f32[64,128]{1,0:T(8,128)S(1)}, f32[64,128]{1,0:T(8,128)S(1)}, u32[]{:S(2)}, u32[]{:S(2)}) collective-permute-start(f32[64,128]{1,0:T(8,128)S(1)} %get-tuple-element.8), channel_id=1, source_target_pairs={{0,2},{4,6},{8,10},{12,14},{16,18},{20,22},{24,26},{28,30}} | collective-permute-start | bytes 98312 | tf_op jit(solution)/shard_map/ppermute | solution.py:360
  20.9 11.2 %collective-permute-start.2 = (f32[64,128]{1,0:T(8,128)S(1)}, f32[64,128]{1,0:T(8,128)S(1)}, u32[]{:S(2)}, u32[]{:S(2)}) collective-permute-start(f32[64,128]{1,0:T(8,128)S(1)} %get-tuple-element.8), channel_id=1, source_target_pairs={{0,1},{2,3},{4,5},{6,7},{8,9},{10,11},{12,13},{14,15},{16,17},{18,... | collective-permute-start | bytes 98312 | tf_op jit(solution)/shard_map/ppermute | solution.py:360
  22.9 14.5 %all-to-all-start = ((s32[32,1,128]{2,1,0:T(1,128)}), s32[32,1,128]{2,1,0:T(1,128)S(1)}, u32[]{:S(2)}, u32[]{:S(2)}) async-start(s32[32,1,128]{2,1,0:T(1,128)} %broadcast_in_dim.30), calls=%async_computation | async-start | bytes 32768 | tf_op jit(solution)/shard_map/all_to_all | solution.py:323
  37.4 32.2 %all-to-all-start.1 = ((f32[32,64,128]{2,1,0:T(8,128)}), f32[32,64,128]{2,1,0:T(8,128)S(1)}, u32[]{:S(2)}, u32[]{:S(2)}) async-start(f32[32,64,128]{2,1,0:T(8,128)} %bitcast.7), calls=%async_computation.1 | async-start | bytes 2097152 | tf_op jit(solution)/shard_map/all_to_all | solution.py:379

commit v3 on v1

--- a/solution.py
+++ b/solution.py
@@ -161,7 +161,7 @@
     out[LANES : 2 * LANES] = nxt
 
 
-def pack_kernel(levels, sign, places, v_in, coarse, lanes, out, x, y, stage):
+def pack_kernel(levels, sign, info, v_in, coarse, lanes, out, blocks, x, y, stage):
     place = lax.axis_index("dom")
     row = lax.broadcasted_iota(jnp.int32, (24, LANES), 0)
     for j in range(TILES):
@@ -230,49 +230,230 @@
         for i in range(2):
             stage[pl.ds(j + i * 8 * TILES, 8, stride=TILES), :] = tile[8 * i : 8 * i + 8]
     for b in range(16 * TILES // 8):
-        out[places[b]] = stage[pl.ds(8 * b, 8), :]
-
-
-def places_kernel(owners, out, seen, *, devices, capacity):
-    def clear(i, carry):
-        seen[i] = 0
-        return carry
-
-    lax.fori_loop(0, devices, clear, 0)
-
-    def one(b, carry):
-        owner = owners[0, b]
-        rank = seen[owner]
-        seen[owner] = rank + 1
-        out[b] = owner * capacity + rank
-        return carry
-
-    lax.fori_loop(0, owners.shape[1], one, 0)
-
-
-def sum_kernel(table, arrived, out, pieces):
-    pieces[...] = jnp.zeros_like(pieces)
-    devices, capacity = table.shape
-
-    def add(d, carry):
-        for i in range(capacity):
-            s = table[d, i]
-            pieces[s] = pieces[s] + arrived[d * capacity + i]
-        return carry
-
-    lax.fori_loop(0, devices, add, 0)
-
-    def give(d, carry):
-        for i in range(capacity):
-            out[d * capacity + i] = pieces[table[d, i]]
-        return carry
-
-    lax.fori_loop(0, devices, give, 0)
-
-
-def unpack_kernel(places, back, out, stage):
+        block = stage[pl.ds(8 * b, 8), :]
+        blocks[b] = block
+        out[info[0, b]] = block
+
+
+def key_parts(keys, rows):
+    owner = keys // SLOTS
+    slot = keys % SLOTS
+    row = owner % rows
+    lane = slot + SLOTS * (owner // rows)
+    return owner, slot, lane, row, (row + slot) % rows
+
+
+def hot(index, count):
+    which = lax.broadcasted_iota(jnp.int32, (count, index.shape[1]), 0)
+    return jnp.where(which == index, 1.0, 0.0)
+
+
+def dot_rows(left, right):
+    return lax.dot_general(
+        left.astype(jnp.bfloat16),
+        right.astype(jnp.bfloat16),
+        (((1,), (1,)), ((), ())),
+        preferred_element_type=jnp.float32,
+    )
+
+
+def dot_plain(left, right):
+    return jnp.dot(
+        left.astype(jnp.bfloat16), right.astype(jnp.bfloat16), preferred_element_type=jnp.float32
+    )
+
+
+def mixed(handler, lane, row):
+    x = (handler * 40503 + lane * 30011 + row * 52711) & 0xFFFF
+    x = ((x ^ (x >> 7)) * 9973) & 0xFFFF
+    x = ((x ^ (x >> 5)) * 12347) & 0xFFFF
+    return (x >> 8).astype(jnp.float32) * (1.0 / 256.0)
+
+
+def handlers_of(assigned, lane, row):
+    return jnp.sum(
+        hot(row, assigned.shape[0]) * dot_plain(assigned, hot(lane, LANES)), axis=0, keepdims=True
+    )
+
+
+def device_number():
+    return lax.axis_index("grid") * lax.axis_size("dom") + lax.axis_index("dom")
+
+
+def write_places(info, handler, ok, me, devices, capacity):
+    taken = hot(handler.astype(jnp.int32), devices)
+    size = handler.shape[1]
+    first = lax.broadcasted_iota(jnp.int32, (size, size), 0)
+    second = lax.broadcasted_iota(jnp.int32, (size, size), 1)
+    before = dot_plain(taken, jnp.where(first < second, 1.0, 0.0))
+    rank = jnp.sum(taken * before, axis=0, keepdims=True)
+    place = handler.astype(jnp.int32) * capacity + rank.astype(jnp.int32)
+    stays = handler == me.astype(jnp.float32)
+    send = jnp.where(stays, devices * capacity, place)
+    get = jnp.where(stays, 0, place)
+    kept = jnp.where(stays, 1, 0)
+    flag = jnp.broadcast_to(ok, kept.shape).astype(jnp.int32)
+    rows = [send, get, kept, flag, flag, flag, flag, flag]
+    info[...] = jnp.concatenate(rows, axis=0)
+
+
+def owner_places_kernel(keys, info, *, devices, capacity):
+    me = device_number()
+    owner = (keys[pl.ds(me, 1), :] // SLOTS).astype(jnp.float32)
+    write_places(info, owner, jnp.int32(0), me, devices, capacity)
+
+
+def balance_kernel(keys, assigned, info, one, two, table, *, devices, capacity, full):
+    rows = devices * SLOTS // LANES
+    keys_all = keys[...]
+    _, _, lane_all, row_one, row_two = key_parts(keys_all, rows)
+    for d in range(devices):
+        pick = slice(d, d + 1)
+        both = jnp.concatenate([hot(row_one[pick], rows), hot(row_two[pick], rows)], axis=0)
+        counts = dot_rows(both, hot(lane_all[pick], LANES))
+        one[pl.ds(d, rows, stride=devices), :] = counts[:rows]
+        two[pl.ds(d, rows, stride=devices), :] = counts[rows:]
+
+    square = (devices, devices)
+    own = lax.broadcasted_iota(jnp.int32, square, 0) == lax.broadcasted_iota(jnp.int32, square, 1)
+
+    def price(load, steep):
+        value = jnp.exp2(load * 0.3785) + steep * jnp.maximum(load - (capacity - 1), 0.0)
+        return jnp.where(own, 0.0, value)
+
+    def settle(counts_ref, group, first, load, number):
+        base = number * group
+        counts = jnp.concatenate(
+            [
+                counts_ref[pl.ds(pl.multiple_of((base + i) * devices, devices), devices), :]
+                for i in range(group)
+            ],
+            axis=1,
+        )
+        shape = (devices, group * LANES)
+        handler = lax.broadcasted_iota(jnp.int32, shape, 0)
+        column = lax.broadcasted_iota(jnp.int32, shape, 1)
+        handler_f = handler.astype(jnp.float32)
+        cost = dot_plain(price(load, 4.0 if first else 8.0), counts)
+        was = None
+        if not first:
+            old = jnp.concatenate([table[pl.ds(base + i, 1), :] for i in range(group)], axis=1)
+            was = handler_f == old
+            cost = jnp.where(was, dot_plain(price(load - 1.0, 8.0), counts) - 1.0, cost)
+        noise = 0.5 * mixed(handler, column % LANES, base + column // LANES)
+        ranked = jnp.floor((jnp.minimum(cost, 4000.0) + noise) * 64.0) * devices + handler_f
+        least = jnp.min(ranked, axis=0, keepdims=True)
+        chosen = least - jnp.floor(least * (1.0 / devices)) * devices
+        for i in range(group):
+            table[pl.ds(base + i, 1), :] = chosen[:, i * LANES : (i + 1) * LANES]
+        change = jnp.where(handler_f == chosen, 1.0, 0.0)
+        if not first:
+            change = change - jnp.where(was, 1.0, 0.0)
+        return load + dot_rows(change, counts)
+
+    load = jnp.zeros(square, jnp.float32)
+    load = lax.fori_loop(0, rows // 2, lambda i, x: settle(one, 2, True, x, i), load)
+    spot = lax.broadcasted_iota(jnp.int32, (rows, LANES), 0)
+    lane = lax.broadcasted_iota(jnp.int32, (rows, LANES), 1)
+    from_row = (spot + rows - (lane % SLOTS) % rows) % rows
+    moved = jnp.zeros((rows, LANES), jnp.float32)
+    for r in range(rows):
+        moved = jnp.where(from_row == r, table[r : r + 1, :], moved)
+    table[...] = moved
+    load = lax.fori_loop(0, rows // 2, lambda i, x: settle(two, 2, False, x, i), load)
+    load = lax.fori_loop(0, rows // 4, lambda i, x: settle(two, 4, False, x, i), load)
+
+    ok = jnp.max(jnp.where(own, 0.0, load)) <= capacity
+    owner = (from_row + rows * (lane // SLOTS)).astype(jnp.float32)
+    final = jnp.where(ok, table[...], owner)
+    assigned[...] = final
+    me = device_number()
+    _, _, my_lane, _, my_row = key_parts(keys[pl.ds(me, 1), :], rows)
+    handler = handlers_of(final, my_lane, my_row)
+    size = jnp.where(ok, capacity, full)
+    write_places(info, handler, ok.astype(jnp.int32), me, devices, size)
+
+
+def table_kernel(*refs, devices, capacity, pieces, balanced):
+    if balanced:
+        keys, assigned, out, handlers = refs
+        rows = devices * SLOTS // LANES
+        table = assigned[...]
+        _, _, lane_all, _, row_all = key_parts(keys[...], rows)
+        for d in range(devices):
+            handlers[d : d + 1, :] = handlers_of(table, lane_all[d : d + 1], row_all[d : d + 1])
+        piece = keys[...]
+    else:
+        keys, out, handlers = refs
+        handlers[...] = (keys[...] // SLOTS).astype(jnp.float32)
+        piece = keys[...] % SLOTS
+    me = device_number()
+    size = keys.shape[1]
+    mine = handlers[...] == me.astype(jnp.float32)
+    sender = lax.broadcasted_iota(jnp.int32, (devices, size), 0)
+    first = lax.broadcasted_iota(jnp.int32, (size, size), 0)
+    second = lax.broadcasted_iota(jnp.int32, (size, size), 1)
+    rank = dot_plain(jnp.where(mine, 1.0, 0.0), jnp.where(first <= second, 1.0, 0.0))
+    comes = mine & (sender != me)
+    column = lax.broadcasted_iota(jnp.int32, (devices, size), 1)
+    found = jnp.full((devices, size), pieces, jnp.int32)
+    for r in range(capacity):
+        hit = comes & (rank == r + 1.0)
+        at = jnp.sum(jnp.where(hit, piece - pieces, 0), axis=1, keepdims=True)
+        found = jnp.where(column == r, pieces + at, found)
+    out[0:devices, :] = found
+    kept = jnp.sum(
+        jnp.where(mine & (sender == me), piece - pieces, 0), axis=0, keepdims=True
+    )
+    out[devices : devices + 8, :] = jnp.broadcast_to(kept + pieces, (8, size))
+
+
+def sum_kernel(table, arrived, own, out, own_out, pieces, *, devices, capacity):
+    blocks = own.shape[0]
+    zero = jnp.zeros((8, LANES), jnp.float32)
+
+    def over_senders(act):
+        def one(d, carry):
+            for i in range(capacity):
+                act(table[d, i], d * capacity + i)
+            return carry
+
+        lax.fori_loop(0, devices, one, 0, unroll=2)
+
+    def over_kept(act):
+        def one(k, carry):
+            for i in range(8):
+                act(table[devices, 8 * k + i], 8 * k + i)
+            return carry
+
+        lax.fori_loop(0, blocks // 8, one, 0)
+
+    def clear(piece, at):
+        pieces[piece] = zero
+
+    def add(piece, at):
+        pieces[piece] = pieces[piece] + arrived[at]
+
+    def add_own(piece, at):
+        pieces[piece] = pieces[piece] + own[at]
+
+    def give(piece, at):
+        out[at] = pieces[piece]
+
+    def give_own(piece, at):
+        own_out[at] = pieces[piece]
+
+    over_senders(clear)
+    over_kept(clear)
+    over_senders(add)
+    over_kept(add_own)
+    over_senders(give)
+    over_kept(give_own)
+
+
+def unpack_kernel(info, back, own, out, stage):
     for b in range(16 * TILES // 8):
-        stage[pl.ds(8 * b, 8), :] = back[places[b]]
+        stage[pl.ds(8 * b, 8), :] = jnp.where(info[2, b] != 0, own[b], back[info[1, b]])
     for j in range(TILES):
         for i in range(2):
             out[8 * i : 8 * i + 8, j * LANES : (j + 1) * LANES] = stage[
@@ -293,6 +474,15 @@
     blocks = owner_list.shape[1]
     capacity = 2 * blocks // devices
 
+    own_keys = owner_list * SLOTS + slot_list
+    keys = lax.all_to_all(
+        jnp.broadcast_to(own_keys[:, None], (devices, 1, blocks)),
+        ("grid", "dom"),
+        split_axis=0,
+        concat_axis=0,
+        tiled=True,
+    )[:, 0]
+
     up = [(i, i + 1) for i in range(dom_count - 1)]
     down = [(i + 1, i) for i in range(dom_count - 1)]
     low_rows = jnp.concatenate([conc[rows - 2 :], dif[rows - 1 :]], axis=0)
@@ -300,15 +490,6 @@
     low = lax.ppermute(low_rows.reshape(3, TILES, LANES), "dom", up)
     high = lax.ppermute(high_rows.reshape(5, TILES, LANES), "dom", down)
 
-    places = pl.pallas_call(
-        functools.partial(places_kernel, devices=devices, capacity=capacity),
-        out_shape=jax.ShapeDtypeStruct((blocks,), jnp.int32),
-        in_specs=[SM],
-        out_specs=SM,
-        scratch_shapes=[pltpu.SMEM((devices,), jnp.int32)],
-        compiler_params=params(),
-        name="places",
-    )(owner_list)
     lanes = pl.pallas_call(
         lane_kernel,
         out_shape=f32(2 * LANES, LANES),
@@ -317,15 +498,6 @@
         compiler_params=params(),
         name="lane_matrix",
     )(levels)
-
-    me = lax.axis_index("grid") * dom_count + lax.axis_index("dom")
-    keys = lax.all_gather(owner_list * SLOTS + slot_list, ("grid", "dom"), axis=0, tiled=True)
-    mine = (keys // SLOTS) == me
-    rank = jnp.cumsum(mine.astype(jnp.int32), axis=1)
-    at_rank = mine[:, None, :] & (
-        rank[:, None, :] == jnp.arange(1, capacity + 1, dtype=jnp.int32)[None, :, None]
-    )
-    table = SLOTS + jnp.sum(jnp.where(at_rank, (keys % SLOTS - SLOTS)[:, None, :], 0), axis=2)
 
     stepped, lead = pl.pallas_call(
         steps_kernel,
@@ -341,6 +513,35 @@
         name="steps",
     )(levels, velocity, conc, dif, low, high)
 
+    balanced = capacity >= 8 and devices * SLOTS % LANES == 0 and devices <= 64
+    info_shape = jax.ShapeDtypeStruct((8, blocks), jnp.int32)
+    if balanced:
+        key_rows = devices * SLOTS // LANES
+        assigned, info = pl.pallas_call(
+            functools.partial(
+                balance_kernel, devices=devices, capacity=capacity // 2, full=capacity
+            ),
+            out_shape=(f32(key_rows, LANES), info_shape),
+            in_specs=[VM],
+            out_specs=(VM, VM),
+            scratch_shapes=[
+                pltpu.VMEM((key_rows * devices, LANES), jnp.float32),
+                pltpu.VMEM((key_rows * devices, LANES), jnp.float32),
+                pltpu.VMEM((key_rows, LANES), jnp.float32),
+            ],
+            compiler_params=params(),
+            name="balance",
+        )(keys)
+    else:
+        info = pl.pallas_call(
+            functools.partial(owner_places_kernel, devices=devices, capacity=capacity),
+            out_shape=info_shape,
+            in_specs=[VM],
+            out_specs=VM,
+            compiler_params=params(),
+            name="places",
+        )(keys)
+
     coarse = None
     distance = 1
     while distance < dom_count:
@@ -354,49 +555,71 @@
                 coarse = part if coarse is None else coarse + part
         distance *= 2
 
-    outgoing = pl.pallas_call(
-        pack_kernel,
-        out_shape=f32(devices * capacity, 8, LANES),
-        in_specs=[SM, SM, SM, VM, VM, VM],
-        out_specs=VM,
-        scratch_shapes=[
-            pltpu.VMEM((TILES + 1, 16, LANES), jnp.float32),
-            pltpu.VMEM((TILES + 64, 16, LANES), jnp.float32),
-            pltpu.VMEM((16 * TILES, LANES), jnp.float32),
-        ],
-        compiler_params=params(),
-        name="pack",
-    )(levels, grid_signs, places, stepped, coarse, lanes)
-
-    def exchange(x):
-        return lax.all_to_all(
-            x.reshape(devices, capacity * 8, LANES),
-            ("grid", "dom"),
-            split_axis=0,
-            concat_axis=0,
-            tiled=True,
-        ).reshape(devices * capacity, 8, LANES)
-
-    arrived = exchange(outgoing)
-    returned = pl.pallas_call(
-        sum_kernel,
-        out_shape=f32(devices * capacity, 8, LANES),
-        in_specs=[SM, VM],
-        out_specs=VM,
-        scratch_shapes=[pltpu.VMEM((SLOTS + 8, 8, LANES), jnp.float32)],
-        compiler_params=params(),
-        name="sum_pieces",
-    )(table, arrived)
-    back = exchange(returned)
-    combined = pl.pallas_call(
-        unpack_kernel,
-        out_shape=f32(rows, TILES * LANES),
-        in_specs=[SM, VM],
-        out_specs=VM,
-        scratch_shapes=[pltpu.VMEM((16 * TILES, LANES), jnp.float32)],
-        compiler_params=params(),
-        name="unpack",
-    )(places, back)
+    def route(slots, balanced, tables):
+        pieces = devices * SLOTS if balanced else SLOTS
+
+        def exchange(x):
+            return lax.all_to_all(
+                x.reshape(devices, slots * 8, LANES),
+                ("grid", "dom"),
+                split_axis=0,
+                concat_axis=0,
+                tiled=True,
+            ).reshape(devices * slots, 8, LANES)
+
+        outgoing, own = pl.pallas_call(
+            pack_kernel,
+            out_shape=(f32(devices * slots + 1, 8, LANES), f32(blocks, 8, LANES)),
+            in_specs=[SM, SM, SM, VM, VM, VM],
+            out_specs=(VM, VM),
+            scratch_shapes=[
+                pltpu.VMEM((TILES + 1, 16, LANES), jnp.float32),
+                pltpu.VMEM((TILES + 64, 16, LANES), jnp.float32),
+                pltpu.VMEM((16 * TILES, LANES), jnp.float32),
+            ],
+            compiler_params=params(),
+            name="pack",
+        )(levels, grid_signs, info, stepped, coarse, lanes)
+        arrived = exchange(outgoing[: devices * slots])
+        table = pl.pallas_call(
+            functools.partial(
+                table_kernel, devices=devices, capacity=slots, pieces=pieces, balanced=balanced
+            ),
+            out_shape=jax.ShapeDtypeStruct((devices + 8, blocks), jnp.int32),
+            in_specs=[VM] * len(tables),
+            out_specs=VM,
+            scratch_shapes=[pltpu.VMEM((devices, blocks), jnp.float32)],
+            compiler_params=params(),
+            name="piece_table",
+        )(*tables)
+        returned, own_back = pl.pallas_call(
+            functools.partial(sum_kernel, devices=devices, capacity=slots),
+            out_shape=(f32(devices * slots, 8, LANES), f32(blocks, 8, LANES)),
+            in_specs=[SM, VM, VM],
+            out_specs=(VM, VM),
+            scratch_shapes=[pltpu.VMEM((pieces + 8, 8, LANES), jnp.float32)],
+            compiler_params=params(),
+            name="sum_pieces",
+        )(table, arrived, own)
+        back = exchange(returned)
+        return pl.pallas_call(
+            unpack_kernel,
+            out_shape=f32(rows, TILES * LANES),
+            in_specs=[SM, VM, VM],
+            out_specs=VM,
+            scratch_shapes=[pltpu.VMEM((16 * TILES, LANES), jnp.float32)],
+            compiler_params=params(),
+            name="unpack",
+        )(info, back, own_back)
+
+    if balanced:
+        combined = lax.cond(
+            info[3, 0] != 0,
+            lambda: route(capacity // 2, True, (keys, assigned)),
+            lambda: route(capacity, True, (keys, assigned)),
+        )
+    else:
+        combined = route(capacity, False, (keys,))
     return combined[None]
 
 

time: 153 us -> 89.5 us (0.58)
  blocking collectives: 110 us -> 18.2 us
  waiting for transfers between devices: 1.86 us -> 22.1 us
  Pallas kernels: 17.9 us -> 21.9 us
  starting transfers between devices: 17.3 us -> 21.1 us
    all_gather x1 -> x0, blocking collectives: 77.2 us -> none  [body(): lax.all_gather(owner_list * SLOTS + slot_list, ('grid', 'dom'), axis=0, t...]
    all_to_all x1 -> x2, waiting for transfers between devices: 0.01 us -> 20.2 us  [the longest x1 14.8 us: exchange(): lax.all_to_all(x.reshape(devices, slots * 8, LANES), ('grid', 'dom'), spl...]
    all_to_all x1, blocking collectives: 33.1 us -> 18.2 us  [exchange(): lax.all_to_all(x.reshape(devices, slots * 8, LANES), ('grid', 'dom'), spl...]
    pallas_call x4 -> x5, Pallas kernels: 11.6 us -> 16.5 us  [the longest x1 6.67 us: body(): pl.pallas_call(functools.partial(balance_kernel, devices=devices, capacit...]
    all_to_all x1 -> x2, starting transfers between devices: 5.04 us -> 8.89 us  [the longest x1 5.94 us: body(): lax.all_to_all(jnp.broadcast_to(own_keys[:, None], (devices, 1, blocks)),...]
    unnamed x18 -> x20, local copies, waits for them, and re-layouts: 3.45 us -> 2.89 us
  transfers between devices with their start and end apart: 5 -> 6, of which waited for: 2 -> 4; matrix products, arithmetic and copies ran while one was open for 1% -> 1% of each run, Pallas kernels for 2% -> 9%
where the time goes in v3:
time: 89.5 us; the launch traced here: 89.2 us
  waiting for transfers between devices  22.1 us (25%)
  Pallas kernels  21.9 us (24%)
  starting transfers between devices  21.1 us (24%)
  blocking collectives  18.2 us (20%)
  local copies, waits for them, and re-layouts  4.88 us (5%)
    all_to_all x1, blocking collectives, exchange(): lax.all_to_all(x.reshape(devices, slots * 8, LANES), ('grid', 'dom'), spl...  18.2 us
    all_to_all x1, waiting for transfers between devices, exchange(): lax.all_to_all(x.reshape(devices, slots * 8, LANES), ('grid', 'dom'), spl...  14.8 us
    pallas_call x1, Pallas kernels, body(): pl.pallas_call(functools.partial(balance_kernel, devices=devices, capacit...  6.67 us
    ppermute x2, starting transfers between devices, body(): part = lax.ppermute(lead, 'dom', pair)  6.26 us
    all_to_all x1, starting transfers between devices, body(): lax.all_to_all(jnp.broadcast_to(own_keys[:, None], (devices, 1, blocks)),...  5.94 us
    all_to_all x1, waiting for transfers between devices, body(): lax.all_to_all(jnp.broadcast_to(own_keys[:, None], (devices, 1, blocks)),...  5.46 us
    pallas_call x1, Pallas kernels, route(): pl.pallas_call(pack_kernel, out_shape=(f32(devices * slots + 1, 8, LANES)...  5.01 us
    ppermute x1, starting transfers between devices, body(): low = lax.ppermute(low_rows.reshape(3, TILES, LANES), 'dom', up)  4.66 us
  transfers between devices with their start and end apart: 6, of which 4 were waited for; matrix products, arithmetic and copies ran while one was open for 1% of the time, Pallas kernels for 9%

profile of v3, /device:TPU:1, one launch (start us, length us, event | category | flops | bytes accessed | tf_op | source)
XLA Modules:
  0.0 89.2 jit_solution(12440499881402301966)
XLA Ops:
  0.0 0.0 copy-start.2
  0.0 1.1 %slice_bitcast_fusion.1 = f32[1,2,64,128]{3,1,2,0:T(2,128)S(1)} fusion(f32[1,16,8192]{2,1,0:T(8,128)} %param.10), kind=kLoop, calls=%fused_computation.6 | loop fusion | bytes 131072
  1.1 1.0 %slice_bitcast_fusion = f32[1,3,64,128]{3,1,2,0:T(4,128)S(1)} fusion(f32[1,16,8192]{2,1,0:T(8,128)} %param.9), kind=kLoop, calls=%fused_computation.1 | loop fusion | bytes 196608
  2.1 0.0 copy-start.5
  2.1 0.0 copy-start.6
  2.1 1.3 %collective-permute-start.1 = (f32[5,64,128]{2,1,0:T(8,128)S(1)}, f32[5,64,128]{2,1,0:T(8,128)S(1)}, u32[]{:S(2)}, u32[]{:S(2)}) collective-permute-start(f32[5,64,128]{2,1,0:T(8,128)S(1)} %pad_maximum_fusion), channel_id=1, source_target_pairs={{1,0},{2,1},{3,2},{5,4},{6,5},{7,6},{9,8},{10,9},{11,10},{13,12},{... | collective-permute-start | bytes 491528 | tf_op jit(solution)/shard_map/ppermute | solution.py:491
  3.6 4.7 %collective-permute-start = (f32[3,64,128]{2,1,0:T(8,128)S(1)}, f32[3,64,128]{2,1,0:T(8,128)S(1)}, u32[]{:S(2)}, u32[]{:S(2)}) collective-permute-start(f32[3,64,128]{2,1,0:T(8,128)S(1)} %pad_maximum_fusion.1), channel_id=1, source_target_pairs={{0,1},{1,2},{2,3},{4,5},{5,6},{6,7},{8,9},{9,10},{10,11},{12,13},{... | collective-permute-start | bytes 294920 | tf_op jit(solution)/shard_map/ppermute | solution.py:490
  8.2 1.6 %collective-permute-done.low = f32[3,64,128]{2,1,0:T(8,128)S(1)} collective-permute-done((f32[3,64,128]{2,1,0:T(8,128)S(1)}, f32[3,64,128]{2,1,0:T(8,128)S(1)}, u32[]{:S(2)}, u32[]{:S(2)}) %collective-permute-start) | collective-permute-done | bytes 98336 | tf_op jit(solution)/shard_map/ppermute | solution.py:490
  9.8 0.2 collective-permute-done.1.high
  10.1 4.2 %steps.1 = (f32[64,24,128]{2,1,0:T(8,128)S(1)}, f32[64,128]{1,0:T(8,128)S(1)}) custom-call(s32[1,3]{1,0:T(1,128)S(1)} %copy-done.4, f32[4]{0:T(128)S(1)} %copy-done.2, f32[16,8192]{1,0:T(8,128)S(1)} %bitcast.40, f32[16,8192]{1,0:T(8,128)S(1)} %bitcast.41, f32[3,64,128]{2,1,0:T(8,128)S(1)} %collective-permute-done.low, ...), custom_call_target="tpu_custom_call" | custom-call | tf_op jit(solution)/shard_map/steps/pallas_call | solution.py:502
  14.3 5.0 %collective-permute-start.3 = (f32[64,128]{1,0:T(8,128)S(1)}, f32[64,128]{1,0:T(8,128)S(1)}, u32[]{:S(2)}, u32[]{:S(2)}) collective-permute-start(f32[64,128]{1,0:T(8,128)S(1)} %get-tuple-element.72), channel_id=1, source_target_pairs={{0,2},{4,6},{8,10},{12,14},{16,18},{20,22},{24,26},{28,30}} | collective-permute-start | bytes 98312 | tf_op jit(solution)/shard_map/ppermute | solution.py:554
  19.3 1.3 %collective-permute-start.2 = (f32[64,128]{1,0:T(8,128)S(1)}, f32[64,128]{1,0:T(8,128)S(1)}, u32[]{:S(2)}, u32[]{:S(2)}) collective-permute-start(f32[64,128]{1,0:T(8,128)S(1)} %get-tuple-element.72), channel_id=1, source_target_pairs={{0,1},{2,3},{4,5},{6,7},{8,9},{10,11},{12,13},{14,15},{16,17},{18,... | collective-permute-start | bytes 98312 | tf_op jit(solution)/shard_map/ppermute | solution.py:554
  20.6 0.0 copy-done.5
  20.6 0.6 broadcast_in_dim.16
  21.3 5.9 %all-to-all-start.4 = ((s32[32,1,128]{2,1,0:T(1,128)}), s32[32,1,128]{2,1,0:T(1,128)S(1)}, u32[]{:S(2)}, u32[]{:S(2)}) async-start(s32[32,1,128]{2,1,0:T(1,128)} %broadcast_in_dim.16), calls=%async_computation.4 | async-start | bytes 32768 | tf_op jit(solution)/shard_map/all_to_all | solution.py:478
  27.2 1.1 %lane_matrix.1 = f32[256,128]{1,0:T(8,128)S(1)} custom-call(s32[1,3]{1,0:T(1,128)S(1)} %copy-done.4), custom_call_target="tpu_custom_call" | custom-call | tf_op jit(solution)/shard_map/lane_matrix/pallas_call | solution.py:493
  28.3 5.5 %all-to-all-done.4 = s32[32,1,128]{2,1,0:T(1,128)S(1)} async-done(((s32[32,1,128]{2,1,0:T(1,128)}), s32[32,1,128]{2,1,0:T(1,128)S(1)}, u32[]{:S(2)}, u32[]{:S(2)}) %all-to-all-start.4) | async-done | bytes 16416 | tf_op jit(solution)/shard_map/all_to_all | solution.py:478
  33.8 6.7 %balance.1 = (f32[16,128]{1,0:T(8,128)S(1)}, s32[8,128]{1,0:T(8,128)S(1)}) custom-call(s32[32,128]{1,0:T(8,128)S(1)} %bitcast.48), custom_call_target="tpu_custom_call" | custom-call | tf_op jit(solution)/shard_map/balance/pallas_call | solution.py:520
  40.5 0.5 slice.25
  41.7 0.0 collective-permute-done.3
  41.7 0.0 collective-permute-done.2
  41.7 46.7 %conditional.1 = (f32[1,16,8192]{2,1,0:T(8,128)S(1)}) conditional(s32[]{:T(128)} %bitcast.12, (s32[32,128]{1,0:T(8,128)S(1)}, f32[16,128]{1,0:T(8,128)S(1)}, s32[1,3]{1,0:T(1,128)S(1)}, s32[1]{0:T(128)}, s32[8,128]{1,0:T(8,128)S(1)}, /*index=5*/f32[64,24,128]{2,1,0:T(8,128)S(1)}, f32[64,128]{1,0:T(8,128)S(1)}, f32[256,128]{1,0:T(8,128)S(1)}, ...), branch_computations={%region_0.0_spmd, %region_1.0_spmd} | conditional | flops 8192 | bytes 7438376 | solution.py:616
  41.7 5.0 %pack.3 = (f32[129,8,128]{2,1,0:T(8,128)S(1)}, f32[128,8,128]{2,1,0:T(8,128)S(1)}) custom-call(s32[1,3]{1,0:T(1,128)S(1)} %get-tuple-element.56.levels, s32[1]{0:T(128)} %get-tuple-element.81.sign, s32[8,128]{1,0:T(8,128)S(1)} %get-tuple-element.53.info, f32[64,24,128]{2,1,0:T(8,128)S(1)} %get-tuple-element.58.v_in, f32[64,128]{1,0:T(8,128)S(1)} %add.9.coarse, ...), custom_call_target="tpu_custom_call" | custom-call | tf_op jit(solution)/shard_map/cond/branch_1_fun/pack/pallas_call | solution.py:570
  46.7 0.8 slice.19
  47.6 2.9 %all-to-all-start.2 = ((f32[32,32,128]{2,1,0:T(8,128)}), f32[32,32,128]{2,1,0:T(8,128)S(1)}, u32[]{:S(2)}, u32[]{:S(2)}) async-start(f32[32,32,128]{2,1,0:T(8,128)} %bitcast.5), calls=%async_computation.2 | async-start | bytes 1048576 | tf_op jit(solution)/shard_map/cond/branch_1_fun/all_to_all | solution.py:562
  50.5 0.6 piece_table.3.table
  51.2 14.8 %all-to-all-done.2 = f32[32,32,128]{2,1,0:T(8,128)S(1)} async-done(((f32[32,32,128]{2,1,0:T(8,128)}), f32[32,32,128]{2,1,0:T(8,128)S(1)}, u32[]{:S(2)}, u32[]{:S(2)}) %all-to-all-start.2) | async-done | bytes 524320 | tf_op jit(solution)/shard_map/cond/branch_1_fun/all_to_all | solution.py:562
  65.9 3.1 %sum_pieces.3 = (f32[128,8,128]{2,1,0:T(8,128)S(1)}, f32[128,8,128]{2,1,0:T(8,128)S(1)}) custom-call(s32[40,128]{1,0:T(8,128)S(1)} %piece_table.3.table, f32[128,8,128]{2,1,0:T(8,128)S(1)} %bitcast.38, f32[128,8,128]{2,1,0:T(8,128)S(1)} %get-tuple-element.62.own), custom_call_target="tpu_custom_call" | custom-call | tf_op jit(solution)/shard_map/cond/branch_1_fun/sum_pieces/pallas_call | solution.py:595
  69.0 18.2 %all_to_all.22 = f32[32,32,128]{2,1,0:T(8,128)S(1)} all-to-all(f32[32,32,128]{2,1,0:T(8,128)S(1)} %bitcast.42), channel_id=1, replica_groups=mesh['grid'=8,'dom'=4] {'grid','dom'}, dimensions={0} | all-to-all | bytes 1048576 | tf_op jit(solution)/shard_map/cond/branch_1_fun/all_to_all | solution.py:562
  87.2 1.1 %unpack.3 = f32[16,8192]{1,0:T(8,128)S(1)} custom-call(s32[8,128]{1,0:T(8,128)S(1)} %get-tuple-element.53.info, f32[128,8,128]{2,1,0:T(8,128)S(1)} %bitcast.37, f32[128,8,128]{2,1,0:T(8,128)S(1)} %get-tuple-element.64.own), custom_call_target="tpu_custom_call" | custom-call | tf_op jit(solution)/shard_map/cond/branch_1_fun/unpack/pallas_call | solution.py:605
  88.4 0.0 copy-start.3
  88.4 0.8 copy-done.3
  (17 shorter events, 0.1 us)
Async XLA Ops:
  0.0 3.4 %copy-start.1 = (f32[1,16,8192]{2,1,0:T(8,128)S(1)}, f32[1,16,8192]{2,1,0:T(8,128)}, u32[]{:S(2)}) copy-start(f32[1,16,8192]{2,1,0:T(8,128)} %param.10) | copy-start | bytes 1572868
  0.0 3.5 %copy-start = (f32[1,16,8192]{2,1,0:T(8,128)S(1)}, f32[1,16,8192]{2,1,0:T(8,128)}, u32[]{:S(2)}) copy-start(f32[1,16,8192]{2,1,0:T(8,128)} %param.9) | copy-start | bytes 1572868
  0.0 10.1 %copy-start.4 = (s32[1,3]{1,0:T(1,128)S(1)}, s32[1,3]{1,0:T(1,128)}, u32[]{:S(2)}) copy-start(s32[1,3]{1,0:T(1,128)} %levels.3) | copy-start | bytes 40
  0.0 10.1 %copy-start.2 = (f32[4]{0:T(128)S(1)}, f32[4]{0:T(128)}, u32[]{:S(2)}) copy-start(f32[4]{0:T(128)} %velocity.1) | copy-start | bytes 52
  2.1 18.5 %copy-start.5 = (s32[1,128]{1,0:T(1,128)S(1)}, s32[1,128]{1,0:T(1,128)}, u32[]{:S(2)}) copy-start(s32[1,128]{1,0:T(1,128)} %param.15) | copy-start | bytes 1540
  2.1 18.5 %copy-start.6 = (s32[1,128]{1,0:T(1,128)S(1)}, s32[1,128]{1,0:T(1,128)}, u32[]{:S(2)}) copy-start(s32[1,128]{1,0:T(1,128)} %param.14) | copy-start | bytes 1540
  2.1 8.0 %collective-permute-start.1 = (f32[5,64,128]{2,1,0:T(8,128)S(1)}, f32[5,64,128]{2,1,0:T(8,128)S(1)}, u32[]{:S(2)}, u32[]{:S(2)}) collective-permute-start(f32[5,64,128]{2,1,0:T(8,128)S(1)} %pad_maximum_fusion), channel_id=1, source_target_pairs={{1,0},{2,1},{3,2},{5,4},{6,5},{7,6},{9,8},{10,9},{11,10},{13,12},{... | collective-permute-start | bytes 491528 | tf_op jit(solution)/shard_map/ppermute | solution.py:491
  3.6 6.3 %collective-permute-start = (f32[3,64,128]{2,1,0:T(8,128)S(1)}, f32[3,64,128]{2,1,0:T(8,128)S(1)}, u32[]{:S(2)}, u32[]{:S(2)}) collective-permute-start(f32[3,64,128]{2,1,0:T(8,128)S(1)} %pad_maximum_fusion.1), channel_id=1, source_target_pairs={{0,1},{1,2},{2,3},{4,5},{5,6},{6,7},{8,9},{9,10},{10,11},{12,13},{... | collective-permute-start | bytes 294920 | tf_op jit(solution)/shard_map/ppermute | solution.py:490
  14.3 27.3 %collective-permute-start.3 = (f32[64,128]{1,0:T(8,128)S(1)}, f32[64,128]{1,0:T(8,128)S(1)}, u32[]{:S(2)}, u32[]{:S(2)}) collective-permute-start(f32[64,128]{1,0:T(8,128)S(1)} %get-tuple-element.72), channel_id=1, source_target_pairs={{0,2},{4,6},{8,10},{12,14},{16,18},{20,22},{24,26},{28,30}} | collective-permute-start | bytes 98312 | tf_op jit(solution)/shard_map/ppermute | solution.py:554
  19.3 22.4 %collective-permute-start.2 = (f32[64,128]{1,0:T(8,128)S(1)}, f32[64,128]{1,0:T(8,128)S(1)}, u32[]{:S(2)}, u32[]{:S(2)}) collective-permute-start(f32[64,128]{1,0:T(8,128)S(1)} %get-tuple-element.72), channel_id=1, source_target_pairs={{0,1},{2,3},{4,5},{6,7},{8,9},{10,11},{12,13},{14,15},{16,17},{18,... | collective-permute-start | bytes 98312 | tf_op jit(solution)/shard_map/ppermute | solution.py:554
  21.3 12.6 %all-to-all-start.4 = ((s32[32,1,128]{2,1,0:T(1,128)}), s32[32,1,128]{2,1,0:T(1,128)S(1)}, u32[]{:S(2)}, u32[]{:S(2)}) async-start(s32[32,1,128]{2,1,0:T(1,128)} %broadcast_in_dim.16), calls=%async_computation.4 | async-start | bytes 32768 | tf_op jit(solution)/shard_map/all_to_all | solution.py:478
  47.6 18.4 %all-to-all-start.2 = ((f32[32,32,128]{2,1,0:T(8,128)}), f32[32,32,128]{2,1,0:T(8,128)S(1)}, u32[]{:S(2)}, u32[]{:S(2)}) async-start(f32[32,32,128]{2,1,0:T(8,128)} %bitcast.5), calls=%async_computation.2 | async-start | bytes 1048576 | tf_op jit(solution)/shard_map/cond/branch_1_fun/all_to_all | solution.py:562
  88.4 0.8 copy-start.3

commit v4 on v3

--- a/solution.py
+++ b/solution.py
@@ -20,6 +20,7 @@
     return pltpu.CompilerParams(vmem_limit_bytes=VMEM_LIMIT)
 
 
+SMALL = pl.CostEstimate(flops=0, transcendentals=0, bytes_accessed=0)
 VM = pl.BlockSpec(memory_space=pltpu.VMEM)
 SM = pl.BlockSpec(memory_space=pltpu.SMEM)
 
@@ -89,7 +90,83 @@
     )
 
 
-def steps_kernel(levels, velocity, conc, dif_in, low, high, out, lead, u_a, u_b, dif):
+def bit_ends(levels, q):
+    one = levels[0, 0]
+    two = one + levels[0, 1]
+    begin = jnp.where(q < one, 0, jnp.where(q < two, one, two))
+    end = jnp.where(q < one, one, jnp.where(q < two, two, LR))
+    return begin, end
+
+
+def lane_matrix(levels):
+    rows = lax.broadcasted_iota(jnp.int32, (LANES, LANES), 0)
+    lane = lax.broadcasted_iota(jnp.int32, (LANES, LANES), 1)
+    own = (rows == lane).astype(jnp.float32)
+    nxt = jnp.zeros((LANES, LANES), jnp.float32)
+    for q in range(7):
+        begin, end = bit_ends(levels, q)
+        below = (1 << q) - (1 << begin)
+        above = (1 << jnp.minimum(end, 7)) - (2 << q)
+        here = ((lane & below) == 0) & ((lane & (1 << q)) != 0)
+        full = (lane & above) == above
+        ahead = pltpu.roll(own, LANES - (1 << q), 1)
+        before = pltpu.roll(own, 1 << q, 1)
+        half = jnp.where(here, -0.5, 0.0)
+        nxt = nxt + jnp.where(full & (end > 7), half * ahead, 0.0)
+        own = own + half * (before + jnp.where(full, 0.0, ahead))
+    return jnp.concatenate([own, nxt], axis=0)
+
+
+def surplus_rows(levels, sign, x, y, matrix, stage):
+    rows = x.shape[1]
+    x[TILES] = jnp.zeros((rows, LANES), jnp.float32)
+    y[pl.ds(0, 32)] = jnp.zeros((32, rows, LANES), jnp.float32)
+    y[pl.ds(32 + TILES, 32)] = jnp.zeros((32, rows, LANES), jnp.float32)
+
+    _, end_six = bit_ends(levels, 6)
+    mask_six = (1 << (jnp.maximum(end_six, 7) - 7)) - 1
+    chunk = 16
+    for j0 in range(0, TILES, chunk):
+        own = x[pl.ds(j0, chunk)].reshape(chunk * rows, LANES)
+        nxt = jnp.concatenate(
+            [
+                jnp.where(((j0 + i) & mask_six) == mask_six, 0.0, x[j0 + i + 1])
+                for i in range(chunk)
+            ],
+            axis=0,
+        )
+        res = jnp.dot(
+            jnp.concatenate([own, nxt], axis=1),
+            matrix,
+            precision=lax.Precision.HIGHEST,
+            preferred_element_type=jnp.float32,
+        )
+        y[pl.ds(32 + j0, chunk)] = res.reshape(chunk, rows, LANES)
+
+    lane = lax.broadcasted_iota(jnp.int32, (1, LANES), 1)
+    for q in range(7, LR):
+        t = 1 << (q - 7)
+        begin, end = bit_ends(levels, q)
+        low_lane = 128 - (1 << jnp.minimum(begin, 7))
+        half = jnp.where((lane & low_lane) == 0, -0.5, 0.0)
+        below = t - (1 << (jnp.maximum(begin, 7) - 7))
+        above = (1 << (end - 7)) - 2 * t
+        for j in range(TILES):
+            if j & t:
+                mine = jnp.where((j & below) == 0, half, 0.0)
+                ahead_on = jnp.where((j & above) == above, 0.0, 1.0)
+                y[32 + j] = y[32 + j] + mine * (y[32 + j - t] + ahead_on * y[32 + j + t])
+
+    factor = sign[0].astype(jnp.float32)
+    for j in range(TILES):
+        tile = factor * y[32 + j]
+        for i in range(0, rows, 8):
+            stage[pl.ds(j + i * TILES, 8, stride=TILES), :] = tile[i : i + 8]
+
+
+def rows_kernel(
+    levels, velocity, sign, conc, dif_in, low, high, out, lead, u_a, u_b, dif, x, y
+):
     place = lax.axis_index("dom")
     count = lax.axis_size("dom")
     zeros = jnp.zeros((PAD, 24, LANES), jnp.float32)
@@ -129,110 +206,62 @@
     pl.when(small_three)(both(True, True))
     pl.when(small_two & jnp.logical_not(small_three))(both(True, False))
     pl.when(jnp.logical_not(small_two))(both(False, False))
-    out[...] = u_a[PAD : PAD + TILES]
     lead[...] = u_a[PAD : PAD + TILES, 0]
-
-
-def bit_ends(levels, q):
-    one = levels[0, 0]
-    two = one + levels[0, 1]
-    begin = jnp.where(q < one, 0, jnp.where(q < two, one, two))
-    end = jnp.where(q < one, one, jnp.where(q < two, two, LR))
-    return begin, end
-
-
-def lane_kernel(levels, out):
-    rows = lax.broadcasted_iota(jnp.int32, (LANES, LANES), 0)
-    lane = lax.broadcasted_iota(jnp.int32, (LANES, LANES), 1)
-    own = (rows == lane).astype(jnp.float32)
-    nxt = jnp.zeros((LANES, LANES), jnp.float32)
-    for q in range(7):
-        begin, end = bit_ends(levels, q)
-        below = (1 << q) - (1 << begin)
-        above = (1 << jnp.minimum(end, 7)) - (2 << q)
-        here = ((lane & below) == 0) & ((lane & (1 << q)) != 0)
-        full = (lane & above) == above
-        ahead = pltpu.roll(own, LANES - (1 << q), 1)
-        before = pltpu.roll(own, 1 << q, 1)
-        half = jnp.where(here, -0.5, 0.0)
-        nxt = nxt + jnp.where(full & (end > 7), half * ahead, 0.0)
-        own = own + half * (before + jnp.where(full, 0.0, ahead))
-    out[0:LANES] = own
-    out[LANES : 2 * LANES] = nxt
-
-
-def pack_kernel(levels, sign, info, v_in, coarse, lanes, out, blocks, x, y, stage):
-    place = lax.axis_index("dom")
-    row = lax.broadcasted_iota(jnp.int32, (24, LANES), 0)
     for j in range(TILES):
-        tile = v_in[j]
+        tile = u_a[PAD + j]
         for p in range(4):
             s = 1 << p
-            both = pltpu.roll(tile, 24 - s, 0) + pltpu.roll(tile, s, 0)
+            around = pltpu.roll(tile, 24 - s, 0) + pltpu.roll(tile, s, 0)
             hit = ((row & (2 * s - 1)) == s) & (row < 16)
-            tile = tile - 0.5 * jnp.where(hit, both, 0.0)
+            tile = tile - 0.5 * jnp.where(hit, around, 0.0)
         x[j] = tile[0:16]
-    own_upper = jnp.where((place & 1) == 1, 0.5, 0.0)
-    fix = 0.5 * coarse[...] + own_upper * v_in[:, 16]
-    x[0:TILES, 0] = x[0:TILES, 0] - fix
-    x[TILES] = jnp.zeros((16, LANES), jnp.float32)
-    y[pl.ds(0, 32)] = jnp.zeros((32, 16, LANES), jnp.float32)
-    y[pl.ds(32 + TILES, 32)] = jnp.zeros((32, 16, LANES), jnp.float32)
-
-    _, end_six = bit_ends(levels, 6)
-    mask_six = (1 << (jnp.maximum(end_six, 7) - 7)) - 1
-    chunk = 8
-    own_mat = lanes[0:LANES]
-    next_mat = lanes[LANES : 2 * LANES]
-
-    def lane_pass(k, carry):
-        j0 = k * chunk
-        own = x[pl.ds(j0, chunk)].reshape(chunk * 16, LANES)
-        nxt = jnp.concatenate(
-            [
-                jnp.where(((j0 + i) & mask_six) == mask_six, 0.0, x[j0 + i + 1])
-                for i in range(chunk)
-            ],
-            axis=0,
-        )
-        res = jnp.dot(
-            own, own_mat, precision=lax.Precision.HIGHEST, preferred_element_type=jnp.float32
-        ) + jnp.dot(
-            nxt, next_mat, precision=lax.Precision.HIGHEST, preferred_element_type=jnp.float32
-        )
-        y[pl.ds(32 + j0, chunk)] = res.reshape(chunk, 16, LANES)
-        return carry
-
-    lax.fori_loop(0, TILES // chunk, lane_pass, 0)
-
-    lane = lax.broadcasted_iota(jnp.int32, (1, LANES), 1)
-    for q in range(7, LR):
-        t = 1 << (q - 7)
-        begin, end = bit_ends(levels, q)
-        low_lane = 128 - (1 << jnp.minimum(begin, 7))
-        half = jnp.where((lane & low_lane) == 0, -0.5, 0.0)
-        below = t - (1 << (jnp.maximum(begin, 7) - 7))
-        above = (1 << (end - 7)) - 2 * t
-
-        def tile_pass(j):
-            hit = (j & below) == 0
-            mine = jnp.where(hit, half, 0.0)
-            ahead_on = jnp.where((j & above) == above, 0.0, 1.0)
-            y[32 + j] = y[32 + j] + mine * (y[32 + j - t] + ahead_on * y[32 + j + t])
-
-        for j in range(TILES):
-            if j & t:
-                tile_pass(j)
-
-    factor = sign[0].astype(jnp.float32)
-    for j in range(TILES):
-        tile = factor * y[32 + j]
-        for i in range(2):
-            stage[pl.ds(j + i * 8 * TILES, 8, stride=TILES), :] = tile[8 * i : 8 * i + 8]
-    for b in range(16 * TILES // 8):
-        block = stage[pl.ds(8 * b, 8), :]
-        blocks[b] = block
-        out[info[0, b]] = block
+    next_lead = u_a[PAD : PAD + TILES, 16]
+    x[0:TILES, 0] = x[0:TILES, 0] - jnp.where((place & 1) == 1, 0.5, 0.0) * next_lead
+    surplus_rows(levels, sign, x, y, lane_matrix(levels), out)
+
+
+def fix_kernel(levels, sign, coarse, blocks, out, x, y, stage):
+    x[...] = jnp.zeros_like(x)
+    x[0:TILES, 0] = coarse[...]
+    surplus_rows(levels, sign, x, y, lane_matrix(levels), stage)
+    out[...] = blocks[...]
+    out[0:TILES, :] = blocks[0:TILES, :] - 0.5 * stage[0:TILES, :]
+
+
+def scatter_kernel(info, blocks, out, *, extras):
+    for b in range(blocks.shape[0]):
+        out[info[0, b]] = blocks[b]
+    for i in range(extras):
+        out[info[4, i]] = -0.5 * blocks[i % 8]
+
+
+def row_zero_uses(dom_count):
+    uses = []
+    distance = 1
+    while distance < dom_count:
+        uses.append((distance, 2 * distance))
+        if distance > 1 and dom_count > 2 * distance:
+            uses.append((-distance, 2 * distance))
+        distance *= 2
+    return uses
+
+
+def has_use(place, offset, period, dom_count):
+    return (place % period == 0) & (place + offset >= 0) & (place + offset < dom_count)
+
+
+def extra_entries(values, dom_count, fill):
+    devices, size = values.shape
+    place = lax.broadcasted_iota(jnp.int32, (devices, size), 0) % dom_count
+    lane = lax.broadcasted_iota(jnp.int32, (devices, size), 1)
+    res = jnp.full((devices, size), fill, values.dtype)
+    for t, (offset, period) in enumerate(row_zero_uses(dom_count)):
+        cut = offset % devices
+        moved = jnp.concatenate([values[cut:], values[:cut]], axis=0)
+        moved = pltpu.roll(moved, 8 * t, 1) if t else moved
+        hit = (lane >= 8 * t) & (lane < 8 * t + 8) & has_use(place, offset, period, dom_count)
+        res = jnp.where(hit, moved, res)
+    return res
 
 
 def key_parts(keys, rows):
@@ -280,37 +309,52 @@
     return lax.axis_index("grid") * lax.axis_size("dom") + lax.axis_index("dom")
 
 
-def write_places(info, handler, ok, me, devices, capacity):
-    taken = hot(handler.astype(jnp.int32), devices)
+def write_places(info, handler, extra, ok, me, devices, capacity):
     size = handler.shape[1]
     first = lax.broadcasted_iota(jnp.int32, (size, size), 0)
     second = lax.broadcasted_iota(jnp.int32, (size, size), 1)
-    before = dot_plain(taken, jnp.where(first < second, 1.0, 0.0))
-    rank = jnp.sum(taken * before, axis=0, keepdims=True)
-    place = handler.astype(jnp.int32) * capacity + rank.astype(jnp.int32)
-    stays = handler == me.astype(jnp.float32)
-    send = jnp.where(stays, devices * capacity, place)
-    get = jnp.where(stays, 0, place)
+    earlier = jnp.where(first < second, 1.0, 0.0)
+
+    def placed(which, ahead):
+        taken = hot(which.astype(jnp.int32), devices)
+        rank = jnp.sum(taken * (dot_plain(taken, earlier) + ahead), axis=0, keepdims=True)
+        place = which.astype(jnp.int32) * capacity + rank.astype(jnp.int32)
+        stays = (which == me.astype(jnp.float32)) | (which < 0.0)
+        return jnp.where(stays, me * capacity, place), stays, taken
+
+    send, stays, taken = placed(handler, 0.0)
+    send_extra, _, _ = placed(extra, jnp.sum(taken, axis=1, keepdims=True))
     kept = jnp.where(stays, 1, 0)
     flag = jnp.broadcast_to(ok, kept.shape).astype(jnp.int32)
-    rows = [send, get, kept, flag, flag, flag, flag, flag]
-    info[...] = jnp.concatenate(rows, axis=0)
+    info[...] = jnp.concatenate([send, send, kept, flag, send_extra, flag, flag, flag], axis=0)
 
 
 def owner_places_kernel(keys, info, *, devices, capacity):
     me = device_number()
     owner = (keys[pl.ds(me, 1), :] // SLOTS).astype(jnp.float32)
-    write_places(info, owner, jnp.int32(0), me, devices, capacity)
+    none = jnp.full(owner.shape, -1.0, jnp.float32)
+    write_places(info, owner, none, jnp.int32(0), me, devices, capacity)
 
 
 def balance_kernel(keys, assigned, info, one, two, table, *, devices, capacity, full):
     rows = devices * SLOTS // LANES
     keys_all = keys[...]
     _, _, lane_all, row_one, row_two = key_parts(keys_all, rows)
+    dom_count = lax.axis_size("dom")
+    lane_more, one_more, two_more = [
+        extra_entries(v, dom_count, -1) for v in (lane_all, row_one, row_two)
+    ]
+
+    def counted(one_row, two_row, lane_row):
+        both = jnp.concatenate([hot(one_row, rows), hot(two_row, rows)], axis=0)
+        return dot_rows(both, hot(lane_row, LANES))
+
     for d in range(devices):
         pick = slice(d, d + 1)
-        both = jnp.concatenate([hot(row_one[pick], rows), hot(row_two[pick], rows)], axis=0)
-        counts = dot_rows(both, hot(lane_all[pick], LANES))
+        counts = counted(row_one[pick], row_two[pick], lane_all[pick])
+        place = d % dom_count
+        if any(has_use(place, *use, dom_count) for use in row_zero_uses(dom_count)):
+            counts = counts + counted(one_more[pick], two_more[pick], lane_more[pick])
         one[pl.ds(d, rows, stride=devices), :] = counts[:rows]
         two[pl.ds(d, rows, stride=devices), :] = counts[rows:]
 
@@ -368,13 +412,24 @@
     final = jnp.where(ok, table[...], owner)
     assigned[...] = final
     me = device_number()
-    _, _, my_lane, _, my_row = key_parts(keys[pl.ds(me, 1), :], rows)
-    handler = handlers_of(final, my_lane, my_row)
+
+    def found(device):
+        _, _, lane_row, _, row = key_parts(keys[pl.ds(device, 1), :], rows)
+        return handlers_of(final, lane_row, row)
+
+    place = lax.axis_index("dom")
+    column = lax.broadcasted_iota(jnp.int32, (1, keys.shape[1]), 1)
+    extra = jnp.full((1, keys.shape[1]), -1.0, jnp.float32)
+    for t, (offset, period) in enumerate(row_zero_uses(dom_count)):
+        there = has_use(place, offset, period, dom_count)
+        moved = found(jnp.where(there, me + offset, me))
+        moved = pltpu.roll(moved, 8 * t, 1) if t else moved
+        extra = jnp.where((column >= 8 * t) & (column < 8 * t + 8) & there, moved, extra)
     size = jnp.where(ok, capacity, full)
-    write_places(info, handler, ok.astype(jnp.int32), me, devices, size)
-
-
-def table_kernel(*refs, devices, capacity, pieces, balanced):
+    write_places(info, found(me), extra, ok.astype(jnp.int32), me, devices, size)
+
+
+def table_kernel(*refs, devices, capacity, pieces, balanced, more):
     if balanced:
         keys, assigned, out, handlers = refs
         rows = devices * SLOTS // LANES
@@ -393,22 +448,40 @@
     sender = lax.broadcasted_iota(jnp.int32, (devices, size), 0)
     first = lax.broadcasted_iota(jnp.int32, (size, size), 0)
     second = lax.broadcasted_iota(jnp.int32, (size, size), 1)
-    rank = dot_plain(jnp.where(mine, 1.0, 0.0), jnp.where(first <= second, 1.0, 0.0))
-    comes = mine & (sender != me)
+    earlier = jnp.where(first <= second, 1.0, 0.0)
     column = lax.broadcasted_iota(jnp.int32, (devices, size), 1)
+
+    def ranked(hits, ahead):
+        count = jnp.where(hits, 1.0, 0.0)
+        return dot_plain(count, earlier) + ahead, jnp.sum(count, axis=1, keepdims=True)
+
+    rank, total = ranked(mine, 0.0)
+    groups = [(mine, rank, piece)]
+    if more:
+        dom_count = lax.axis_size("dom")
+        mine_more = extra_entries(handlers[...], dom_count, -1.0) == me.astype(jnp.float32)
+        rank_more, _ = ranked(mine_more, total)
+        groups.append((mine_more, rank_more, extra_entries(piece, dom_count, 0)))
     found = jnp.full((devices, size), pieces, jnp.int32)
     for r in range(capacity):
-        hit = comes & (rank == r + 1.0)
-        at = jnp.sum(jnp.where(hit, piece - pieces, 0), axis=1, keepdims=True)
+        at = jnp.zeros((devices, 1), jnp.int32)
+        for hits, ranks, piece_of in groups:
+            hit = hits & (sender != me) & (ranks == r + 1.0)
+            at = at + jnp.sum(jnp.where(hit, piece_of - pieces, 0), axis=1, keepdims=True)
         found = jnp.where(column == r, pieces + at, found)
     out[0:devices, :] = found
-    kept = jnp.sum(
-        jnp.where(mine & (sender == me), piece - pieces, 0), axis=0, keepdims=True
-    )
-    out[devices : devices + 8, :] = jnp.broadcast_to(kept + pieces, (8, size))
-
-
-def sum_kernel(table, arrived, own, out, own_out, pieces, *, devices, capacity):
+    rows_kept = [
+        jnp.sum(
+            jnp.where(hits & (sender == me), piece_of - pieces, 0), axis=0, keepdims=True
+        )
+        + pieces
+        for hits, _, piece_of in groups
+    ]
+    rows_kept += [jnp.full((1, size), pieces, jnp.int32)] * (8 - len(rows_kept))
+    out[devices : devices + 8, :] = jnp.concatenate(rows_kept, axis=0)
+
+
+def sum_kernel(table, arrived, own, out, own_out, pieces, *, devices, capacity, extras):
     blocks = own.shape[0]
     zero = jnp.zeros((8, LANES), jnp.float32)
 
@@ -445,8 +518,13 @@
 
     over_senders(clear)
     over_kept(clear)
+    for i in range(extras):
+        clear(table[devices + 1, i], i)
     over_senders(add)
     over_kept(add_own)
+    for i in range(extras):
+        piece = table[devices + 1, i]
+        pieces[piece] = pieces[piece] - 0.5 * own[i % 8]
     over_senders(give)
     over_kept(give_own)
 
@@ -476,7 +554,7 @@
 
     own_keys = owner_list * SLOTS + slot_list
     keys = lax.all_to_all(
-        jnp.broadcast_to(own_keys[:, None], (devices, 1, blocks)),
+        jnp.broadcast_to(own_keys[:, None], (devices, 4, blocks)),
         ("grid", "dom"),
         split_axis=0,
         concat_axis=0,
@@ -490,29 +568,24 @@
     low = lax.ppermute(low_rows.reshape(3, TILES, LANES), "dom", up)
     high = lax.ppermute(high_rows.reshape(5, TILES, LANES), "dom", down)
 
-    lanes = pl.pallas_call(
-        lane_kernel,
-        out_shape=f32(2 * LANES, LANES),
-        in_specs=[SM],
-        out_specs=VM,
-        compiler_params=params(),
-        name="lane_matrix",
-    )(levels)
-
-    stepped, lead = pl.pallas_call(
-        steps_kernel,
-        out_shape=(f32(TILES, 24, LANES), f32(TILES, LANES)),
-        in_specs=[SM, SM, VM, VM, VM, VM],
+    blocks_in, lead = pl.pallas_call(
+        rows_kernel,
+        out_shape=(f32(rows * TILES, LANES), f32(TILES, LANES)),
+        in_specs=[SM, SM, SM, VM, VM, VM, VM],
         out_specs=(VM, VM),
         scratch_shapes=[
             pltpu.VMEM((TILES + 2 * PAD, 24, LANES), jnp.float32),
             pltpu.VMEM((TILES + 2 * PAD, 24, LANES), jnp.float32),
             pltpu.VMEM((TILES, 24, LANES), jnp.float32),
+            pltpu.VMEM((TILES + 1, 16, LANES), jnp.float32),
+            pltpu.VMEM((TILES + 64, 16, LANES), jnp.float32),
         ],
         compiler_params=params(),
-        name="steps",
-    )(levels, velocity, conc, dif, low, high)
-
+        name="rows",
+        cost_estimate=SMALL,
+    )(levels, velocity, grid_signs, conc, dif, low, high)
+
+    keys, blocks_in = lax.optimization_barrier((keys, blocks_in))
     balanced = capacity >= 8 and devices * SLOTS % LANES == 0 and devices <= 64
     info_shape = jax.ShapeDtypeStruct((8, blocks), jnp.int32)
     if balanced:
@@ -531,6 +604,7 @@
             ],
             compiler_params=params(),
             name="balance",
+            cost_estimate=SMALL,
         )(keys)
     else:
         info = pl.pallas_call(
@@ -540,22 +614,32 @@
             out_specs=VM,
             compiler_params=params(),
             name="places",
+            cost_estimate=SMALL,
         )(keys)
 
-    coarse = None
-    distance = 1
-    while distance < dom_count:
-        targets = range(distance, dom_count, 2 * distance)
-        pairs = [[(d - distance, d) for d in targets]]
-        if distance > 1:
-            pairs.append([(d + distance, d) for d in targets if d + distance < dom_count])
-        for pair in pairs:
-            if pair:
-                part = lax.ppermute(lead, "dom", pair)
-                coarse = part if coarse is None else coarse + part
-        distance *= 2
-
-    def route(slots, balanced, tables):
+    def fixed():
+        coarse = None
+        for offset, period in row_zero_uses(dom_count):
+            pairs = [
+                (d, d + offset) for d in range(dom_count) if has_use(d, offset, period, dom_count)
+            ]
+            part = lax.ppermute(lead, "dom", pairs)
+            coarse = part if coarse is None else coarse + part
+        return pl.pallas_call(
+            fix_kernel,
+            out_shape=f32(rows * TILES, LANES),
+            in_specs=[SM, SM, VM, VM],
+            out_specs=VM,
+            scratch_shapes=[
+                pltpu.VMEM((TILES + 1, 8, LANES), jnp.float32),
+                pltpu.VMEM((TILES + 64, 8, LANES), jnp.float32),
+                pltpu.VMEM((8 * TILES, LANES), jnp.float32),
+            ],
+            compiler_params=params(),
+            name="fix_row",
+        )(levels, grid_signs, coarse, blocks_in)
+
+    def route(own, slots, balanced, extras, tables):
         pieces = devices * SLOTS if balanced else SLOTS
 
         def exchange(x):
@@ -567,23 +651,24 @@
                 tiled=True,
             ).reshape(devices * slots, 8, LANES)
 
-        outgoing, own = pl.pallas_call(
-            pack_kernel,
-            out_shape=(f32(devices * slots + 1, 8, LANES), f32(blocks, 8, LANES)),
-            in_specs=[SM, SM, SM, VM, VM, VM],
-            out_specs=(VM, VM),
-            scratch_shapes=[
-                pltpu.VMEM((TILES + 1, 16, LANES), jnp.float32),
-                pltpu.VMEM((TILES + 64, 16, LANES), jnp.float32),
-                pltpu.VMEM((16 * TILES, LANES), jnp.float32),
-            ],
+        own = own.reshape(blocks, 8, LANES)
+        outgoing = pl.pallas_call(
+            functools.partial(scatter_kernel, extras=extras),
+            out_shape=f32(devices * slots, 8, LANES),
+            in_specs=[SM, VM],
+            out_specs=VM,
             compiler_params=params(),
-            name="pack",
-        )(levels, grid_signs, info, stepped, coarse, lanes)
-        arrived = exchange(outgoing[: devices * slots])
+            name="scatter",
+        )(info, own)
+        arrived = exchange(outgoing)
         table = pl.pallas_call(
             functools.partial(
-                table_kernel, devices=devices, capacity=slots, pieces=pieces, balanced=balanced
+                table_kernel,
+                devices=devices,
+                capacity=slots,
+                pieces=pieces,
+                balanced=balanced,
+                more=extras > 0,
             ),
             out_shape=jax.ShapeDtypeStruct((devices + 8, blocks), jnp.int32),
             in_specs=[VM] * len(tables),
@@ -593,7 +678,7 @@
             name="piece_table",
         )(*tables)
         returned, own_back = pl.pallas_call(
-            functools.partial(sum_kernel, devices=devices, capacity=slots),
+            functools.partial(sum_kernel, devices=devices, capacity=slots, extras=extras),
             out_shape=(f32(devices * slots, 8, LANES), f32(blocks, 8, LANES)),
             in_specs=[SM, VM, VM],
             out_specs=(VM, VM),
@@ -615,11 +700,13 @@
     if balanced:
         combined = lax.cond(
             info[3, 0] != 0,
-            lambda: route(capacity // 2, True, (keys, assigned)),
-            lambda: route(capacity, True, (keys, assigned)),
+            lambda: route(
+                blocks_in, capacity // 2, True, 8 * len(row_zero_uses(dom_count)), (keys, assigned)
+            ),
+            lambda: route(fixed(), capacity, True, 0, (keys, assigned)),
         )
     else:
-        combined = route(capacity, False, (keys,))
+        combined = route(fixed(), capacity, False, 0, (keys,))
     return combined[None]
 
 

time: 89.5 us -> 82.9 us (0.926)
  waiting for transfers between devices: 22.1 us -> 15.9 us
  starting transfers between devices: 21.1 us -> 19.8 us
    ppermute x2 -> x0, starting transfers between devices: 6.26 us -> none  [body(): part = lax.ppermute(lead, 'dom', pair)]
    all_to_all x1, waiting for transfers between devices: 5.46 us -> 0.01 us  [body(): lax.all_to_all(jnp.broadcast_to(own_keys[:, None], (devices, 4, blocks)),...]
    all_to_all x1, starting transfers between devices: 2.95 us -> 7.46 us  [exchange(): lax.all_to_all(x.reshape(devices, slots * 8, LANES), ('grid', 'dom'), spl...]
    all_to_all x1, starting transfers between devices: 5.94 us -> 7.1 us  [body(): lax.all_to_all(jnp.broadcast_to(own_keys[:, None], (devices, 4, blocks)),...]
    pallas_call x3 -> x2, Pallas kernels: 10.4 us -> 9.27 us  [the longest x1 7.77 us: body(): pl.pallas_call(rows_kernel, out_shape=(f32(rows * TILES, LANES), f32(TILE...]
    unnamed x20 -> x16, local copies, waits for them, and re-layouts: 2.89 us -> 3.58 us
  transfers between devices with their start and end apart: 6 -> 4, of which waited for: 4 -> 3; matrix products, arithmetic and copies ran while one was open for 1% -> 3% of each run, Pallas kernels for 9% -> 1%
where the time goes in v4:
time: 82.9 us; the launch traced here: 82.4 us
  Pallas kernels  21.4 us (26%)
  starting transfers between devices  19.8 us (24%)
  blocking collectives  18.3 us (22%)
  waiting for transfers between devices  15.9 us (19%)
  local copies, waits for them, and re-layouts  4.78 us (6%)
  between operations  1.46 us (2%)
    all_to_all x1, blocking collectives, exchange(): lax.all_to_all(x.reshape(devices, slots * 8, LANES), ('grid', 'dom'), spl...  18.3 us
    all_to_all x1, waiting for transfers between devices, exchange(): lax.all_to_all(x.reshape(devices, slots * 8, LANES), ('grid', 'dom'), spl...  14.6 us
    pallas_call x1, Pallas kernels, body(): pl.pallas_call(rows_kernel, out_shape=(f32(rows * TILES, LANES), f32(TILE...  7.77 us
    all_to_all x1, starting transfers between devices, exchange(): lax.all_to_all(x.reshape(devices, slots * 8, LANES), ('grid', 'dom'), spl...  7.46 us
    pallas_call x1, Pallas kernels, body(): pl.pallas_call(functools.partial(balance_kernel, devices=devices, capacit...  7.1 us
    all_to_all x1, starting transfers between devices, body(): lax.all_to_all(jnp.broadcast_to(own_keys[:, None], (devices, 4, blocks)),...  7.1 us
    ppermute x1, starting transfers between devices, body(): low = lax.ppermute(low_rows.reshape(3, TILES, LANES), 'dom', up)  3.99 us
    unnamed x16, local copies, waits for them, and re-layouts  3.58 us
  transfers between devices with their start and end apart: 4, of which 3 were waited for; matrix products, arithmetic and copies ran while one was open for 3% of the time, Pallas kernels for 1%

profile of v4, /device:TPU:1, one launch (start us, length us, event | category | flops | bytes accessed | tf_op | source)
XLA Modules:
  0.0 82.4 jit_solution(1703622481449766890)
XLA Ops:
  0.0 0.7 add_bitcast_fusion
  0.7 0.6 broadcast_in_dim.16
  1.3 7.1 %all-to-all-start.4 = ((s32[32,4,128]{2,1,0:T(4,128)}), s32[32,4,128]{2,1,0:T(4,128)S(1)}, u32[]{:S(2)}, u32[]{:S(2)}) async-start(s32[32,4,128]{2,1,0:T(4,128)} %broadcast_in_dim.16), calls=%async_computation.4 | async-start | bytes 131072 | tf_op jit(solution)/shard_map/all_to_all | solution.py:556
  8.4 0.0 copy-start.1
  8.4 1.0 %slice_bitcast_fusion.1 = f32[1,2,64,128]{3,1,2,0:T(2,128)S(1)} fusion(f32[1,16,8192]{2,1,0:T(8,128)} %param.10), kind=kLoop, calls=%fused_computation.6 | loop fusion | bytes 131072
  9.5 0.0 copy-start
  9.5 1.0 %slice_bitcast_fusion = f32[1,3,64,128]{3,1,2,0:T(4,128)S(1)} fusion(f32[1,16,8192]{2,1,0:T(8,128)} %param.9), kind=kLoop, calls=%fused_computation.1 | loop fusion | bytes 196608
  10.6 1.3 %collective-permute-start.3 = (f32[5,64,128]{2,1,0:T(8,128)S(1)}, f32[5,64,128]{2,1,0:T(8,128)S(1)}, u32[]{:S(2)}, u32[]{:S(2)}) collective-permute-start(f32[5,64,128]{2,1,0:T(8,128)S(1)} %pad_maximum_fusion), channel_id=1, source_target_pairs={{1,0},{2,1},{3,2},{5,4},{6,5},{7,6},{9,8},{10,9},{11,10},{13,12},{... | collective-permute-start | bytes 491528 | tf_op jit(solution)/shard_map/ppermute | solution.py:569
  11.9 0.0 copy-done.1
  11.9 0.0 copy-done
  12.0 4.0 %collective-permute-start.2 = (f32[3,64,128]{2,1,0:T(8,128)S(1)}, f32[3,64,128]{2,1,0:T(8,128)S(1)}, u32[]{:S(2)}, u32[]{:S(2)}) collective-permute-start(f32[3,64,128]{2,1,0:T(8,128)S(1)} %pad_maximum_fusion.1), channel_id=1, source_target_pairs={{0,1},{1,2},{2,3},{4,5},{5,6},{6,7},{8,9},{9,10},{10,11},{12,13},{... | collective-permute-start | bytes 294920 | tf_op jit(solution)/shard_map/ppermute | solution.py:568
  16.6 0.0 all-to-all-done.4
  16.7 0.9 %collective-permute-done.2.low = f32[3,64,128]{2,1,0:T(8,128)S(1)} collective-permute-done((f32[3,64,128]{2,1,0:T(8,128)S(1)}, f32[3,64,128]{2,1,0:T(8,128)S(1)}, u32[]{:S(2)}, u32[]{:S(2)}) %collective-permute-start.2) | collective-permute-done | bytes 98336 | tf_op jit(solution)/shard_map/ppermute | solution.py:568
  17.6 0.4 collective-permute-done.3.high
  18.0 0.0 copy-start.2
  18.0 0.0 copy-start.4
  18.0 0.7 copy-done.2
  18.6 0.0 copy-done.4
  18.7 7.8 %rows.1 = (f32[1024,128]{1,0:T(8,128)S(1)}, f32[64,128]{1,0:T(8,128)S(1)}) custom-call(s32[1,3]{1,0:T(1,128)S(1)} %copy-done.4, f32[4]{0:T(128)S(1)} %copy-done.2, s32[1]{0:T(128)S(6)} %copy.23.sign, f32[16,8192]{1,0:T(8,128)S(1)} %bitcast.46, f32[16,8192]{1,0:T(8,128)S(1)} %bitcast.47, f32[3,64,128]{2,1,0:T(8,128)S(1)} %collective-permute-done.2.low, ...), custom_call_target="tpu_custom_call" | custom-call | tf_op jit(solution)/shard_map/rows/pallas_call | solution.py:571
  26.4 7.1 %balance.1 = (f32[16,128]{1,0:T(8,128)S(1)}, s32[8,128]{1,0:T(8,128)S(1)}) custom-call(s32[32,128]{1,0:T(8,128)S(1)} %bitcast.56), custom_call_target="tpu_custom_call" | custom-call | tf_op jit(solution)/shard_map/balance/pallas_call | solution.py:593
  33.5 0.5 slice.27
  34.7 46.9 %conditional.1 = (f32[1,16,8192]{2,1,0:T(8,128)S(1)}) conditional(s32[]{:T(128)} %bitcast.17, (s32[32,128]{1,0:T(8,128)S(1)}, f32[16,128]{1,0:T(8,128)S(1)}, f32[64,128]{1,0:T(8,128)S(1)}, s32[1,3]{1,0:T(1,128)S(1)}, s32[1]{0:T(128)}, /*index=5*/f32[1024,128]{1,0:T(8,128)S(1)}, s32[8,128]{1,0:T(8,128)S(1)}) %tuple.24, (s32[32,128]{1,0:T(8,128)S(1)}, ...), branch_computations={%region_0.0_spmd, %region_1.0_spmd} | conditional | flops 8192 | bytes 5603448 | solution.py:701
  34.7 1.5 %scatter.3 = f32[128,8,128]{2,1,0:T(8,128)} custom-call(s32[8,128]{1,0:T(8,128)S(1)} %get-tuple-element.40.info, f32[128,8,128]{2,1,0:T(8,128)S(1)} %bitcast.49), custom_call_target="tpu_custom_call" | custom-call | tf_op jit(solution)/shard_map/cond/branch_1_fun/scatter/pallas_call | solution.py:655
  36.2 7.5 %all-to-all-start.2 = ((f32[32,32,128]{2,1,0:T(8,128)}), f32[32,32,128]{2,1,0:T(8,128)S(1)}, u32[]{:S(2)}, u32[]{:S(2)}) async-start(f32[32,32,128]{2,1,0:T(8,128)} %bitcast.7), calls=%async_computation.2 | async-start | bytes 1048576 | tf_op jit(solution)/shard_map/cond/branch_1_fun/all_to_all | solution.py:646
  43.7 0.7 piece_table.3.table
  44.4 14.6 %all-to-all-done.2 = f32[32,32,128]{2,1,0:T(8,128)S(1)} async-done(((f32[32,32,128]{2,1,0:T(8,128)}), f32[32,32,128]{2,1,0:T(8,128)S(1)}, u32[]{:S(2)}, u32[]{:S(2)}) %all-to-all-start.2) | async-done | bytes 524320 | tf_op jit(solution)/shard_map/cond/branch_1_fun/all_to_all | solution.py:646
  59.0 3.2 %sum_pieces.3 = (f32[128,8,128]{2,1,0:T(8,128)S(1)}, f32[128,8,128]{2,1,0:T(8,128)S(1)}) custom-call(s32[40,128]{1,0:T(8,128)S(1)} %piece_table.3.table, f32[128,8,128]{2,1,0:T(8,128)S(1)} %bitcast.44, f32[128,8,128]{2,1,0:T(8,128)S(1)} %bitcast.50), custom_call_target="tpu_custom_call" | custom-call | tf_op jit(solution)/shard_map/cond/branch_1_fun/sum_pieces/pallas_call | solution.py:680
  62.2 18.3 %all_to_all.22 = f32[32,32,128]{2,1,0:T(8,128)S(1)} all-to-all(f32[32,32,128]{2,1,0:T(8,128)S(1)} %bitcast.48), channel_id=1, replica_groups=mesh['grid'=8,'dom'=4] {'grid','dom'}, dimensions={0} | all-to-all | bytes 1048576 | tf_op jit(solution)/shard_map/cond/branch_1_fun/all_to_all | solution.py:646
  80.5 1.1 %unpack.3 = f32[16,8192]{1,0:T(8,128)S(1)} custom-call(s32[8,128]{1,0:T(8,128)S(1)} %get-tuple-element.40.info, f32[128,8,128]{2,1,0:T(8,128)S(1)} %bitcast.43, f32[128,8,128]{2,1,0:T(8,128)S(1)} %get-tuple-element.45.own), custom_call_target="tpu_custom_call" | custom-call | tf_op jit(solution)/shard_map/cond/branch_1_fun/unpack/pallas_call | solution.py:690
  81.7 0.0 copy-start.3
  81.7 0.8 copy-done.3
  (8 shorter events, 0.1 us)
Async XLA Ops:
  1.3 15.3 %all-to-all-start.4 = ((s32[32,4,128]{2,1,0:T(4,128)}), s32[32,4,128]{2,1,0:T(4,128)S(1)}, u32[]{:S(2)}, u32[]{:S(2)}) async-start(s32[32,4,128]{2,1,0:T(4,128)} %broadcast_in_dim.16), calls=%async_computation.4 | async-start | bytes 131072 | tf_op jit(solution)/shard_map/all_to_all | solution.py:556
  8.4 3.4 %copy-start.1 = (f32[1,16,8192]{2,1,0:T(8,128)S(1)}, f32[1,16,8192]{2,1,0:T(8,128)}, u32[]{:S(2)}) copy-start(f32[1,16,8192]{2,1,0:T(8,128)} %param.10) | copy-start | bytes 1572868
  9.5 2.4 %copy-start = (f32[1,16,8192]{2,1,0:T(8,128)S(1)}, f32[1,16,8192]{2,1,0:T(8,128)}, u32[]{:S(2)}) copy-start(f32[1,16,8192]{2,1,0:T(8,128)} %param.9) | copy-start | bytes 1572868
  10.6 7.4 %collective-permute-start.3 = (f32[5,64,128]{2,1,0:T(8,128)S(1)}, f32[5,64,128]{2,1,0:T(8,128)S(1)}, u32[]{:S(2)}, u32[]{:S(2)}) collective-permute-start(f32[5,64,128]{2,1,0:T(8,128)S(1)} %pad_maximum_fusion), channel_id=1, source_target_pairs={{1,0},{2,1},{3,2},{5,4},{6,5},{7,6},{9,8},{10,9},{11,10},{13,12},{... | collective-permute-start | bytes 491528 | tf_op jit(solution)/shard_map/ppermute | solution.py:569
  12.0 5.6 %collective-permute-start.2 = (f32[3,64,128]{2,1,0:T(8,128)S(1)}, f32[3,64,128]{2,1,0:T(8,128)S(1)}, u32[]{:S(2)}, u32[]{:S(2)}) collective-permute-start(f32[3,64,128]{2,1,0:T(8,128)S(1)} %pad_maximum_fusion.1), channel_id=1, source_target_pairs={{0,1},{1,2},{2,3},{4,5},{5,6},{6,7},{8,9},{9,10},{10,11},{12,13},{... | collective-permute-start | bytes 294920 | tf_op jit(solution)/shard_map/ppermute | solution.py:568
  18.0 0.7 copy-start.2
  18.0 0.7 copy-start.4
  36.2 22.8 %all-to-all-start.2 = ((f32[32,32,128]{2,1,0:T(8,128)}), f32[32,32,128]{2,1,0:T(8,128)S(1)}, u32[]{:S(2)}, u32[]{:S(2)}) async-start(f32[32,32,128]{2,1,0:T(8,128)} %bitcast.7), calls=%async_computation.2 | async-start | bytes 1048576 | tf_op jit(solution)/shard_map/cond/branch_1_fun/all_to_all | solution.py:646
  81.7 0.8 copy-start.3

commit v5 on v4

--- a/solution.py
+++ b/solution.py
@@ -165,8 +165,29 @@
 
 
 def rows_kernel(
-    levels, velocity, sign, conc, dif_in, low, high, out, lead, u_a, u_b, dif, x, y
+    levels,
+    velocity,
+    sign,
+    info_in,
+    conc,
+    dif_in,
+    low,
+    high,
+    out,
+    lead,
+    outgoing,
+    u_a,
+    u_b,
+    dif,
+    x,
+    y,
+    info,
+    info_sem,
+    *,
+    extras,
 ):
+    places = pltpu.make_async_copy(info_in, info, info_sem)
+    places.start()
     place = lax.axis_index("dom")
     count = lax.axis_size("dom")
     zeros = jnp.zeros((PAD, 24, LANES), jnp.float32)
@@ -218,6 +239,16 @@
     next_lead = u_a[PAD : PAD + TILES, 16]
     x[0:TILES, 0] = x[0:TILES, 0] - jnp.where((place & 1) == 1, 0.5, 0.0) * next_lead
     surplus_rows(levels, sign, x, y, lane_matrix(levels), out)
+    places.wait()
+    send_blocks(info, lambda b: out[8 * b : 8 * b + 8, :], outgoing, extras)
+
+
+def send_blocks(info, block, outgoing, extras):
+    use = info[3, 0]
+    for b in range(info.shape[1]):
+        outgoing[info[0, b] * use] = block(b)
+    for i in range(extras):
+        outgoing[info[4, i] * use] = -0.5 * block(i % 8)
 
 
 def fix_kernel(levels, sign, coarse, blocks, out, x, y, stage):
@@ -228,11 +259,9 @@
     out[0:TILES, :] = blocks[0:TILES, :] - 0.5 * stage[0:TILES, :]
 
 
-def scatter_kernel(info, blocks, out, *, extras):
+def scatter_kernel(info, blocks, out):
     for b in range(blocks.shape[0]):
         out[info[0, b]] = blocks[b]
-    for i in range(extras):
-        out[info[4, i]] = -0.5 * blocks[i % 8]
 
 
 def row_zero_uses(dom_count):
@@ -336,7 +365,7 @@
     write_places(info, owner, none, jnp.int32(0), me, devices, capacity)
 
 
-def balance_kernel(keys, assigned, info, one, two, table, *, devices, capacity, full):
+def balance_kernel(keys, assigned, info, good, one, two, table, *, devices, capacity, full):
     rows = devices * SLOTS // LANES
     keys_all = keys[...]
     _, _, lane_all, row_one, row_two = key_parts(keys_all, rows)
@@ -378,12 +407,12 @@
         handler = lax.broadcasted_iota(jnp.int32, shape, 0)
         column = lax.broadcasted_iota(jnp.int32, shape, 1)
         handler_f = handler.astype(jnp.float32)
-        cost = dot_plain(price(load, 4.0 if first else 8.0), counts)
+        cost = dot_plain(price(load, 4.0 if first else 16.0), counts)
         was = None
         if not first:
             old = jnp.concatenate([table[pl.ds(base + i, 1), :] for i in range(group)], axis=1)
             was = handler_f == old
-            cost = jnp.where(was, dot_plain(price(load - 1.0, 8.0), counts) - 1.0, cost)
+            cost = jnp.where(was, dot_plain(price(load - 1.0, 16.0), counts) - 5.0, cost)
         noise = 0.5 * mixed(handler, column % LANES, base + column // LANES)
         ranked = jnp.floor((jnp.minimum(cost, 4000.0) + noise) * 64.0) * devices + handler_f
         least = jnp.min(ranked, axis=0, keepdims=True)
@@ -395,8 +424,15 @@
             change = change - jnp.where(was, 1.0, 0.0)
         return load + dot_rows(change, counts)
 
-    load = jnp.zeros(square, jnp.float32)
-    load = lax.fori_loop(0, rows // 2, lambda i, x: settle(one, 2, True, x, i), load)
+    def sweep(counts_ref, group, first, load):
+        return lax.fori_loop(
+            0, rows // group, lambda i, x: settle(counts_ref, group, first, x, i), load
+        )
+
+    def worst(load):
+        return jnp.max(jnp.where(own, 0.0, load))
+
+    load = sweep(one, 4, True, jnp.zeros(square, jnp.float32))
     spot = lax.broadcasted_iota(jnp.int32, (rows, LANES), 0)
     lane = lax.broadcasted_iota(jnp.int32, (rows, LANES), 1)
     from_row = (spot + rows - (lane % SLOTS) % rows) % rows
@@ -404,10 +440,23 @@
     for r in range(rows):
         moved = jnp.where(from_row == r, table[r : r + 1, :], moved)
     table[...] = moved
-    load = lax.fori_loop(0, rows // 2, lambda i, x: settle(two, 2, False, x, i), load)
-    load = lax.fori_loop(0, rows // 4, lambda i, x: settle(two, 4, False, x, i), load)
-
-    ok = jnp.max(jnp.where(own, 0.0, load)) <= capacity
+    load = sweep(two, 4, False, load)
+
+    def again(state):
+        count, _, load = state
+        load = lax.cond(
+            count == 0,
+            lambda x: sweep(two, 4, False, x),
+            lambda x: sweep(two, 2, False, x),
+            load,
+        )
+        return count + 1, worst(load), load
+
+    _, most, _ = lax.while_loop(
+        lambda state: (state[0] < 6) & (state[1] > capacity), again, (0, worst(load), load)
+    )
+    ok = most <= capacity
+    good[0] = ok.astype(jnp.int32)
     owner = (from_row + rows * (lane // SLOTS)).astype(jnp.float32)
     final = jnp.where(ok, table[...], owner)
     assigned[...] = final
@@ -568,35 +617,17 @@
     low = lax.ppermute(low_rows.reshape(3, TILES, LANES), "dom", up)
     high = lax.ppermute(high_rows.reshape(5, TILES, LANES), "dom", down)
 
-    blocks_in, lead = pl.pallas_call(
-        rows_kernel,
-        out_shape=(f32(rows * TILES, LANES), f32(TILES, LANES)),
-        in_specs=[SM, SM, SM, VM, VM, VM, VM],
-        out_specs=(VM, VM),
-        scratch_shapes=[
-            pltpu.VMEM((TILES + 2 * PAD, 24, LANES), jnp.float32),
-            pltpu.VMEM((TILES + 2 * PAD, 24, LANES), jnp.float32),
-            pltpu.VMEM((TILES, 24, LANES), jnp.float32),
-            pltpu.VMEM((TILES + 1, 16, LANES), jnp.float32),
-            pltpu.VMEM((TILES + 64, 16, LANES), jnp.float32),
-        ],
-        compiler_params=params(),
-        name="rows",
-        cost_estimate=SMALL,
-    )(levels, velocity, grid_signs, conc, dif, low, high)
-
-    keys, blocks_in = lax.optimization_barrier((keys, blocks_in))
     balanced = capacity >= 8 and devices * SLOTS % LANES == 0 and devices <= 64
     info_shape = jax.ShapeDtypeStruct((8, blocks), jnp.int32)
     if balanced:
         key_rows = devices * SLOTS // LANES
-        assigned, info = pl.pallas_call(
+        assigned, info, good = pl.pallas_call(
             functools.partial(
                 balance_kernel, devices=devices, capacity=capacity // 2, full=capacity
             ),
-            out_shape=(f32(key_rows, LANES), info_shape),
+            out_shape=(f32(key_rows, LANES), info_shape, jax.ShapeDtypeStruct((1,), jnp.int32)),
             in_specs=[VM],
-            out_specs=(VM, VM),
+            out_specs=(VM, VM, SM),
             scratch_shapes=[
                 pltpu.VMEM((key_rows * devices, LANES), jnp.float32),
                 pltpu.VMEM((key_rows * devices, LANES), jnp.float32),
@@ -616,6 +647,32 @@
             name="places",
             cost_estimate=SMALL,
         )(keys)
+
+    low, high, info = lax.optimization_barrier((low, high, info))
+    slots = capacity // 2 if balanced else capacity
+    extras = 8 * len(row_zero_uses(dom_count)) if balanced else 0
+    blocks_in, lead, outgoing = pl.pallas_call(
+        functools.partial(rows_kernel, extras=extras),
+        out_shape=(
+            f32(rows * TILES, LANES),
+            f32(TILES, LANES),
+            f32(devices * slots, 8, LANES),
+        ),
+        in_specs=[SM, SM, SM, VM, VM, VM, VM, VM],
+        out_specs=(VM, VM, VM),
+        scratch_shapes=[
+            pltpu.VMEM((TILES + 2 * PAD, 24, LANES), jnp.float32),
+            pltpu.VMEM((TILES + 2 * PAD, 24, LANES), jnp.float32),
+            pltpu.VMEM((TILES, 24, LANES), jnp.float32),
+            pltpu.VMEM((TILES + 1, 16, LANES), jnp.float32),
+            pltpu.VMEM((TILES + 64, 16, LANES), jnp.float32),
+            pltpu.SMEM((8, blocks), jnp.int32),
+            pltpu.SemaphoreType.DMA,
+        ],
+        compiler_params=params(),
+        name="rows",
+        cost_estimate=SMALL,
+    )(levels, velocity, grid_signs, info, conc, dif, low, high)
 
     def fixed():
         coarse = None
@@ -639,7 +696,7 @@
             name="fix_row",
         )(levels, grid_signs, coarse, blocks_in)
 
-    def route(own, slots, balanced, extras, tables):
+    def route(own, outgoing, slots, extras, tables):
         pieces = devices * SLOTS if balanced else SLOTS
 
         def exchange(x):
@@ -652,14 +709,15 @@
             ).reshape(devices * slots, 8, LANES)
 
         own = own.reshape(blocks, 8, LANES)
-        outgoing = pl.pallas_call(
-            functools.partial(scatter_kernel, extras=extras),
-            out_shape=f32(devices * slots, 8, LANES),
-            in_specs=[SM, VM],
-            out_specs=VM,
-            compiler_params=params(),
-            name="scatter",
-        )(info, own)
+        if outgoing is None:
+            outgoing = pl.pallas_call(
+                scatter_kernel,
+                out_shape=f32(devices * slots, 8, LANES),
+                in_specs=[SM, VM],
+                out_specs=VM,
+                compiler_params=params(),
+                name="scatter",
+            )(info, own)
         arrived = exchange(outgoing)
         table = pl.pallas_call(
             functools.partial(
@@ -699,14 +757,12 @@
 
     if balanced:
         combined = lax.cond(
-            info[3, 0] != 0,
-            lambda: route(
-                blocks_in, capacity // 2, True, 8 * len(row_zero_uses(dom_count)), (keys, assigned)
-            ),
-            lambda: route(fixed(), capacity, True, 0, (keys, assigned)),
+            good[0] != 0,
+            lambda: route(blocks_in, outgoing, slots, extras, (keys, assigned)),
+            lambda: route(fixed(), None, capacity, 0, (keys, assigned)),
         )
     else:
-        combined = route(fixed(), capacity, False, 0, (keys,))
+        combined = route(fixed(), None, capacity, 0, (keys,))
     return combined[None]
 
 

time: 82.9 us -> 76.8 us (0.926)
  Pallas kernels: 21.4 us -> 19.3 us
  starting transfers between devices: 19.8 us -> 17.8 us
  waiting for transfers between devices: 15.9 us -> 14.6 us
    all_to_all x1, starting transfers between devices: 7.46 us -> 5.41 us  [exchange(): lax.all_to_all(x.reshape(devices, slots * 8, LANES), ('grid', 'dom'), spl...]
    pallas_call x1, Pallas kernels: 7.1 us -> 5.42 us  [body(): pl.pallas_call(functools.partial(balance_kernel, devices=devices, capacit...]
    ppermute x1, waiting for transfers between devices: 0.94 us -> 0.01 us  [body(): low = lax.ppermute(low_rows.reshape(3, TILES, LANES), 'dom', up)]
    pallas_call x2 -> x1, Pallas kernels: 9.27 us -> 8.78 us  [body(): pl.pallas_call(functools.partial(rows_kernel, extras=extras), out_shape=(...]
  transfers between devices with their start and end apart: 4 -> 4, of which waited for: 3 -> 1; matrix products, arithmetic and copies ran while one was open for 3% -> 3% of each run, Pallas kernels for 1% -> 8%
where the time goes in v5:
time: 76.8 us; the launch traced here: 76.4 us
  Pallas kernels  19.3 us (25%)
  blocking collectives  18.3 us (24%)
  starting transfers between devices  17.8 us (23%)
  waiting for transfers between devices  14.6 us (19%)
  local copies, waits for them, and re-layouts  4.25 us (6%)
  between operations  1.49 us (2%)
    all_to_all x1, blocking collectives, exchange(): lax.all_to_all(x.reshape(devices, slots * 8, LANES), ('grid', 'dom'), spl...  18.3 us
    all_to_all x1, waiting for transfers between devices, exchange(): lax.all_to_all(x.reshape(devices, slots * 8, LANES), ('grid', 'dom'), spl...  14.6 us
    pallas_call x1, Pallas kernels, body(): pl.pallas_call(functools.partial(rows_kernel, extras=extras), out_shape=(...  8.78 us
    all_to_all x1, starting transfers between devices, body(): lax.all_to_all(jnp.broadcast_to(own_keys[:, None], (devices, 4, blocks)),...  7.1 us
    pallas_call x1, Pallas kernels, body(): pl.pallas_call(functools.partial(balance_kernel, devices=devices, capacit...  5.42 us
    all_to_all x1, starting transfers between devices, exchange(): lax.all_to_all(x.reshape(devices, slots * 8, LANES), ('grid', 'dom'), spl...  5.41 us
    ppermute x1, starting transfers between devices, body(): low = lax.ppermute(low_rows.reshape(3, TILES, LANES), 'dom', up)  3.99 us
    unnamed x16, local copies, waits for them, and re-layouts  3.57 us
  transfers between devices with their start and end apart: 4, of which 1 were waited for; matrix products, arithmetic and copies ran while one was open for 3% of the time, Pallas kernels for 8%

profile of v5, /device:TPU:1, one launch (start us, length us, event | category | flops | bytes accessed | tf_op | source)
XLA Modules:
  0.0 76.4 jit_solution(17634934661587783192)
XLA Ops:
  0.0 0.7 add_bitcast_fusion
  0.7 0.6 broadcast_in_dim.16
  1.3 7.1 %all-to-all-start.4 = ((s32[32,4,128]{2,1,0:T(4,128)}), s32[32,4,128]{2,1,0:T(4,128)S(1)}, u32[]{:S(2)}, u32[]{:S(2)}) async-start(s32[32,4,128]{2,1,0:T(4,128)} %broadcast_in_dim.16), calls=%async_computation.4 | async-start | bytes 131072 | tf_op jit(solution)/shard_map/all_to_all | solution.py:605
  8.4 0.0 copy-start.1
  8.4 1.0 %slice_bitcast_fusion.1 = f32[1,2,64,128]{3,1,2,0:T(2,128)S(1)} fusion(f32[1,16,8192]{2,1,0:T(8,128)} %param.10), kind=kLoop, calls=%fused_computation.6 | loop fusion | bytes 131072
  9.5 0.0 copy-start
  9.5 1.0 %slice_bitcast_fusion = f32[1,3,64,128]{3,1,2,0:T(4,128)S(1)} fusion(f32[1,16,8192]{2,1,0:T(8,128)} %param.9), kind=kLoop, calls=%fused_computation.1 | loop fusion | bytes 196608
  10.6 1.3 %collective-permute-start.3 = (f32[5,64,128]{2,1,0:T(8,128)S(1)}, f32[5,64,128]{2,1,0:T(8,128)S(1)}, u32[]{:S(2)}, u32[]{:S(2)}) collective-permute-start(f32[5,64,128]{2,1,0:T(8,128)S(1)} %pad_maximum_fusion), channel_id=1, source_target_pairs={{1,0},{2,1},{3,2},{5,4},{6,5},{7,6},{9,8},{10,9},{11,10},{13,12},{... | collective-permute-start | bytes 491528 | tf_op jit(solution)/shard_map/ppermute | solution.py:618
  11.9 0.0 copy-done.1
  11.9 0.0 copy-done
  12.0 4.0 %collective-permute-start.2 = (f32[3,64,128]{2,1,0:T(8,128)S(1)}, f32[3,64,128]{2,1,0:T(8,128)S(1)}, u32[]{:S(2)}, u32[]{:S(2)}) collective-permute-start(f32[3,64,128]{2,1,0:T(8,128)S(1)} %pad_maximum_fusion.1), channel_id=1, source_target_pairs={{0,1},{1,2},{2,3},{4,5},{5,6},{6,7},{8,9},{9,10},{10,11},{12,13},{... | collective-permute-start | bytes 294920 | tf_op jit(solution)/shard_map/ppermute | solution.py:617
  16.6 0.0 all-to-all-done.4
  16.7 5.4 %balance.1 = (f32[16,128]{1,0:T(8,128)S(1)}, s32[8,128]{1,0:T(8,128)S(1)}, s32[1]{0:T(128)}) custom-call(s32[32,128]{1,0:T(8,128)S(1)} %bitcast.55), custom_call_target="tpu_custom_call" | custom-call | tf_op jit(solution)/shard_map/balance/pallas_call | solution.py:624
  22.7 0.0 collective-permute-done.2.low
  22.7 0.0 collective-permute-done.3.high
  22.8 0.0 copy-start.2
  22.8 0.0 copy-start.4
  22.8 0.6 copy-done.2
  23.4 0.0 copy-done.4
  23.4 8.8 %rows.1 = (f32[1024,128]{1,0:T(8,128)S(1)}, f32[64,128]{1,0:T(8,128)S(1)}, f32[128,8,128]{2,1,0:T(8,128)}) custom-call(s32[1,3]{1,0:T(1,128)S(1)} %copy-done.4, f32[4]{0:T(128)S(1)} %copy-done.2, s32[1]{0:T(128)S(6)} %copy.23.sign, s32[8,128]{1,0:T(8,128)S(1)} %get-tuple-element.61.info_in, f32[16,8192]{1,0:T(8,128)S(1)} %bitcast.46, ...), custom_call_target="tpu_custom_call" | custom-call | tf_op jit(solution)/shard_map/rows/pallas_call | solution.py:654
  32.2 43.4 %conditional.1 = (f32[1,16,8192]{2,1,0:T(8,128)S(1)}) conditional(s32[]{:T(128)} %bitcast.14, (s32[32,128]{1,0:T(8,128)S(1)}, f32[16,128]{1,0:T(8,128)S(1)}, f32[64,128]{1,0:T(8,128)S(1)}, s32[1,3]{1,0:T(1,128)S(1)}, s32[1]{0:T(128)}, /*index=5*/f32[1024,128]{1,0:T(8,128)S(1)}, s32[8,128]{1,0:T(8,128)S(1)}) %tuple.24, (s32[32,128]{1,0:T(8,128)S(1)}, ...), branch_computations={%region_0.0_spmd, %region_1.0_spmd} | conditional | flops 8192 | bytes 5603448 | solution.py:759
  32.2 5.4 %all-to-all-start.2 = ((f32[32,32,128]{2,1,0:T(8,128)}), f32[32,32,128]{2,1,0:T(8,128)S(1)}, u32[]{:S(2)}, u32[]{:S(2)}) async-start(f32[32,32,128]{2,1,0:T(8,128)} %bitcast.6), calls=%async_computation.2 | async-start | bytes 1048576 | tf_op jit(solution)/shard_map/cond/branch_1_fun/all_to_all | solution.py:703
  37.7 0.7 piece_table.3.table
  38.4 14.6 %all-to-all-done.2 = f32[32,32,128]{2,1,0:T(8,128)S(1)} async-done(((f32[32,32,128]{2,1,0:T(8,128)}), f32[32,32,128]{2,1,0:T(8,128)S(1)}, u32[]{:S(2)}, u32[]{:S(2)}) %all-to-all-start.2) | async-done | bytes 524320 | tf_op jit(solution)/shard_map/cond/branch_1_fun/all_to_all | solution.py:703
  53.0 3.2 %sum_pieces.3 = (f32[128,8,128]{2,1,0:T(8,128)S(1)}, f32[128,8,128]{2,1,0:T(8,128)S(1)}) custom-call(s32[40,128]{1,0:T(8,128)S(1)} %piece_table.3.table, f32[128,8,128]{2,1,0:T(8,128)S(1)} %bitcast.44, f32[128,8,128]{2,1,0:T(8,128)S(1)} %bitcast.49), custom_call_target="tpu_custom_call" | custom-call | tf_op jit(solution)/shard_map/cond/branch_1_fun/sum_pieces/pallas_call | solution.py:738
  56.2 18.3 %all_to_all.22 = f32[32,32,128]{2,1,0:T(8,128)S(1)} all-to-all(f32[32,32,128]{2,1,0:T(8,128)S(1)} %bitcast.48), channel_id=1, replica_groups=mesh['grid'=8,'dom'=4] {'grid','dom'}, dimensions={0} | all-to-all | bytes 1048576 | tf_op jit(solution)/shard_map/cond/branch_1_fun/all_to_all | solution.py:703
  74.5 1.1 %unpack.3 = f32[16,8192]{1,0:T(8,128)S(1)} custom-call(s32[8,128]{1,0:T(8,128)S(1)} %get-tuple-element.42.info, f32[128,8,128]{2,1,0:T(8,128)S(1)} %bitcast.43, f32[128,8,128]{2,1,0:T(8,128)S(1)} %get-tuple-element.48.own), custom_call_target="tpu_custom_call" | custom-call | tf_op jit(solution)/shard_map/cond/branch_1_fun/unpack/pallas_call | solution.py:748
  75.6 0.0 copy-start.3
  75.6 0.8 %copy-done.3 = f32[1,16,8192]{2,1,0:T(8,128)} copy-done((f32[1,16,8192]{2,1,0:T(8,128)}, f32[1,16,8192]{2,1,0:T(8,128)S(1)}, u32[]{:S(2)}) %copy-start.3) | copy-done | bytes 524312
  (8 shorter events, 0.1 us)
Async XLA Ops:
  1.3 15.3 %all-to-all-start.4 = ((s32[32,4,128]{2,1,0:T(4,128)}), s32[32,4,128]{2,1,0:T(4,128)S(1)}, u32[]{:S(2)}, u32[]{:S(2)}) async-start(s32[32,4,128]{2,1,0:T(4,128)} %broadcast_in_dim.16), calls=%async_computation.4 | async-start | bytes 131072 | tf_op jit(solution)/shard_map/all_to_all | solution.py:605
  8.4 3.4 %copy-start.1 = (f32[1,16,8192]{2,1,0:T(8,128)S(1)}, f32[1,16,8192]{2,1,0:T(8,128)}, u32[]{:S(2)}) copy-start(f32[1,16,8192]{2,1,0:T(8,128)} %param.10) | copy-start | bytes 1572868
  9.5 2.4 %copy-start = (f32[1,16,8192]{2,1,0:T(8,128)S(1)}, f32[1,16,8192]{2,1,0:T(8,128)}, u32[]{:S(2)}) copy-start(f32[1,16,8192]{2,1,0:T(8,128)} %param.9) | copy-start | bytes 1572868
  10.6 12.2 %collective-permute-start.3 = (f32[5,64,128]{2,1,0:T(8,128)S(1)}, f32[5,64,128]{2,1,0:T(8,128)S(1)}, u32[]{:S(2)}, u32[]{:S(2)}) collective-permute-start(f32[5,64,128]{2,1,0:T(8,128)S(1)} %pad_maximum_fusion), channel_id=1, source_target_pairs={{1,0},{2,1},{3,2},{5,4},{6,5},{7,6},{9,8},{10,9},{11,10},{13,12},{... | collective-permute-start | bytes 491528 | tf_op jit(solution)/shard_map/ppermute | solution.py:618
  12.0 10.8 %collective-permute-start.2 = (f32[3,64,128]{2,1,0:T(8,128)S(1)}, f32[3,64,128]{2,1,0:T(8,128)S(1)}, u32[]{:S(2)}, u32[]{:S(2)}) collective-permute-start(f32[3,64,128]{2,1,0:T(8,128)S(1)} %pad_maximum_fusion.1), channel_id=1, source_target_pairs={{0,1},{1,2},{2,3},{4,5},{5,6},{6,7},{8,9},{9,10},{10,11},{12,13},{... | collective-permute-start | bytes 294920 | tf_op jit(solution)/shard_map/ppermute | solution.py:617
  22.8 0.7 copy-start.2
  22.8 0.7 copy-start.4
  32.2 20.7 %all-to-all-start.2 = ((f32[32,32,128]{2,1,0:T(8,128)}), f32[32,32,128]{2,1,0:T(8,128)S(1)}, u32[]{:S(2)}, u32[]{:S(2)}) async-start(f32[32,32,128]{2,1,0:T(8,128)} %bitcast.6), calls=%async_computation.2 | async-start | bytes 1048576 | tf_op jit(solution)/shard_map/cond/branch_1_fun/all_to_all | solution.py:703
  75.6 0.8 %copy-start.3 = (f32[1,16,8192]{2,1,0:T(8,128)}, f32[1,16,8192]{2,1,0:T(8,128)S(1)}, u32[]{:S(2)}) copy-start(f32[1,16,8192]{2,1,0:T(8,128)S(1)} %get-tuple-element.74) | copy-start | bytes 1572868

commit v6 on v5

--- a/solution.py
+++ b/solution.py
@@ -13,6 +13,8 @@
 LANES = 128
 TILES = 2**LR // LANES
 PAD = 9
+COPIES = 4
+MOST_KEYS = 256
 VMEM_LIMIT = 48 * 1024 * 1024
 
 
@@ -22,6 +24,7 @@
 
 SMALL = pl.CostEstimate(flops=0, transcendentals=0, bytes_accessed=0)
 VM = pl.BlockSpec(memory_space=pltpu.VMEM)
+HBM = pl.BlockSpec(memory_space=pltpu.HBM)
 SM = pl.BlockSpec(memory_space=pltpu.SMEM)
 
 
@@ -334,6 +337,14 @@
     )
 
 
+def all_keys(keys):
+    return keys[pl.ds(0, keys.shape[0] // COPIES, stride=COPIES), :]
+
+
+def keys_of(keys, device):
+    return keys[pl.ds(device * COPIES, 1), :]
+
+
 def device_number():
     return lax.axis_index("grid") * lax.axis_size("dom") + lax.axis_index("dom")
 
@@ -360,14 +371,15 @@
 
 def owner_places_kernel(keys, info, *, devices, capacity):
     me = device_number()
-    owner = (keys[pl.ds(me, 1), :] // SLOTS).astype(jnp.float32)
+    owner = (keys_of(keys, me) // SLOTS).astype(jnp.float32)
     none = jnp.full(owner.shape, -1.0, jnp.float32)
     write_places(info, owner, none, jnp.int32(0), me, devices, capacity)
 
 
 def balance_kernel(keys, assigned, info, good, one, two, table, *, devices, capacity, full):
     rows = devices * SLOTS // LANES
-    keys_all = keys[...]
+    deep = devices + 8
+    keys_all = all_keys(keys)
     _, _, lane_all, row_one, row_two = key_parts(keys_all, rows)
     dom_count = lax.axis_size("dom")
     lane_more, one_more, two_more = [
@@ -384,11 +396,16 @@
         place = d % dom_count
         if any(has_use(place, *use, dom_count) for use in row_zero_uses(dom_count)):
             counts = counts + counted(one_more[pick], two_more[pick], lane_more[pick])
-        one[pl.ds(d, rows, stride=devices), :] = counts[:rows]
-        two[pl.ds(d, rows, stride=devices), :] = counts[rows:]
-
-    square = (devices, devices)
-    own = lax.broadcasted_iota(jnp.int32, square, 0) == lax.broadcasted_iota(jnp.int32, square, 1)
+        one[pl.ds(d, rows, stride=deep), :] = counts[:rows]
+        two[pl.ds(d, rows, stride=deep), :] = counts[rows:]
+    for r in range(rows):
+        spare = pl.ds(r * deep + devices, deep - devices)
+        one[spare, :] = jnp.ones((deep - devices, LANES), jnp.float32)
+        two[spare, :] = jnp.ones((deep - devices, LANES), jnp.float32)
+
+    square = (devices, deep)
+    sender = lax.broadcasted_iota(jnp.int32, square, 1)
+    own = (lax.broadcasted_iota(jnp.int32, square, 0) == sender) | (sender >= devices)
 
     def price(load, steep):
         value = jnp.exp2(load * 0.3785) + steep * jnp.maximum(load - (capacity - 1), 0.0)
@@ -398,7 +415,7 @@
         base = number * group
         counts = jnp.concatenate(
             [
-                counts_ref[pl.ds(pl.multiple_of((base + i) * devices, devices), devices), :]
+                counts_ref[pl.ds(pl.multiple_of((base + i) * deep, 8), deep), :]
                 for i in range(group)
             ],
             axis=1,
@@ -452,10 +469,10 @@
         )
         return count + 1, worst(load), load
 
-    _, most, _ = lax.while_loop(
+    _, most, load = lax.while_loop(
         lambda state: (state[0] < 6) & (state[1] > capacity), again, (0, worst(load), load)
     )
-    ok = most <= capacity
+    ok = (most <= capacity) & (jnp.max(jnp.where(sender < devices, 0.0, load)) <= MOST_KEYS)
     good[0] = ok.astype(jnp.int32)
     owner = (from_row + rows * (lane // SLOTS)).astype(jnp.float32)
     final = jnp.where(ok, table[...], owner)
@@ -463,7 +480,7 @@
     me = device_number()
 
     def found(device):
-        _, _, lane_row, _, row = key_parts(keys[pl.ds(device, 1), :], rows)
+        _, _, lane_row, _, row = key_parts(keys_of(keys, device), rows)
         return handlers_of(final, lane_row, row)
 
     place = lax.axis_index("dom")
@@ -478,27 +495,45 @@
     write_places(info, found(me), extra, ok.astype(jnp.int32), me, devices, size)
 
 
+def flat_rows(devices, capacity):
+    return -(-devices * capacity // LANES)
+
+
 def table_kernel(*refs, devices, capacity, pieces, balanced, more):
     if balanced:
-        keys, assigned, out, handlers = refs
+        keys, assigned, out, handlers, numbers = refs
+        me = device_number()
         rows = devices * SLOTS // LANES
         table = assigned[...]
-        _, _, lane_all, _, row_all = key_parts(keys[...], rows)
+        mine = jnp.where(table == me.astype(jnp.float32), 1.0, 0.0)
+        first = lax.broadcasted_iota(jnp.int32, (LANES, LANES), 0)
+        second = lax.broadcasted_iota(jnp.int32, (LANES, LANES), 1)
+        in_row = dot_plain(mine, jnp.where(first < second, 1.0, 0.0))
+        upper = lax.broadcasted_iota(jnp.int32, (rows, rows), 0)
+        lower = lax.broadcasted_iota(jnp.int32, (rows, rows), 1)
+        above = dot_plain(jnp.where(lower < upper, 1.0, 0.0), mine)
+        number = in_row + jnp.sum(above, axis=1, keepdims=True)
+        both = jnp.concatenate([table, jnp.where(mine > 0.0, number, 0.0)], axis=0)
+        _, _, lane_all, _, row_all = key_parts(all_keys(keys), rows)
         for d in range(devices):
-            handlers[d : d + 1, :] = handlers_of(table, lane_all[d : d + 1], row_all[d : d + 1])
-        piece = keys[...]
+            at = slice(d, d + 1)
+            found = dot_plain(both, hot(lane_all[at], LANES))
+            pick = hot(row_all[at], rows)
+            handlers[at, :] = jnp.sum(pick * found[:rows], axis=0, keepdims=True)
+            numbers[at, :] = jnp.sum(pick * found[rows:], axis=0, keepdims=True)
+        piece = numbers[...].astype(jnp.int32)
     else:
-        keys, out, handlers = refs
-        handlers[...] = (keys[...] // SLOTS).astype(jnp.float32)
-        piece = keys[...] % SLOTS
-    me = device_number()
-    size = keys.shape[1]
+        keys, out, handlers, numbers = refs
+        me = device_number()
+        handlers[...] = (all_keys(keys) // SLOTS).astype(jnp.float32)
+        piece = all_keys(keys) % SLOTS
+    size = piece.shape[1]
     mine = handlers[...] == me.astype(jnp.float32)
     sender = lax.broadcasted_iota(jnp.int32, (devices, size), 0)
     first = lax.broadcasted_iota(jnp.int32, (size, size), 0)
     second = lax.broadcasted_iota(jnp.int32, (size, size), 1)
     earlier = jnp.where(first <= second, 1.0, 0.0)
-    column = lax.broadcasted_iota(jnp.int32, (devices, size), 1)
+    column = lax.broadcasted_iota(jnp.int32, (devices, LANES), 1)
 
     def ranked(hits, ahead):
         count = jnp.where(hits, 1.0, 0.0)
@@ -511,81 +546,73 @@
         mine_more = extra_entries(handlers[...], dom_count, -1.0) == me.astype(jnp.float32)
         rank_more, _ = ranked(mine_more, total)
         groups.append((mine_more, rank_more, extra_entries(piece, dom_count, 0)))
-    found = jnp.full((devices, size), pieces, jnp.int32)
+    lines = [jnp.zeros((devices, LANES), jnp.int32) for _ in range(flat_rows(devices, capacity))]
+    spot = lax.broadcasted_iota(jnp.int32, (devices, LANES), 0) * capacity
     for r in range(capacity):
         at = jnp.zeros((devices, 1), jnp.int32)
         for hits, ranks, piece_of in groups:
             hit = hits & (sender != me) & (ranks == r + 1.0)
             at = at + jnp.sum(jnp.where(hit, piece_of - pieces, 0), axis=1, keepdims=True)
-        found = jnp.where(column == r, pieces + at, found)
-    out[0:devices, :] = found
-    rows_kept = [
-        jnp.sum(
-            jnp.where(hits & (sender == me), piece_of - pieces, 0), axis=0, keepdims=True
-        )
-        + pieces
-        for hits, _, piece_of in groups
-    ]
-    rows_kept += [jnp.full((1, size), pieces, jnp.int32)] * (8 - len(rows_kept))
-    out[devices : devices + 8, :] = jnp.concatenate(rows_kept, axis=0)
-
-
-def sum_kernel(table, arrived, own, out, own_out, pieces, *, devices, capacity, extras):
-    blocks = own.shape[0]
+        for i in range(len(lines)):
+            lines[i] = jnp.where(column + LANES * i == spot + r, at, lines[i])
+    lines = [jnp.sum(line, axis=0, keepdims=True) for line in lines]
+    for hits, _, piece_of in groups:
+        stays = hits & (sender == me)
+        lines.append(jnp.sum(jnp.where(stays, piece_of - pieces, 0), axis=0, keepdims=True))
+    lines += [jnp.zeros((1, LANES), jnp.int32)] * (8 - len(lines))
+    out[...] = jnp.concatenate(lines, axis=0) + pieces
+
+
+def own_sum_kernel(table, own, pieces, *, arrive_rows, extras):
     zero = jnp.zeros((8, LANES), jnp.float32)
 
-    def over_senders(act):
-        def one(d, carry):
-            for i in range(capacity):
-                act(table[d, i], d * capacity + i)
-            return carry
-
-        lax.fori_loop(0, devices, one, 0, unroll=2)
-
-    def over_kept(act):
-        def one(k, carry):
-            for i in range(8):
-                act(table[devices, 8 * k + i], 8 * k + i)
-            return carry
-
-        lax.fori_loop(0, blocks // 8, one, 0)
-
-    def clear(piece, at):
-        pieces[piece] = zero
-
-    def add(piece, at):
-        pieces[piece] = pieces[piece] + arrived[at]
-
-    def add_own(piece, at):
-        pieces[piece] = pieces[piece] + own[at]
-
-    def give(piece, at):
-        out[at] = pieces[piece]
-
-    def give_own(piece, at):
-        own_out[at] = pieces[piece]
-
-    over_senders(clear)
-    over_kept(clear)
+    def clear(k, carry):
+        for i in range(8):
+            pieces[8 * k + i] = zero
+        return carry
+
+    lax.fori_loop(0, pieces.shape[0] // 8, clear, 0)
+
+    def add(k, carry):
+        for i in range(8):
+            piece = table[arrive_rows, 8 * k + i]
+            pieces[piece] = pieces[piece] + own[8 * k + i]
+        return carry
+
+    lax.fori_loop(0, own.shape[0] // 8, add, 0)
     for i in range(extras):
-        clear(table[devices + 1, i], i)
-    over_senders(add)
-    over_kept(add_own)
-    for i in range(extras):
-        piece = table[devices + 1, i]
+        piece = table[arrive_rows + 1, i]
         pieces[piece] = pieces[piece] - 0.5 * own[i % 8]
-    over_senders(give)
-    over_kept(give_own)
-
-
-def unpack_kernel(info, back, own, out, stage):
-    for b in range(16 * TILES // 8):
-        stage[pl.ds(8 * b, 8), :] = jnp.where(info[2, b] != 0, own[b], back[info[1, b]])
-    for j in range(TILES):
-        for i in range(2):
-            out[8 * i : 8 * i + 8, j * LANES : (j + 1) * LANES] = stage[
+
+
+def sum_kernel(table, arrived, pieces_in, out, pieces):
+    places = arrived.shape[0]
+    for i in range(places):
+        piece = table[i // LANES, i % LANES]
+        pieces[piece] = pieces[piece] + arrived[i]
+    for i in range(places):
+        out[i] = pieces[table[i // LANES, i % LANES]]
+
+
+def own_back_kernel(table, pieces, out, *, arrive_rows):
+    for b in range(out.shape[0]):
+        out[b] = pieces[table[arrive_rows, b]]
+
+
+def unpack_kernel(info, back, own, out, stage, rows, sems):
+    halves = []
+    for i in range(2):
+        for b in range(TILES * i, TILES * (i + 1)):
+            stage[pl.ds(8 * b, 8), :] = jnp.where(info[2, b] != 0, own[b], back[info[1, b]])
+        for j in range(TILES):
+            rows[8 * i : 8 * i + 8, j * LANES : (j + 1) * LANES] = stage[
                 pl.ds(j + i * 8 * TILES, 8, stride=TILES), :
             ]
+        half = pl.ds(8 * i, 8)
+        halves.append(pltpu.make_async_copy(rows.at[half], out.at[half], sems.at[i]))
+        halves[i].start()
+    for half in halves:
+        half.wait()
 
 
 def f32(*shape):
@@ -603,12 +630,12 @@
 
     own_keys = owner_list * SLOTS + slot_list
     keys = lax.all_to_all(
-        jnp.broadcast_to(own_keys[:, None], (devices, 4, blocks)),
+        jnp.broadcast_to(own_keys[:, None], (devices, COPIES, blocks)),
         ("grid", "dom"),
         split_axis=0,
         concat_axis=0,
         tiled=True,
-    )[:, 0]
+    ).reshape(devices * COPIES, blocks)
 
     up = [(i, i + 1) for i in range(dom_count - 1)]
     down = [(i + 1, i) for i in range(dom_count - 1)]
@@ -629,8 +656,8 @@
             in_specs=[VM],
             out_specs=(VM, VM, SM),
             scratch_shapes=[
-                pltpu.VMEM((key_rows * devices, LANES), jnp.float32),
-                pltpu.VMEM((key_rows * devices, LANES), jnp.float32),
+                pltpu.VMEM((key_rows * (devices + 8), LANES), jnp.float32),
+                pltpu.VMEM((key_rows * (devices + 8), LANES), jnp.float32),
                 pltpu.VMEM((key_rows, LANES), jnp.float32),
             ],
             compiler_params=params(),
@@ -697,7 +724,8 @@
         )(levels, grid_signs, coarse, blocks_in)
 
     def route(own, outgoing, slots, extras, tables):
-        pieces = devices * SLOTS if balanced else SLOTS
+        pieces = MOST_KEYS if balanced else SLOTS
+        arrive_rows = flat_rows(devices, slots)
 
         def exchange(x):
             return lax.all_to_all(
@@ -728,29 +756,50 @@
                 balanced=balanced,
                 more=extras > 0,
             ),
-            out_shape=jax.ShapeDtypeStruct((devices + 8, blocks), jnp.int32),
+            out_shape=jax.ShapeDtypeStruct((8, LANES), jnp.int32),
             in_specs=[VM] * len(tables),
             out_specs=VM,
-            scratch_shapes=[pltpu.VMEM((devices, blocks), jnp.float32)],
+            scratch_shapes=[pltpu.VMEM((devices, blocks), jnp.float32)] * 2,
             compiler_params=params(),
             name="piece_table",
         )(*tables)
-        returned, own_back = pl.pallas_call(
-            functools.partial(sum_kernel, devices=devices, capacity=slots, extras=extras),
-            out_shape=(f32(devices * slots, 8, LANES), f32(blocks, 8, LANES)),
+        all_pieces = f32(pieces + 8, 8, LANES)
+        started = pl.pallas_call(
+            functools.partial(own_sum_kernel, arrive_rows=arrive_rows, extras=extras),
+            out_shape=all_pieces,
+            in_specs=[SM, VM],
+            out_specs=VM,
+            compiler_params=params(),
+            name="sum_own",
+        )(table, own)
+        returned, summed = pl.pallas_call(
+            sum_kernel,
+            out_shape=(f32(devices * slots, 8, LANES), all_pieces),
             in_specs=[SM, VM, VM],
             out_specs=(VM, VM),
-            scratch_shapes=[pltpu.VMEM((pieces + 8, 8, LANES), jnp.float32)],
+            input_output_aliases={2: 1},
             compiler_params=params(),
-            name="sum_pieces",
-        )(table, arrived, own)
+            name="sum_arrived",
+        )(table, arrived, started)
+        own_back = pl.pallas_call(
+            functools.partial(own_back_kernel, arrive_rows=arrive_rows),
+            out_shape=f32(blocks, 8, LANES),
+            in_specs=[SM, VM],
+            out_specs=VM,
+            compiler_params=params(),
+            name="own_back",
+        )(table, summed)
         back = exchange(returned)
         return pl.pallas_call(
             unpack_kernel,
             out_shape=f32(rows, TILES * LANES),
             in_specs=[SM, VM, VM],
-            out_specs=VM,
-            scratch_shapes=[pltpu.VMEM((16 * TILES, LANES), jnp.float32)],
+            out_specs=HBM,
+            scratch_shapes=[
+                pltpu.VMEM((16 * TILES, LANES), jnp.float32),
+                pltpu.VMEM((16, TILES * LANES), jnp.float32),
+                pltpu.SemaphoreType.DMA((2,)),
+            ],
             compiler_params=params(),
             name="unpack",
         )(info, back, own_back)

time: 76.8 us -> 73.8 us (0.961)
  blocking collectives: 18.3 us -> 0 us
  waiting for transfers between devices: 14.6 us -> 27.5 us
  starting transfers between devices: 17.8 us -> 21 us
  local copies, waits for them, and re-layouts: 4.25 us -> 3.47 us
    all_to_all x1 -> x0, blocking collectives: 18.3 us -> none  [exchange(): lax.all_to_all(x.reshape(devices, slots * 8, LANES), ('grid', 'dom'), spl...]
    all_to_all x1 -> x2, waiting for transfers between devices: 14.6 us -> 27.5 us  [exchange(): lax.all_to_all(x.reshape(devices, slots * 8, LANES), ('grid', 'dom'), spl...]
    all_to_all x1 -> x2, starting transfers between devices: 5.41 us -> 8.59 us  [exchange(): lax.all_to_all(x.reshape(devices, slots * 8, LANES), ('grid', 'dom'), spl...]
    pallas_call x1, Pallas kernels: 5.42 us -> 4.07 us  [body(): pl.pallas_call(functools.partial(balance_kernel, devices=devices, capacit...]
    pallas_call x1 -> x3, Pallas kernels: 3.23 us -> 4.14 us  [the longest x1 1.94 us: route(): pl.pallas_call(sum_kernel, out_shape=(f32(devices * slots, 8, LANES), all...]
    unnamed x16, local copies, waits for them, and re-layouts: 3.57 us -> 2.79 us
  transfers between devices with their start and end apart: 4 -> 5, of which waited for: 1 -> 2; matrix products, arithmetic and copies ran while one was open for 3% -> 3% of each run, Pallas kernels for 8% -> 10%
where the time goes in v6:
time: 73.8 us; the launch traced here: 73.3 us
  waiting for transfers between devices  27.5 us (37%)
  starting transfers between devices  21 us (28%)
  Pallas kernels  19.1 us (26%)
  local copies, waits for them, and re-layouts  3.47 us (5%)
  between operations  1.48 us (2%)
  other arithmetic  0.78 us (1%)
    all_to_all x2, waiting for transfers between devices, exchange(): lax.all_to_all(x.reshape(devices, slots * 8, LANES), ('grid', 'dom'), spl...  27.5 us
    pallas_call x1, Pallas kernels, body(): pl.pallas_call(functools.partial(rows_kernel, extras=extras), out_shape=(...  8.79 us
    all_to_all x2, starting transfers between devices, exchange(): lax.all_to_all(x.reshape(devices, slots * 8, LANES), ('grid', 'dom'), spl...  8.59 us
    all_to_all x1, starting transfers between devices, body(): lax.all_to_all(jnp.broadcast_to(own_keys[:, None], (devices, COPIES, bloc...  7.1 us
    pallas_call x1, Pallas kernels, body(): pl.pallas_call(functools.partial(balance_kernel, devices=devices, capacit...  4.07 us
    ppermute x1, starting transfers between devices, body(): low = lax.ppermute(low_rows.reshape(3, TILES, LANES), 'dom', up)  3.99 us
    unnamed x16, local copies, waits for them, and re-layouts  2.79 us
    pallas_call x1, Pallas kernels, route(): pl.pallas_call(sum_kernel, out_shape=(f32(devices * slots, 8, LANES), all...  1.94 us
  transfers between devices with their start and end apart: 5, of which 2 were waited for; matrix products, arithmetic and copies ran while one was open for 3% of the time, Pallas kernels for 10%

profile of v6, /device:TPU:1, one launch (start us, length us, event | category | flops | bytes accessed | tf_op | source)
XLA Modules:
  0.0 73.3 jit_solution(2309972384662738652)
XLA Ops:
  0.0 0.0 copy-start.2
  0.0 0.0 copy-start.1
  0.0 0.0 copy-start.5
  0.0 0.0 copy-start.3
  0.0 0.8 %add_bitcast_fusion = s32[128]{0:T(128)S(1)} fusion(s32[1,128]{1,0:T(1,128)} %param.15, s32[1,128]{1,0:T(1,128)} %param.14), kind=kLoop, calls=%fused_computation.8 | loop fusion | flops 256 | bytes 1536 | tf_op jit(solution)/shard_map/broadcast_in_dim | solution.py:633
  0.8 0.6 broadcast_in_dim.16
  1.4 7.1 %all-to-all-start.4 = ((s32[32,4,128]{2,1,0:T(4,128)}), s32[32,4,128]{2,1,0:T(4,128)S(1)}, u32[]{:S(2)}, u32[]{:S(2)}) async-start(s32[32,4,128]{2,1,0:T(4,128)} %broadcast_in_dim.16), calls=%async_computation.4 | async-start | bytes 131072 | tf_op jit(solution)/shard_map/all_to_all | solution.py:632
  8.5 1.0 %slice_bitcast_fusion.1 = f32[1,2,64,128]{3,1,2,0:T(2,128)S(1)} fusion(f32[1,16,8192]{2,1,0:T(8,128)} %param.10), kind=kLoop, calls=%fused_computation.6 | loop fusion | bytes 131072
  9.5 1.0 %slice_bitcast_fusion = f32[1,3,64,128]{3,1,2,0:T(4,128)S(1)} fusion(f32[1,16,8192]{2,1,0:T(8,128)} %param.9), kind=kLoop, calls=%fused_computation.1 | loop fusion | bytes 196608
  10.5 1.3 %collective-permute-start.3 = (f32[5,64,128]{2,1,0:T(8,128)S(1)}, f32[5,64,128]{2,1,0:T(8,128)S(1)}, u32[]{:S(2)}, u32[]{:S(2)}) collective-permute-start(f32[5,64,128]{2,1,0:T(8,128)S(1)} %pad_maximum_fusion), channel_id=1, source_target_pairs={{1,0},{2,1},{3,2},{5,4},{6,5},{7,6},{9,8},{10,9},{11,10},{13,12},{... | collective-permute-start | bytes 491528 | tf_op jit(solution)/shard_map/ppermute | solution.py:645
  11.8 0.0 copy-done.2
  11.9 0.0 copy-done.1
  12.0 4.0 %collective-permute-start.2 = (f32[3,64,128]{2,1,0:T(8,128)S(1)}, f32[3,64,128]{2,1,0:T(8,128)S(1)}, u32[]{:S(2)}, u32[]{:S(2)}) collective-permute-start(f32[3,64,128]{2,1,0:T(8,128)S(1)} %pad_maximum_fusion.1), channel_id=1, source_target_pairs={{0,1},{1,2},{2,3},{4,5},{5,6},{6,7},{8,9},{9,10},{10,11},{12,13},{... | collective-permute-start | bytes 294920 | tf_op jit(solution)/shard_map/ppermute | solution.py:644
  16.6 0.0 all-to-all-done.4
  16.6 4.1 %balance.1 = (f32[16,128]{1,0:T(8,128)S(1)}, s32[8,128]{1,0:T(8,128)S(1)}, s32[1]{0:T(128)}) custom-call(s32[128,128]{1,0:T(8,128)S(1)} %bitcast.47), custom_call_target="tpu_custom_call" | custom-call | tf_op jit(solution)/shard_map/balance/pallas_call | solution.py:651
  21.3 0.0 collective-permute-done.2.low
  21.4 0.0 collective-permute-done.3.high
  21.4 0.0 copy-done.5
  21.4 0.0 copy-done.3
  21.4 8.8 %rows.1 = (f32[1024,128]{1,0:T(8,128)S(1)}, f32[64,128]{1,0:T(8,128)S(1)}, f32[128,8,128]{2,1,0:T(8,128)}) custom-call(s32[1,3]{1,0:T(1,128)S(1)} %copy-done.5, f32[4]{0:T(128)S(1)} %copy-done.3, s32[1]{0:T(128)S(6)} %copy.25.sign, s32[8,128]{1,0:T(8,128)S(1)} %get-tuple-element.61.info_in, f32[16,8192]{1,0:T(8,128)S(1)} %bitcast.44, ...), custom_call_target="tpu_custom_call" | custom-call | tf_op jit(solution)/shard_map/rows/pallas_call | solution.py:681
  30.2 42.3 %conditional.1 = (f32[1,16,8192]{2,1,0:T(8,128)S(1)}) conditional(s32[]{:T(128)} %bitcast.14, (s32[128,128]{1,0:T(8,128)S(1)}, f32[16,128]{1,0:T(8,128)S(1)}, f32[64,128]{1,0:T(8,128)S(1)}, s32[1,3]{1,0:T(1,128)S(1)}, s32[1]{0:T(128)}, /*index=5*/f32[1024,128]{1,0:T(8,128)S(1)}, s32[8,128]{1,0:T(8,128)S(1)}) %tuple.24, (s32[128,128]{1,0:T(8,128)S(1)}, ...), branch_computations={%region_0.0_spmd, %region_1.0_spmd} | conditional | flops 8192 | bytes 10846388 | solution.py:808
  30.2 5.4 %all-to-all-start.2 = ((f32[32,32,128]{2,1,0:T(8,128)}), f32[32,32,128]{2,1,0:T(8,128)S(1)}, u32[]{:S(2)}, u32[]{:S(2)}) async-start(f32[32,32,128]{2,1,0:T(8,128)} %bitcast.50), calls=%async_computation.2 | async-start | bytes 1048576 | tf_op jit(solution)/shard_map/cond/branch_1_fun/all_to_all | solution.py:731
  35.6 0.9 %piece_table.3.table = s32[8,128]{1,0:T(8,128)S(1)} custom-call(s32[128,128]{1,0:T(8,128)S(1)} %get-tuple-element.43.refs_0_, f32[16,128]{1,0:T(8,128)S(1)} %get-tuple-element.44.refs_1_), custom_call_target="tpu_custom_call" | custom-call | tf_op jit(solution)/shard_map/cond/branch_1_fun/piece_table/pallas_call | solution.py:750
  36.5 1.5 %sum_own.3.pieces_in = f32[264,8,128]{2,1,0:T(8,128)S(1)} custom-call(s32[8,128]{1,0:T(8,128)S(1)} %piece_table.3.table, f32[128,8,128]{2,1,0:T(8,128)S(1)} %bitcast.46), custom_call_target="tpu_custom_call" | custom-call | tf_op jit(solution)/shard_map/cond/branch_1_fun/sum_own/pallas_call | solution.py:767
  38.0 12.9 %all-to-all-done.2 = f32[32,32,128]{2,1,0:T(8,128)S(1)} async-done(((f32[32,32,128]{2,1,0:T(8,128)}), f32[32,32,128]{2,1,0:T(8,128)S(1)}, u32[]{:S(2)}, u32[]{:S(2)}) %all-to-all-start.2) | async-done | bytes 524320 | tf_op jit(solution)/shard_map/cond/branch_1_fun/all_to_all | solution.py:731
  50.9 1.9 %sum_arrived.3 = (f32[128,8,128]{2,1,0:T(8,128)}, f32[264,8,128]{2,1,0:T(8,128)S(1)}) custom-call(s32[8,128]{1,0:T(8,128)S(1)} %piece_table.3.table, f32[128,8,128]{2,1,0:T(8,128)S(1)} %bitcast.42, f32[264,8,128]{2,1,0:T(8,128)S(1)} %sum_own.3.pieces_in), custom_call_target="tpu_custom_call", output_to_operand_aliasing={{1}: (2, {})} | custom-call | tf_op jit(solution)/shard_map/cond/branch_1_fun/sum_arrived/pallas_call | solution.py:775
  52.9 3.2 %all-to-all-start.3 = ((f32[32,32,128]{2,1,0:T(8,128)}), f32[32,32,128]{2,1,0:T(8,128)S(1)}, u32[]{:S(2)}, u32[]{:S(2)}) async-start(f32[32,32,128]{2,1,0:T(8,128)} %bitcast.9), calls=%async_computation.3 | async-start | bytes 1048576 | tf_op jit(solution)/shard_map/cond/branch_1_fun/all_to_all | solution.py:731
  56.0 0.7 own_back.3.own
  56.8 14.6 %all-to-all-done.3 = f32[32,32,128]{2,1,0:T(8,128)S(1)} async-done(((f32[32,32,128]{2,1,0:T(8,128)}), f32[32,32,128]{2,1,0:T(8,128)S(1)}, u32[]{:S(2)}, u32[]{:S(2)}) %all-to-all-start.3) | async-done | bytes 524320 | tf_op jit(solution)/shard_map/cond/branch_1_fun/all_to_all | solution.py:731
  71.3 1.2 %unpack.3 = f32[16,8192]{1,0:T(8,128)S(1)} custom-call(s32[8,128]{1,0:T(8,128)S(1)} %get-tuple-element.42.info, f32[128,8,128]{2,1,0:T(8,128)S(1)} %bitcast.41, f32[128,8,128]{2,1,0:T(8,128)S(1)} %own_back.3.own), custom_call_target="tpu_custom_call" | custom-call | tf_op jit(solution)/shard_map/cond/branch_1_fun/unpack/pallas_call | solution.py:793
  72.5 0.0 copy-start.4
  72.5 0.8 %copy-done.4 = f32[1,16,8192]{2,1,0:T(8,128)} copy-done((f32[1,16,8192]{2,1,0:T(8,128)}, f32[1,16,8192]{2,1,0:T(8,128)S(1)}, u32[]{:S(2)}) %copy-start.4) | copy-done | bytes 524312
  (7 shorter events, 0.1 us)
Async XLA Ops:
  0.0 11.8 %copy-start.2 = (f32[1,16,8192]{2,1,0:T(8,128)S(1)}, f32[1,16,8192]{2,1,0:T(8,128)}, u32[]{:S(2)}) copy-start(f32[1,16,8192]{2,1,0:T(8,128)} %param.10) | copy-start | bytes 1572868
  0.0 11.9 %copy-start.1 = (f32[1,16,8192]{2,1,0:T(8,128)S(1)}, f32[1,16,8192]{2,1,0:T(8,128)}, u32[]{:S(2)}) copy-start(f32[1,16,8192]{2,1,0:T(8,128)} %param.9) | copy-start | bytes 1572868
  0.0 21.4 %copy-start.5 = (s32[1,3]{1,0:T(1,128)S(1)}, s32[1,3]{1,0:T(1,128)}, u32[]{:S(2)}) copy-start(s32[1,3]{1,0:T(1,128)} %levels.1) | copy-start | bytes 40
  0.0 21.4 %copy-start.3 = (f32[4]{0:T(128)S(1)}, f32[4]{0:T(128)}, u32[]{:S(2)}) copy-start(f32[4]{0:T(128)} %velocity.1) | copy-start | bytes 52
  1.4 15.2 %all-to-all-start.4 = ((s32[32,4,128]{2,1,0:T(4,128)}), s32[32,4,128]{2,1,0:T(4,128)S(1)}, u32[]{:S(2)}, u32[]{:S(2)}) async-start(s32[32,4,128]{2,1,0:T(4,128)} %broadcast_in_dim.16), calls=%async_computation.4 | async-start | bytes 131072 | tf_op jit(solution)/shard_map/all_to_all | solution.py:632
  10.5 10.8 %collective-permute-start.3 = (f32[5,64,128]{2,1,0:T(8,128)S(1)}, f32[5,64,128]{2,1,0:T(8,128)S(1)}, u32[]{:S(2)}, u32[]{:S(2)}) collective-permute-start(f32[5,64,128]{2,1,0:T(8,128)S(1)} %pad_maximum_fusion), channel_id=1, source_target_pairs={{1,0},{2,1},{3,2},{5,4},{6,5},{7,6},{9,8},{10,9},{11,10},{13,12},{... | collective-permute-start | bytes 491528 | tf_op jit(solution)/shard_map/ppermute | solution.py:645
  12.0 9.4 %collective-permute-start.2 = (f32[3,64,128]{2,1,0:T(8,128)S(1)}, f32[3,64,128]{2,1,0:T(8,128)S(1)}, u32[]{:S(2)}, u32[]{:S(2)}) collective-permute-start(f32[3,64,128]{2,1,0:T(8,128)S(1)} %pad_maximum_fusion.1), channel_id=1, source_target_pairs={{0,1},{1,2},{2,3},{4,5},{5,6},{6,7},{8,9},{9,10},{10,11},{12,13},{... | collective-permute-start | bytes 294920 | tf_op jit(solution)/shard_map/ppermute | solution.py:644
  30.2 20.7 %all-to-all-start.2 = ((f32[32,32,128]{2,1,0:T(8,128)}), f32[32,32,128]{2,1,0:T(8,128)S(1)}, u32[]{:S(2)}, u32[]{:S(2)}) async-start(f32[32,32,128]{2,1,0:T(8,128)} %bitcast.50), calls=%async_computation.2 | async-start | bytes 1048576 | tf_op jit(solution)/shard_map/cond/branch_1_fun/all_to_all | solution.py:731
  52.9 18.5 %all-to-all-start.3 = ((f32[32,32,128]{2,1,0:T(8,128)}), f32[32,32,128]{2,1,0:T(8,128)S(1)}, u32[]{:S(2)}, u32[]{:S(2)}) async-start(f32[32,32,128]{2,1,0:T(8,128)} %bitcast.9), calls=%async_computation.3 | async-start | bytes 1048576 | tf_op jit(solution)/shard_map/cond/branch_1_fun/all_to_all | solution.py:731
  72.5 0.8 %copy-start.4 = (f32[1,16,8192]{2,1,0:T(8,128)}, f32[1,16,8192]{2,1,0:T(8,128)S(1)}, u32[]{:S(2)}) copy-start(f32[1,16,8192]{2,1,0:T(8,128)S(1)} %get-tuple-element.81) | copy-start | bytes 1572868

commit v7 on v6

--- a/solution.py
+++ b/solution.py
@@ -13,7 +13,7 @@
 LANES = 128
 TILES = 2**LR // LANES
 PAD = 9
-COPIES = 4
+COPIES = 8
 MOST_KEYS = 256
 VMEM_LIMIT = 48 * 1024 * 1024
 
@@ -120,7 +120,7 @@
     return jnp.concatenate([own, nxt], axis=0)
 
 
-def surplus_rows(levels, sign, x, y, matrix, stage):
+def surplus_rows(levels, factor, x, y, matrix, stage):
     rows = x.shape[1]
     x[TILES] = jnp.zeros((rows, LANES), jnp.float32)
     y[pl.ds(0, 32)] = jnp.zeros((32, rows, LANES), jnp.float32)
@@ -160,7 +160,6 @@
                 ahead_on = jnp.where((j & above) == above, 0.0, 1.0)
                 y[32 + j] = y[32 + j] + mine * (y[32 + j - t] + ahead_on * y[32 + j + t])
 
-    factor = sign[0].astype(jnp.float32)
     for j in range(TILES):
         tile = factor * y[32 + j]
         for i in range(0, rows, 8):
@@ -170,7 +169,7 @@
 def rows_kernel(
     levels,
     velocity,
-    sign,
+    sign_in,
     info_in,
     conc,
     dif_in,
@@ -185,12 +184,15 @@
     x,
     y,
     info,
-    info_sem,
+    sign,
+    sems,
     *,
     extras,
 ):
-    places = pltpu.make_async_copy(info_in, info, info_sem)
+    places = pltpu.make_async_copy(info_in, info, sems.at[0])
     places.start()
+    signs = pltpu.make_async_copy(sign_in, sign, sems.at[1])
+    signs.start()
     place = lax.axis_index("dom")
     count = lax.axis_size("dom")
     zeros = jnp.zeros((PAD, 24, LANES), jnp.float32)
@@ -230,7 +232,9 @@
     pl.when(small_three)(both(True, True))
     pl.when(small_two & jnp.logical_not(small_three))(both(True, False))
     pl.when(jnp.logical_not(small_two))(both(False, False))
-    lead[...] = u_a[PAD : PAD + TILES, 0]
+    signs.wait()
+    factor = sign[0].astype(jnp.float32)
+    lead[...] = factor * u_a[PAD : PAD + TILES, 0]
     for j in range(TILES):
         tile = u_a[PAD + j]
         for p in range(4):
@@ -241,7 +245,7 @@
         x[j] = tile[0:16]
     next_lead = u_a[PAD : PAD + TILES, 16]
     x[0:TILES, 0] = x[0:TILES, 0] - jnp.where((place & 1) == 1, 0.5, 0.0) * next_lead
-    surplus_rows(levels, sign, x, y, lane_matrix(levels), out)
+    surplus_rows(levels, factor, x, y, lane_matrix(levels), out)
     places.wait()
     send_blocks(info, lambda b: out[8 * b : 8 * b + 8, :], outgoing, extras)
 
@@ -254,10 +258,10 @@
         outgoing[info[4, i] * use] = -0.5 * block(i % 8)
 
 
-def fix_kernel(levels, sign, coarse, blocks, out, x, y, stage):
+def fix_kernel(levels, coarse, blocks, out, x, y, stage):
     x[...] = jnp.zeros_like(x)
     x[0:TILES, 0] = coarse[...]
-    surplus_rows(levels, sign, x, y, lane_matrix(levels), stage)
+    surplus_rows(levels, 1.0, x, y, lane_matrix(levels), stage)
     out[...] = blocks[...]
     out[0:TILES, :] = blocks[0:TILES, :] - 0.5 * stage[0:TILES, :]
 
@@ -369,6 +373,20 @@
     info[...] = jnp.concatenate([send, send, kept, flag, send_extra, flag, flag, flag], axis=0)
 
 
+def spread_kernel(keys, out):
+    out[...] = jnp.broadcast_to(keys[...], out.shape)
+
+
+def halo_kernel(conc, dif, low, high):
+    last = conc.shape[0] - 1
+    for j in range(TILES):
+        cols = slice(j * LANES, (j + 1) * LANES)
+        for i, (ref, row) in enumerate(((conc, last - 1), (conc, last), (dif, last))):
+            low[i, j : j + 1, :] = ref[row : row + 1, cols]
+        for i, (ref, row) in enumerate(((conc, 0), (conc, 1), (conc, 2), (dif, 0), (dif, 1))):
+            high[i, j : j + 1, :] = ref[row : row + 1, cols]
+
+
 def owner_places_kernel(keys, info, *, devices, capacity):
     me = device_number()
     owner = (keys_of(keys, me) // SLOTS).astype(jnp.float32)
@@ -376,7 +394,9 @@
     write_places(info, owner, none, jnp.int32(0), me, devices, capacity)
 
 
-def balance_kernel(keys, assigned, info, good, one, two, table, *, devices, capacity, full):
+def balance_kernel(
+    keys, assigned, info, good_out, one, two, table, good, good_sem, *, devices, capacity, full
+):
     rows = devices * SLOTS // LANES
     deep = devices + 8
     keys_all = all_keys(keys)
@@ -474,6 +494,8 @@
     )
     ok = (most <= capacity) & (jnp.max(jnp.where(sender < devices, 0.0, load)) <= MOST_KEYS)
     good[0] = ok.astype(jnp.int32)
+    tell = pltpu.make_async_copy(good, good_out, good_sem)
+    tell.start()
     owner = (from_row + rows * (lane // SLOTS)).astype(jnp.float32)
     final = jnp.where(ok, table[...], owner)
     assigned[...] = final
@@ -493,6 +515,7 @@
         extra = jnp.where((column >= 8 * t) & (column < 8 * t + 8) & there, moved, extra)
     size = jnp.where(ok, capacity, full)
     write_places(info, found(me), extra, ok.astype(jnp.int32), me, devices, size)
+    tell.wait()
 
 
 def flat_rows(devices, capacity):
@@ -628,9 +651,18 @@
     blocks = owner_list.shape[1]
     capacity = 2 * blocks // devices
 
-    own_keys = owner_list * SLOTS + slot_list
+    spread = pl.pallas_call(
+        spread_kernel,
+        out_shape=jax.ShapeDtypeStruct((devices * COPIES, blocks), jnp.int32),
+        in_specs=[VM],
+        out_specs=VM,
+        compiler_params=params(),
+        name="spread_keys",
+        cost_estimate=pl.CostEstimate(flops=10**10, transcendentals=0, bytes_accessed=0),
+    )(owner_list * SLOTS + slot_list)
+    spread, conc, dif = lax.optimization_barrier((spread, conc, dif))
     keys = lax.all_to_all(
-        jnp.broadcast_to(own_keys[:, None], (devices, COPIES, blocks)),
+        spread.reshape(devices, COPIES, blocks),
         ("grid", "dom"),
         split_axis=0,
         concat_axis=0,
@@ -639,10 +671,16 @@
 
     up = [(i, i + 1) for i in range(dom_count - 1)]
     down = [(i + 1, i) for i in range(dom_count - 1)]
-    low_rows = jnp.concatenate([conc[rows - 2 :], dif[rows - 1 :]], axis=0)
-    high_rows = jnp.concatenate([conc[:3], dif[:2]], axis=0)
-    low = lax.ppermute(low_rows.reshape(3, TILES, LANES), "dom", up)
-    high = lax.ppermute(high_rows.reshape(5, TILES, LANES), "dom", down)
+    low_rows, high_rows = pl.pallas_call(
+        halo_kernel,
+        out_shape=(f32(3, TILES, LANES), f32(5, TILES, LANES)),
+        in_specs=[VM, VM],
+        out_specs=(VM, VM),
+        compiler_params=params(),
+        name="halo_rows",
+    )(conc, dif)
+    low = lax.ppermute(low_rows, "dom", up)
+    high = lax.ppermute(high_rows, "dom", down)
 
     balanced = capacity >= 8 and devices * SLOTS % LANES == 0 and devices <= 64
     info_shape = jax.ShapeDtypeStruct((8, blocks), jnp.int32)
@@ -654,11 +692,13 @@
             ),
             out_shape=(f32(key_rows, LANES), info_shape, jax.ShapeDtypeStruct((1,), jnp.int32)),
             in_specs=[VM],
-            out_specs=(VM, VM, SM),
+            out_specs=(VM, VM, HBM),
             scratch_shapes=[
                 pltpu.VMEM((key_rows * (devices + 8), LANES), jnp.float32),
                 pltpu.VMEM((key_rows * (devices + 8), LANES), jnp.float32),
                 pltpu.VMEM((key_rows, LANES), jnp.float32),
+                pltpu.SMEM((1,), jnp.int32),
+                pltpu.SemaphoreType.DMA,
             ],
             compiler_params=params(),
             name="balance",
@@ -685,7 +725,7 @@
             f32(TILES, LANES),
             f32(devices * slots, 8, LANES),
         ),
-        in_specs=[SM, SM, SM, VM, VM, VM, VM, VM],
+        in_specs=[SM, SM, HBM, VM, VM, VM, VM, VM],
         out_specs=(VM, VM, VM),
         scratch_shapes=[
             pltpu.VMEM((TILES + 2 * PAD, 24, LANES), jnp.float32),
@@ -694,7 +734,8 @@
             pltpu.VMEM((TILES + 1, 16, LANES), jnp.float32),
             pltpu.VMEM((TILES + 64, 16, LANES), jnp.float32),
             pltpu.SMEM((8, blocks), jnp.int32),
-            pltpu.SemaphoreType.DMA,
+            pltpu.SMEM((1,), jnp.int32),
+            pltpu.SemaphoreType.DMA((2,)),
         ],
         compiler_params=params(),
         name="rows",
@@ -712,7 +753,7 @@
         return pl.pallas_call(
             fix_kernel,
             out_shape=f32(rows * TILES, LANES),
-            in_specs=[SM, SM, VM, VM],
+            in_specs=[SM, VM, VM],
             out_specs=VM,
             scratch_shapes=[
                 pltpu.VMEM((TILES + 1, 8, LANES), jnp.float32),
@@ -721,7 +762,7 @@
             ],
             compiler_params=params(),
             name="fix_row",
-        )(levels, grid_signs, coarse, blocks_in)
+        )(levels, coarse, blocks_in)
 
     def route(own, outgoing, slots, extras, tables):
         pieces = MOST_KEYS if balanced else SLOTS
@@ -789,7 +830,9 @@
             compiler_params=params(),
             name="own_back",
         )(table, summed)
-        back = exchange(returned)
+        return exchange(returned), own_back
+
+    def unpacked(back, own_back):
         return pl.pallas_call(
             unpack_kernel,
             out_shape=f32(rows, TILES * LANES),
@@ -805,13 +848,14 @@
         )(info, back, own_back)
 
     if balanced:
+        brought = route(blocks_in, outgoing, slots, extras, (keys, assigned))
         combined = lax.cond(
             good[0] != 0,
-            lambda: route(blocks_in, outgoing, slots, extras, (keys, assigned)),
-            lambda: route(fixed(), None, capacity, 0, (keys, assigned)),
+            lambda: unpacked(*brought),
+            lambda: unpacked(*route(fixed(), None, capacity, 0, (keys, assigned))),
         )
     else:
-        combined = route(fixed(), None, capacity, 0, (keys,))
+        combined = unpacked(*route(fixed(), None, capacity, 0, (keys,)))
     return combined[None]
 
 

time: 73.8 us -> 71.2 us (0.965)
  local copies, waits for them, and re-layouts: 3.47 us -> 0.8 us
  starting transfers between devices: 21 us -> 19.8 us
  Pallas kernels: 19.1 us -> 20 us
    unnamed x16 -> x10, local copies, waits for them, and re-layouts: 2.79 us -> 0.8 us
    all_to_all x2, starting transfers between devices: 8.59 us -> 7.41 us  [exchange(): lax.all_to_all(x.reshape(devices, slots * 8, LANES), ('grid', 'dom'), spl...]
    all_to_all x1, waiting for transfers between devices: 0.01 us -> 1.15 us  [body(): lax.all_to_all(spread.reshape(devices, COPIES, blocks), ('grid', 'dom'),...]
    pallas_call x1 -> x3, Pallas kernels: 1.17 us -> 2.02 us  [the longest x1 1.17 us: unpacked(): pl.pallas_call(unpack_kernel, out_shape=f32(rows, TILES * LANES), in_spec...]
    broadcast_in_dim x1 -> x0, other arithmetic: 0.76 us -> none  [body(): jnp.broadcast_to(own_keys[:, None], (devices, COPIES, blocks))]
  transfers between devices with their start and end apart: 5 -> 5, of which waited for: 2 -> 3; matrix products, arithmetic and copies ran while one was open for 3% -> 0% of each run, Pallas kernels for 10% -> 10%
where the time goes in v7:
time: 71.2 us; the launch traced here: 70.7 us
  waiting for transfers between devices  27.9 us (39%)
  Pallas kernels  20 us (28%)
  starting transfers between devices  19.8 us (28%)
  between operations  1.47 us (2%)
  local copies, waits for them, and re-layouts  0.8 us (1%)
    all_to_all x2, waiting for transfers between devices, exchange(): lax.all_to_all(x.reshape(devices, slots * 8, LANES), ('grid', 'dom'), spl...  26.8 us
    pallas_call x1, Pallas kernels, body(): pl.pallas_call(functools.partial(rows_kernel, extras=extras), out_shape=(...  8.8 us
    all_to_all x2, starting transfers between devices, exchange(): lax.all_to_all(x.reshape(devices, slots * 8, LANES), ('grid', 'dom'), spl...  7.41 us
    all_to_all x1, starting transfers between devices, body(): lax.all_to_all(spread.reshape(devices, COPIES, blocks), ('grid', 'dom'),...  7.1 us
    pallas_call x1, Pallas kernels, body(): pl.pallas_call(functools.partial(balance_kernel, devices=devices, capacit...  4.08 us
    ppermute x1, starting transfers between devices, body(): low = lax.ppermute(low_rows, 'dom', up)  3.99 us
    pallas_call x1, Pallas kernels, route(): pl.pallas_call(sum_kernel, out_shape=(f32(devices * slots, 8, LANES), all...  1.97 us
    pallas_call x1, Pallas kernels, route(): pl.pallas_call(functools.partial(own_sum_kernel, arrive_rows=arrive_rows,...  1.52 us
  transfers between devices with their start and end apart: 5, of which 3 were waited for; matrix products, arithmetic and copies ran while one was open for 0% of the time, Pallas kernels for 10%

profile of v7, /device:TPU:1, one launch (start us, length us, event | category | flops | bytes accessed | tf_op | source)
XLA Modules:
  0.0 70.7 jit_solution(7221720671228921493)
XLA Ops:
  0.0 0.7 multiply_add_fusion.keys
  0.7 0.0 copy-start
  0.7 0.0 copy-start.1
  0.7 0.7 spread_keys.1
  1.3 0.0 copy-start.3
  1.3 0.0 copy-start.5
  1.3 7.1 %all-to-all-start.2 = ((s32[32,8,128]{2,1,0:T(8,128)}), s32[32,8,128]{2,1,0:T(8,128)S(1)}, u32[]{:S(2)}, u32[]{:S(2)}) async-start(s32[32,8,128]{2,1,0:T(8,128)} %bitcast.10), calls=%async_computation.2 | async-start | bytes 262144 | tf_op jit(solution)/shard_map/all_to_all | solution.py:664
  8.5 0.0 copy-done
  8.5 0.0 copy-done.1
  8.5 0.2 halo_rows.1
  8.7 1.3 %collective-permute-start.3 = (f32[5,64,128]{2,1,0:T(8,128)S(1)}, f32[5,64,128]{2,1,0:T(8,128)S(1)}, u32[]{:S(2)}, u32[]{:S(2)}) collective-permute-start(f32[5,64,128]{2,1,0:T(8,128)S(1)} %get-tuple-element.61), channel_id=1, source_target_pairs={{1,0},{2,1},{3,2},{5,4},{6,5},{7,6},{9,8},{10,9},{11,10},{13,12},{... | collective-permute-start | bytes 491528 | tf_op jit(solution)/shard_map/ppermute | solution.py:683
  10.0 4.0 %collective-permute-start.2 = (f32[3,64,128]{2,1,0:T(8,128)S(1)}, f32[3,64,128]{2,1,0:T(8,128)S(1)}, u32[]{:S(2)}, u32[]{:S(2)}) collective-permute-start(f32[3,64,128]{2,1,0:T(8,128)S(1)} %get-tuple-element.60), channel_id=1, source_target_pairs={{0,1},{1,2},{2,3},{4,5},{5,6},{6,7},{8,9},{9,10},{10,11},{12,13},{... | collective-permute-start | bytes 294920 | tf_op jit(solution)/shard_map/ppermute | solution.py:682
  14.6 1.2 %all-to-all-done.2 = s32[32,8,128]{2,1,0:T(8,128)S(1)} async-done(((s32[32,8,128]{2,1,0:T(8,128)}), s32[32,8,128]{2,1,0:T(8,128)S(1)}, u32[]{:S(2)}, u32[]{:S(2)}) %all-to-all-start.2) | async-done | bytes 131104 | tf_op jit(solution)/shard_map/all_to_all | solution.py:664
  15.8 4.1 %balance.1 = (f32[16,128]{1,0:T(8,128)S(1)}, s32[8,128]{1,0:T(8,128)S(1)}, s32[1]{0:T(128)}) custom-call(s32[256,128]{1,0:T(8,128)S(1)} %bitcast.29), custom_call_target="tpu_custom_call" | custom-call | tf_op jit(solution)/shard_map/balance/pallas_call | solution.py:689
  19.9 0.0 collective-permute-done.2.low
  19.9 0.0 collective-permute-done.3.high
  19.9 0.0 copy-done.3
  19.9 0.0 copy-done.5
  19.9 8.8 %rows.1 = (f32[1024,128]{1,0:T(8,128)S(1)}, f32[64,128]{1,0:T(8,128)S(1)}, f32[128,8,128]{2,1,0:T(8,128)}) custom-call(s32[1,3]{1,0:T(1,128)S(1)} %copy-done.5, f32[4]{0:T(128)S(1)} %copy-done.3, s32[1]{0:T(128)S(6)} %copy.16.sign_in, s32[8,128]{1,0:T(8,128)S(1)} %get-tuple-element.63.info_in, f32[16,8192]{1,0:T(8,128)S(1)} %bitcast.23, ...), custom_call_target="tpu_custom_call" | custom-call | tf_op jit(solution)/shard_map/rows/pallas_call | solution.py:721
  28.7 4.3 %all-to-all-start.3 = ((f32[32,32,128]{2,1,0:T(8,128)}), f32[32,32,128]{2,1,0:T(8,128)S(1)}, u32[]{:S(2)}, u32[]{:S(2)}) async-start(f32[32,32,128]{2,1,0:T(8,128)} %bitcast.13), calls=%async_computation.3 | async-start | bytes 1048576 | tf_op jit(solution)/shard_map/all_to_all | solution.py:772
  33.0 0.9 %piece_table.3.table = s32[8,128]{1,0:T(8,128)S(1)} custom-call(s32[256,128]{1,0:T(8,128)S(1)} %bitcast.30, f32[16,128]{1,0:T(8,128)S(1)} %get-tuple-element.57.refs_1_), custom_call_target="tpu_custom_call" | custom-call | tf_op jit(solution)/shard_map/piece_table/pallas_call | solution.py:791
  33.9 1.5 %sum_own.3.pieces_in = f32[264,8,128]{2,1,0:T(8,128)S(1)} custom-call(s32[8,128]{1,0:T(8,128)S(1)} %piece_table.3.table, f32[128,8,128]{2,1,0:T(8,128)S(1)} %bitcast.28), custom_call_target="tpu_custom_call" | custom-call | tf_op jit(solution)/shard_map/sum_own/pallas_call | solution.py:808
  35.4 12.9 %all-to-all-done.3 = f32[32,32,128]{2,1,0:T(8,128)S(1)} async-done(((f32[32,32,128]{2,1,0:T(8,128)}), f32[32,32,128]{2,1,0:T(8,128)S(1)}, u32[]{:S(2)}, u32[]{:S(2)}) %all-to-all-start.3) | async-done | bytes 524320 | tf_op jit(solution)/shard_map/all_to_all | solution.py:772
  48.3 2.0 %sum_arrived.3 = (f32[128,8,128]{2,1,0:T(8,128)}, f32[264,8,128]{2,1,0:T(8,128)S(1)}) custom-call(s32[8,128]{1,0:T(8,128)S(1)} %piece_table.3.table, f32[128,8,128]{2,1,0:T(8,128)S(1)} %bitcast.21, f32[264,8,128]{2,1,0:T(8,128)S(1)} %sum_own.3.pieces_in), custom_call_target="tpu_custom_call", output_to_operand_aliasing={{1}: (2, {})} | custom-call | tf_op jit(solution)/shard_map/sum_arrived/pallas_call | solution.py:816
  50.3 3.1 %all-to-all-start.4 = ((f32[32,32,128]{2,1,0:T(8,128)}), f32[32,32,128]{2,1,0:T(8,128)S(1)}, u32[]{:S(2)}, u32[]{:S(2)}) async-start(f32[32,32,128]{2,1,0:T(8,128)} %bitcast.16), calls=%async_computation.4 | async-start | bytes 1048576 | tf_op jit(solution)/shard_map/all_to_all | solution.py:772
  54.1 0.7 own_back.3
  54.8 13.9 %all-to-all-done.4 = f32[32,32,128]{2,1,0:T(8,128)S(1)} async-done(((f32[32,32,128]{2,1,0:T(8,128)}), f32[32,32,128]{2,1,0:T(8,128)S(1)}, u32[]{:S(2)}, u32[]{:S(2)}) %all-to-all-start.4) | async-done | bytes 524320 | tf_op jit(solution)/shard_map/all_to_all | solution.py:772
  68.7 1.2 %conditional.1 = (f32[1,16,8192]{2,1,0:T(8,128)S(1)}) conditional(s32[]{:T(128)} %bitcast.12, (s32[256,128]{1,0:T(8,128)S(1)}, f32[16,128]{1,0:T(8,128)S(1)}, f32[64,128]{1,0:T(8,128)S(1)}, s32[1,3]{1,0:T(1,128)S(1)}, f32[1024,128]{1,0:T(8,128)S(1)}, /*index=5*/s32[8,128]{1,0:T(8,128)S(1)}) %tuple.25, (f32[32,32,128]{2,1,0:T(8,128)S(1)}, ...), branch_computations={%region_0.0_spmd, %region_1.0_spmd} | conditional | flops 8192 | bytes 10846388 | solution.py:852
  68.7 1.2 %unpack.3 = f32[16,8192]{1,0:T(8,128)S(1)} custom-call(s32[8,128]{1,0:T(8,128)S(1)} %get-tuple-element.36.info, f32[128,8,128]{2,1,0:T(8,128)S(1)} %bitcast.27, f32[128,8,128]{2,1,0:T(8,128)S(1)} %get-tuple-element.38.own), custom_call_target="tpu_custom_call" | custom-call | tf_op jit(solution)/shard_map/cond/branch_1_fun/unpack/pallas_call | solution.py:836
  69.9 0.0 copy-start.4
  69.9 0.8 %copy-done.4 = f32[1,16,8192]{2,1,0:T(8,128)} copy-done((f32[1,16,8192]{2,1,0:T(8,128)}, f32[1,16,8192]{2,1,0:T(8,128)S(1)}, u32[]{:S(2)}) %copy-start.4) | copy-done | bytes 524312
Async XLA Ops:
  0.7 7.8 %copy-start = (f32[1,16,8192]{2,1,0:T(8,128)S(1)}, f32[1,16,8192]{2,1,0:T(8,128)}, u32[]{:S(2)}) copy-start(f32[1,16,8192]{2,1,0:T(8,128)} %param.9) | copy-start | bytes 1572868
  0.7 7.8 %copy-start.1 = (f32[1,16,8192]{2,1,0:T(8,128)S(1)}, f32[1,16,8192]{2,1,0:T(8,128)}, u32[]{:S(2)}) copy-start(f32[1,16,8192]{2,1,0:T(8,128)} %param.10) | copy-start | bytes 1572868
  1.3 18.5 %copy-start.3 = (f32[4]{0:T(128)S(1)}, f32[4]{0:T(128)}, u32[]{:S(2)}) copy-start(f32[4]{0:T(128)} %velocity.1) | copy-start | bytes 52
  1.3 18.5 %copy-start.5 = (s32[1,3]{1,0:T(1,128)S(1)}, s32[1,3]{1,0:T(1,128)}, u32[]{:S(2)}) copy-start(s32[1,3]{1,0:T(1,128)} %levels.1) | copy-start | bytes 40
  1.3 14.4 %all-to-all-start.2 = ((s32[32,8,128]{2,1,0:T(8,128)}), s32[32,8,128]{2,1,0:T(8,128)S(1)}, u32[]{:S(2)}, u32[]{:S(2)}) async-start(s32[32,8,128]{2,1,0:T(8,128)} %bitcast.10), calls=%async_computation.2 | async-start | bytes 262144 | tf_op jit(solution)/shard_map/all_to_all | solution.py:664
  8.7 11.2 %collective-permute-start.3 = (f32[5,64,128]{2,1,0:T(8,128)S(1)}, f32[5,64,128]{2,1,0:T(8,128)S(1)}, u32[]{:S(2)}, u32[]{:S(2)}) collective-permute-start(f32[5,64,128]{2,1,0:T(8,128)S(1)} %get-tuple-element.61), channel_id=1, source_target_pairs={{1,0},{2,1},{3,2},{5,4},{6,5},{7,6},{9,8},{10,9},{11,10},{13,12},{... | collective-permute-start | bytes 491528 | tf_op jit(solution)/shard_map/ppermute | solution.py:683
  10.0 9.9 %collective-permute-start.2 = (f32[3,64,128]{2,1,0:T(8,128)S(1)}, f32[3,64,128]{2,1,0:T(8,128)S(1)}, u32[]{:S(2)}, u32[]{:S(2)}) collective-permute-start(f32[3,64,128]{2,1,0:T(8,128)S(1)} %get-tuple-element.60), channel_id=1, source_target_pairs={{0,1},{1,2},{2,3},{4,5},{5,6},{6,7},{8,9},{9,10},{10,11},{12,13},{... | collective-permute-start | bytes 294920 | tf_op jit(solution)/shard_map/ppermute | solution.py:682
  28.7 19.6 %all-to-all-start.3 = ((f32[32,32,128]{2,1,0:T(8,128)}), f32[32,32,128]{2,1,0:T(8,128)S(1)}, u32[]{:S(2)}, u32[]{:S(2)}) async-start(f32[32,32,128]{2,1,0:T(8,128)} %bitcast.13), calls=%async_computation.3 | async-start | bytes 1048576 | tf_op jit(solution)/shard_map/all_to_all | solution.py:772
  50.3 18.4 %all-to-all-start.4 = ((f32[32,32,128]{2,1,0:T(8,128)}), f32[32,32,128]{2,1,0:T(8,128)S(1)}, u32[]{:S(2)}, u32[]{:S(2)}) async-start(f32[32,32,128]{2,1,0:T(8,128)} %bitcast.16), calls=%async_computation.4 | async-start | bytes 1048576 | tf_op jit(solution)/shard_map/all_to_all | solution.py:772
  69.9 0.8 %copy-start.4 = (f32[1,16,8192]{2,1,0:T(8,128)}, f32[1,16,8192]{2,1,0:T(8,128)S(1)}, u32[]{:S(2)}) copy-start(f32[1,16,8192]{2,1,0:T(8,128)S(1)} %get-tuple-element.85) | copy-start | bytes 1572868

commit v8 on v7

--- a/solution.py
+++ b/solution.py
@@ -81,13 +81,13 @@
         return up_here, down_here, jnp.zeros((24, LANES), jnp.float32)
 
     def several(k, carry):
-        for i in range(4):
-            carry = one_tile(4 * k + i, carry)
+        for i in range(8):
+            carry = one_tile(8 * k + i, carry)
         return carry
 
     lax.fori_loop(
         0,
-        TILES // 4,
+        TILES // 8,
         several,
         (src[PAD], start(stride_two, lane_two), start(stride_three, lane_three)),
     )
@@ -120,6 +120,16 @@
     return jnp.concatenate([own, nxt], axis=0)
 
 
+def exact_dot(left, right):
+    total = None
+    for _ in range(3):
+        part = left.astype(jnp.bfloat16)
+        term = jnp.dot(part, right, preferred_element_type=jnp.float32)
+        total = term if total is None else total + term
+        left = left - part.astype(jnp.float32)
+    return total
+
+
 def surplus_rows(levels, factor, x, y, matrix, stage):
     rows = x.shape[1]
     x[TILES] = jnp.zeros((rows, LANES), jnp.float32)
@@ -129,6 +139,7 @@
     _, end_six = bit_ends(levels, 6)
     mask_six = (1 << (jnp.maximum(end_six, 7) - 7)) - 1
     chunk = 16
+    matrix = matrix.astype(jnp.bfloat16)
     for j0 in range(0, TILES, chunk):
         own = x[pl.ds(j0, chunk)].reshape(chunk * rows, LANES)
         nxt = jnp.concatenate(
@@ -138,12 +149,7 @@
             ],
             axis=0,
         )
-        res = jnp.dot(
-            jnp.concatenate([own, nxt], axis=1),
-            matrix,
-            precision=lax.Precision.HIGHEST,
-            preferred_element_type=jnp.float32,
-        )
+        res = exact_dot(jnp.concatenate([own, nxt], axis=1), matrix)
         y[pl.ds(32 + j0, chunk)] = res.reshape(chunk, rows, LANES)
 
     lane = lax.broadcasted_iota(jnp.int32, (1, LANES), 1)

time: 71.2 us -> 69.8 us (0.980)
  Pallas kernels: 20 us -> 18.4 us
    pallas_call x1, Pallas kernels: 8.8 us -> 7.21 us  [body(): pl.pallas_call(functools.partial(rows_kernel, extras=extras), out_shape=(...]
  transfers between devices with their start and end apart: 5 -> 5, of which waited for: 3 -> 3; matrix products, arithmetic and copies ran while one was open for 0% -> 0% of each run, Pallas kernels for 10% -> 11%
where the time goes in v8:
time: 69.8 us; the launch traced here: 69.1 us
  waiting for transfers between devices  27.9 us (40%)
  starting transfers between devices  19.8 us (28%)
  Pallas kernels  18.4 us (26%)
  between operations  1.47 us (2%)
  local copies, waits for them, and re-layouts  0.8 us (1%)
    all_to_all x2, waiting for transfers between devices, exchange(): lax.all_to_all(x.reshape(devices, slots * 8, LANES), ('grid', 'dom'), spl...  26.8 us
    all_to_all x2, starting transfers between devices, exchange(): lax.all_to_all(x.reshape(devices, slots * 8, LANES), ('grid', 'dom'), spl...  7.45 us
    pallas_call x1, Pallas kernels, body(): pl.pallas_call(functools.partial(rows_kernel, extras=extras), out_shape=(...  7.21 us
    all_to_all x1, starting transfers between devices, body(): lax.all_to_all(spread.reshape(devices, COPIES, blocks), ('grid', 'dom'),...  7.1 us
    pallas_call x1, Pallas kernels, body(): pl.pallas_call(functools.partial(balance_kernel, devices=devices, capacit...  4.08 us
    ppermute x1, starting transfers between devices, body(): low = lax.ppermute(low_rows, 'dom', up)  3.99 us
    pallas_call x1, Pallas kernels, route(): pl.pallas_call(sum_kernel, out_shape=(f32(devices * slots, 8, LANES), all...  1.92 us
    pallas_call x1, Pallas kernels, route(): pl.pallas_call(functools.partial(own_sum_kernel, arrive_rows=arrive_rows,...  1.51 us
  transfers between devices with their start and end apart: 5, of which 3 were waited for; matrix products, arithmetic and copies ran while one was open for 0% of the time, Pallas kernels for 11%

profile of v8, /device:TPU:1, one launch (start us, length us, event | category | flops | bytes accessed | tf_op | source)
XLA Modules:
  0.0 69.1 jit_solution(15970235307727698785)
XLA Ops:
  0.0 0.7 multiply_add_fusion.keys
  0.7 0.0 copy-start
  0.7 0.0 copy-start.1
  0.7 0.7 spread_keys.1
  1.3 0.0 copy-start.3
  1.3 0.0 copy-start.5
  1.3 7.1 %all-to-all-start.2 = ((s32[32,8,128]{2,1,0:T(8,128)}), s32[32,8,128]{2,1,0:T(8,128)S(1)}, u32[]{:S(2)}, u32[]{:S(2)}) async-start(s32[32,8,128]{2,1,0:T(8,128)} %bitcast.10), calls=%async_computation.2 | async-start | bytes 262144 | tf_op jit(solution)/shard_map/all_to_all | solution.py:670
  8.5 0.0 copy-done
  8.5 0.0 copy-done.1
  8.5 0.2 halo_rows.1
  8.7 1.3 %collective-permute-start.3 = (f32[5,64,128]{2,1,0:T(8,128)S(1)}, f32[5,64,128]{2,1,0:T(8,128)S(1)}, u32[]{:S(2)}, u32[]{:S(2)}) collective-permute-start(f32[5,64,128]{2,1,0:T(8,128)S(1)} %get-tuple-element.61), channel_id=1, source_target_pairs={{1,0},{2,1},{3,2},{5,4},{6,5},{7,6},{9,8},{10,9},{11,10},{13,12},{... | collective-permute-start | bytes 491528 | tf_op jit(solution)/shard_map/ppermute | solution.py:689
  10.0 4.0 %collective-permute-start.2 = (f32[3,64,128]{2,1,0:T(8,128)S(1)}, f32[3,64,128]{2,1,0:T(8,128)S(1)}, u32[]{:S(2)}, u32[]{:S(2)}) collective-permute-start(f32[3,64,128]{2,1,0:T(8,128)S(1)} %get-tuple-element.60), channel_id=1, source_target_pairs={{0,1},{1,2},{2,3},{4,5},{5,6},{6,7},{8,9},{9,10},{10,11},{12,13},{... | collective-permute-start | bytes 294920 | tf_op jit(solution)/shard_map/ppermute | solution.py:688
  14.6 1.2 %all-to-all-done.2 = s32[32,8,128]{2,1,0:T(8,128)S(1)} async-done(((s32[32,8,128]{2,1,0:T(8,128)}), s32[32,8,128]{2,1,0:T(8,128)S(1)}, u32[]{:S(2)}, u32[]{:S(2)}) %all-to-all-start.2) | async-done | bytes 131104 | tf_op jit(solution)/shard_map/all_to_all | solution.py:670
  15.8 4.1 %balance.1 = (f32[16,128]{1,0:T(8,128)S(1)}, s32[8,128]{1,0:T(8,128)S(1)}, s32[1]{0:T(128)}) custom-call(s32[256,128]{1,0:T(8,128)S(1)} %bitcast.29), custom_call_target="tpu_custom_call" | custom-call | tf_op jit(solution)/shard_map/balance/pallas_call | solution.py:695
  19.9 0.0 collective-permute-done.2.low
  19.9 0.0 collective-permute-done.3.high
  19.9 0.0 copy-done.3
  19.9 0.0 copy-done.5
  19.9 7.2 %rows.1 = (f32[1024,128]{1,0:T(8,128)S(1)}, f32[64,128]{1,0:T(8,128)S(1)}, f32[128,8,128]{2,1,0:T(8,128)}) custom-call(s32[1,3]{1,0:T(1,128)S(1)} %copy-done.5, f32[4]{0:T(128)S(1)} %copy-done.3, s32[1]{0:T(128)S(6)} %copy.16.sign_in, s32[8,128]{1,0:T(8,128)S(1)} %get-tuple-element.63.info_in, f32[16,8192]{1,0:T(8,128)S(1)} %bitcast.23, ...), custom_call_target="tpu_custom_call" | custom-call | tf_op jit(solution)/shard_map/rows/pallas_call | solution.py:727
  27.1 4.3 %all-to-all-start.3 = ((f32[32,32,128]{2,1,0:T(8,128)}), f32[32,32,128]{2,1,0:T(8,128)S(1)}, u32[]{:S(2)}, u32[]{:S(2)}) async-start(f32[32,32,128]{2,1,0:T(8,128)} %bitcast.13), calls=%async_computation.3 | async-start | bytes 1048576 | tf_op jit(solution)/shard_map/all_to_all | solution.py:778
  31.4 0.9 %piece_table.3.table = s32[8,128]{1,0:T(8,128)S(1)} custom-call(s32[256,128]{1,0:T(8,128)S(1)} %bitcast.30, f32[16,128]{1,0:T(8,128)S(1)} %get-tuple-element.57.refs_1_), custom_call_target="tpu_custom_call" | custom-call | tf_op jit(solution)/shard_map/piece_table/pallas_call | solution.py:797
  32.3 1.5 %sum_own.3.pieces_in = f32[264,8,128]{2,1,0:T(8,128)S(1)} custom-call(s32[8,128]{1,0:T(8,128)S(1)} %piece_table.3.table, f32[128,8,128]{2,1,0:T(8,128)S(1)} %bitcast.28), custom_call_target="tpu_custom_call" | custom-call | tf_op jit(solution)/shard_map/sum_own/pallas_call | solution.py:814
  33.8 12.9 %all-to-all-done.3 = f32[32,32,128]{2,1,0:T(8,128)S(1)} async-done(((f32[32,32,128]{2,1,0:T(8,128)}), f32[32,32,128]{2,1,0:T(8,128)S(1)}, u32[]{:S(2)}, u32[]{:S(2)}) %all-to-all-start.3) | async-done | bytes 524320 | tf_op jit(solution)/shard_map/all_to_all | solution.py:778
  46.7 1.9 %sum_arrived.3 = (f32[128,8,128]{2,1,0:T(8,128)}, f32[264,8,128]{2,1,0:T(8,128)S(1)}) custom-call(s32[8,128]{1,0:T(8,128)S(1)} %piece_table.3.table, f32[128,8,128]{2,1,0:T(8,128)S(1)} %bitcast.21, f32[264,8,128]{2,1,0:T(8,128)S(1)} %sum_own.3.pieces_in), custom_call_target="tpu_custom_call", output_to_operand_aliasing={{1}: (2, {})} | custom-call | tf_op jit(solution)/shard_map/sum_arrived/pallas_call | solution.py:822
  48.6 3.2 %all-to-all-start.4 = ((f32[32,32,128]{2,1,0:T(8,128)}), f32[32,32,128]{2,1,0:T(8,128)S(1)}, u32[]{:S(2)}, u32[]{:S(2)}) async-start(f32[32,32,128]{2,1,0:T(8,128)} %bitcast.16), calls=%async_computation.4 | async-start | bytes 1048576 | tf_op jit(solution)/shard_map/all_to_all | solution.py:778
  52.5 0.7 %own_back.3 = f32[128,8,128]{2,1,0:T(8,128)S(1)} custom-call(s32[8,128]{1,0:T(8,128)S(1)} %piece_table.3.table, f32[264,8,128]{2,1,0:T(8,128)S(1)} %get-tuple-element.70.pieces), custom_call_target="tpu_custom_call" | custom-call | tf_op jit(solution)/shard_map/own_back/pallas_call | solution.py:831
  53.2 13.9 %all-to-all-done.4 = f32[32,32,128]{2,1,0:T(8,128)S(1)} async-done(((f32[32,32,128]{2,1,0:T(8,128)}), f32[32,32,128]{2,1,0:T(8,128)S(1)}, u32[]{:S(2)}, u32[]{:S(2)}) %all-to-all-start.4) | async-done | bytes 524320 | tf_op jit(solution)/shard_map/all_to_all | solution.py:778
  67.1 1.2 %conditional.1 = (f32[1,16,8192]{2,1,0:T(8,128)S(1)}) conditional(s32[]{:T(128)} %bitcast.12, (s32[256,128]{1,0:T(8,128)S(1)}, f32[16,128]{1,0:T(8,128)S(1)}, f32[64,128]{1,0:T(8,128)S(1)}, s32[1,3]{1,0:T(1,128)S(1)}, f32[1024,128]{1,0:T(8,128)S(1)}, /*index=5*/s32[8,128]{1,0:T(8,128)S(1)}) %tuple.25, (f32[32,32,128]{2,1,0:T(8,128)S(1)}, ...), branch_computations={%region_0.0_spmd, %region_1.0_spmd} | conditional | flops 8192 | bytes 10846388 | solution.py:858
  67.1 1.2 %unpack.3 = f32[16,8192]{1,0:T(8,128)S(1)} custom-call(s32[8,128]{1,0:T(8,128)S(1)} %get-tuple-element.36.info, f32[128,8,128]{2,1,0:T(8,128)S(1)} %bitcast.27, f32[128,8,128]{2,1,0:T(8,128)S(1)} %get-tuple-element.38.own), custom_call_target="tpu_custom_call" | custom-call | tf_op jit(solution)/shard_map/cond/branch_1_fun/unpack/pallas_call | solution.py:842
  68.3 0.0 copy-start.4
  68.3 0.8 %copy-done.4 = f32[1,16,8192]{2,1,0:T(8,128)} copy-done((f32[1,16,8192]{2,1,0:T(8,128)}, f32[1,16,8192]{2,1,0:T(8,128)S(1)}, u32[]{:S(2)}) %copy-start.4) | copy-done | bytes 524312
Async XLA Ops:
  0.7 7.8 %copy-start = (f32[1,16,8192]{2,1,0:T(8,128)S(1)}, f32[1,16,8192]{2,1,0:T(8,128)}, u32[]{:S(2)}) copy-start(f32[1,16,8192]{2,1,0:T(8,128)} %param.9) | copy-start | bytes 1572868
  0.7 7.8 %copy-start.1 = (f32[1,16,8192]{2,1,0:T(8,128)S(1)}, f32[1,16,8192]{2,1,0:T(8,128)}, u32[]{:S(2)}) copy-start(f32[1,16,8192]{2,1,0:T(8,128)} %param.10) | copy-start | bytes 1572868
  1.3 18.5 %copy-start.3 = (f32[4]{0:T(128)S(1)}, f32[4]{0:T(128)}, u32[]{:S(2)}) copy-start(f32[4]{0:T(128)} %velocity.1) | copy-start | bytes 52
  1.3 18.5 %copy-start.5 = (s32[1,3]{1,0:T(1,128)S(1)}, s32[1,3]{1,0:T(1,128)}, u32[]{:S(2)}) copy-start(s32[1,3]{1,0:T(1,128)} %levels.1) | copy-start | bytes 40
  1.3 14.4 %all-to-all-start.2 = ((s32[32,8,128]{2,1,0:T(8,128)}), s32[32,8,128]{2,1,0:T(8,128)S(1)}, u32[]{:S(2)}, u32[]{:S(2)}) async-start(s32[32,8,128]{2,1,0:T(8,128)} %bitcast.10), calls=%async_computation.2 | async-start | bytes 262144 | tf_op jit(solution)/shard_map/all_to_all | solution.py:670
  8.7 11.2 %collective-permute-start.3 = (f32[5,64,128]{2,1,0:T(8,128)S(1)}, f32[5,64,128]{2,1,0:T(8,128)S(1)}, u32[]{:S(2)}, u32[]{:S(2)}) collective-permute-start(f32[5,64,128]{2,1,0:T(8,128)S(1)} %get-tuple-element.61), channel_id=1, source_target_pairs={{1,0},{2,1},{3,2},{5,4},{6,5},{7,6},{9,8},{10,9},{11,10},{13,12},{... | collective-permute-start | bytes 491528 | tf_op jit(solution)/shard_map/ppermute | solution.py:689
  10.0 9.9 %collective-permute-start.2 = (f32[3,64,128]{2,1,0:T(8,128)S(1)}, f32[3,64,128]{2,1,0:T(8,128)S(1)}, u32[]{:S(2)}, u32[]{:S(2)}) collective-permute-start(f32[3,64,128]{2,1,0:T(8,128)S(1)} %get-tuple-element.60), channel_id=1, source_target_pairs={{0,1},{1,2},{2,3},{4,5},{5,6},{6,7},{8,9},{9,10},{10,11},{12,13},{... | collective-permute-start | bytes 294920 | tf_op jit(solution)/shard_map/ppermute | solution.py:688
  27.1 19.6 %all-to-all-start.3 = ((f32[32,32,128]{2,1,0:T(8,128)}), f32[32,32,128]{2,1,0:T(8,128)S(1)}, u32[]{:S(2)}, u32[]{:S(2)}) async-start(f32[32,32,128]{2,1,0:T(8,128)} %bitcast.13), calls=%async_computation.3 | async-start | bytes 1048576 | tf_op jit(solution)/shard_map/all_to_all | solution.py:778
  48.6 18.5 %all-to-all-start.4 = ((f32[32,32,128]{2,1,0:T(8,128)}), f32[32,32,128]{2,1,0:T(8,128)S(1)}, u32[]{:S(2)}, u32[]{:S(2)}) async-start(f32[32,32,128]{2,1,0:T(8,128)} %bitcast.16), calls=%async_computation.4 | async-start | bytes 1048576 | tf_op jit(solution)/shard_map/all_to_all | solution.py:778
  68.3 0.8 %copy-start.4 = (f32[1,16,8192]{2,1,0:T(8,128)}, f32[1,16,8192]{2,1,0:T(8,128)S(1)}, u32[]{:S(2)}) copy-start(f32[1,16,8192]{2,1,0:T(8,128)S(1)} %get-tuple-element.85) | copy-start | bytes 1572868

commit v9 on v8

--- a/solution.py
+++ b/solution.py
@@ -13,6 +13,7 @@
 LANES = 128
 TILES = 2**LR // LANES
 PAD = 9
+BESIDE = 4
 COPIES = 8
 MOST_KEYS = 256
 VMEM_LIMIT = 48 * 1024 * 1024
@@ -28,7 +29,9 @@
 SM = pl.BlockSpec(memory_space=pltpu.SMEM)
 
 
-def grid_step(first_bits, second_bits, weights, valid, src, dst, dif, lane_two, lane_three):
+def grid_step(
+    first_bits, second_bits, weights, valid, src, dst, dif, lane_two, lane_three, beside, state
+):
     lane = lax.broadcasted_iota(jnp.int32, (1, LANES), 1)
     first_mask = (1 << first_bits) - 1
     stride_two = 1 << first_bits
@@ -80,17 +83,19 @@
         up_here, down_here = rolled(src[PAD], stride)
         return up_here, down_here, jnp.zeros((24, LANES), jnp.float32)
 
+    turns = BESIDE if beside is not None else 8
+    tiles = TILES // turns
+
     def several(k, carry):
-        for i in range(8):
-            carry = one_tile(8 * k + i, carry)
-        return carry
-
-    lax.fori_loop(
-        0,
-        TILES // 8,
-        several,
-        (src[PAD], start(stride_two, lane_two), start(stride_three, lane_three)),
-    )
+        tile_carry, state = carry
+        if beside is not None:
+            state = beside(k, state)
+        for i in range(tiles):
+            tile_carry = one_tile(tiles * k + i, tile_carry)
+        return tile_carry, state
+
+    first = (src[PAD], start(stride_two, lane_two), start(stride_three, lane_three))
+    return lax.fori_loop(0, turns, several, (first, state))[1]
 
 
 def bit_ends(levels, q):
@@ -172,31 +177,25 @@
             stage[pl.ds(j + i * TILES, 8, stride=TILES), :] = tile[i : i + 8]
 
 
-def rows_kernel(
-    levels,
-    velocity,
-    sign_in,
-    info_in,
-    conc,
-    dif_in,
-    low,
-    high,
-    out,
-    lead,
-    outgoing,
-    u_a,
-    u_b,
-    dif,
-    x,
-    y,
-    info,
-    sign,
-    sems,
-    *,
-    extras,
-):
+def rows_kernel(*refs, extras, balance):
+    levels, velocity, sign_in, keys, conc, dif_in, low, high, *refs = refs
+    if balance is not None:
+        two, table_in, loads_in, *refs = refs
+    out, lead, outgoing, *refs = refs
+    balancing = None
+    if balance is None:
+        info_in = keys
+    else:
+        assigned, info_in, good_out, *refs = refs
+    u_a, u_b, dif, x, y, info, sign, sems, *refs = refs
     places = pltpu.make_async_copy(info_in, info, sems.at[0])
-    places.start()
+    if balance is None:
+        places.start()
+    else:
+        table, loads, good = refs
+        table[...] = table_in[...]
+        balancing = Balancing(keys, None, two, table, **balance)
+        tell = pltpu.make_async_copy(good, good_out, sems.at[2])
     signs = pltpu.make_async_copy(sign_in, sign, sems.at[1])
     signs.start()
     place = lax.axis_index("dom")
@@ -225,11 +224,28 @@
     second_bits = levels[0, 1]
 
     def both(lane_two, lane_three):
+        def step(src, dst, beside, state):
+            return grid_step(
+                first_bits,
+                second_bits,
+                weights,
+                valid,
+                src,
+                dst,
+                dif,
+                lane_two,
+                lane_three,
+                beside,
+                state,
+            )
+
         def run():
-            for src, dst in ((u_a, u_b), (u_b, u_a)):
-                grid_step(
-                    first_bits, second_bits, weights, valid, src, dst, dif, lane_two, lane_three
-                )
+            if balancing is None:
+                step(u_a, u_b, None, 0)
+                step(u_b, u_a, None, 0)
+            else:
+                load = step(u_a, u_b, balancing.later_round, loads_in[...])
+                loads[...] = step(u_b, u_a, balancing.later_round, load)
 
         return run
 
@@ -238,6 +254,9 @@
     pl.when(small_three)(both(True, True))
     pl.when(small_two & jnp.logical_not(small_three))(both(True, False))
     pl.when(jnp.logical_not(small_two))(both(False, False))
+    if balancing is not None:
+        balancing.finish(loads[...], assigned, info_in, good, tell)
+        places.start()
     signs.wait()
     factor = sign[0].astype(jnp.float32)
     lead[...] = factor * u_a[PAD : PAD + TILES, 0]
@@ -254,6 +273,8 @@
     surplus_rows(levels, factor, x, y, lane_matrix(levels), out)
     places.wait()
     send_blocks(info, lambda b: out[8 * b : 8 * b + 8, :], outgoing, extras)
+    if balancing is not None:
+        tell.wait()
 
 
 def send_blocks(info, block, outgoing, extras):
@@ -400,9 +421,7 @@
     write_places(info, owner, none, jnp.int32(0), me, devices, capacity)
 
 
-def balance_kernel(
-    keys, assigned, info, good_out, one, two, table, good, good_sem, *, devices, capacity, full
-):
+def first_rounds_kernel(keys, two, table, loads, one, *, devices, capacity, full):
     rows = devices * SLOTS // LANES
     deep = devices + 8
     keys_all = all_keys(keys)
@@ -428,16 +447,35 @@
         spare = pl.ds(r * deep + devices, deep - devices)
         one[spare, :] = jnp.ones((deep - devices, LANES), jnp.float32)
         two[spare, :] = jnp.ones((deep - devices, LANES), jnp.float32)
-
-    square = (devices, deep)
-    sender = lax.broadcasted_iota(jnp.int32, square, 1)
-    own = (lax.broadcasted_iota(jnp.int32, square, 0) == sender) | (sender >= devices)
-
-    def price(load, steep):
-        value = jnp.exp2(load * 0.3785) + steep * jnp.maximum(load - (capacity - 1), 0.0)
-        return jnp.where(own, 0.0, value)
-
-    def settle(counts_ref, group, first, load, number):
+    balancing = Balancing(
+        keys, one, two, table, devices=devices, capacity=capacity, full=full
+    )
+    loads[...] = lax.fori_loop(0, BESIDE, balancing.first_round, balancing.no_load())
+    balancing.rearrange()
+
+
+class Balancing:
+    def __init__(self, keys, one, two, table, *, devices, capacity, full):
+        self.keys, self.one, self.two, self.table = keys, one, two, table
+        self.devices, self.capacity, self.full = devices, capacity, full
+        self.rows = devices * SLOTS // LANES
+        self.deep = devices + 8
+
+    def own(self):
+        square = (self.devices, self.deep)
+        sender = lax.broadcasted_iota(jnp.int32, square, 1)
+        own = lax.broadcasted_iota(jnp.int32, square, 0) == sender
+        return own | (sender >= self.devices), sender
+
+    def no_load(self):
+        return jnp.zeros((self.devices, self.deep), jnp.float32)
+
+    def price(self, load, steep):
+        value = jnp.exp2(load * 0.3785) + steep * jnp.maximum(load - (self.capacity - 1), 0.0)
+        return jnp.where(self.own()[0], 0.0, value)
+
+    def settle(self, counts_ref, group, first, load, number):
+        devices, deep, table = self.devices, self.deep, self.table
         base = number * group
         counts = jnp.concatenate(
             [
@@ -450,12 +488,12 @@
         handler = lax.broadcasted_iota(jnp.int32, shape, 0)
         column = lax.broadcasted_iota(jnp.int32, shape, 1)
         handler_f = handler.astype(jnp.float32)
-        cost = dot_plain(price(load, 4.0 if first else 16.0), counts)
+        cost = dot_plain(self.price(load, 4.0 if first else 16.0), counts)
         was = None
         if not first:
             old = jnp.concatenate([table[pl.ds(base + i, 1), :] for i in range(group)], axis=1)
             was = handler_f == old
-            cost = jnp.where(was, dot_plain(price(load - 1.0, 16.0), counts) - 5.0, cost)
+            cost = jnp.where(was, dot_plain(self.price(load - 1.0, 16.0), counts) - 5.0, cost)
         noise = 0.5 * mixed(handler, column % LANES, base + column // LANES)
         ranked = jnp.floor((jnp.minimum(cost, 4000.0) + noise) * 64.0) * devices + handler_f
         least = jnp.min(ranked, axis=0, keepdims=True)
@@ -467,61 +505,68 @@
             change = change - jnp.where(was, 1.0, 0.0)
         return load + dot_rows(change, counts)
 
-    def sweep(counts_ref, group, first, load):
-        return lax.fori_loop(
-            0, rows // group, lambda i, x: settle(counts_ref, group, first, x, i), load
+    def first_round(self, number, load):
+        return self.settle(self.one, self.rows // BESIDE, True, load, number)
+
+    def later_round(self, number, load):
+        return self.settle(self.two, self.rows // BESIDE, False, load, number)
+
+    def from_row(self):
+        spot = lax.broadcasted_iota(jnp.int32, (self.rows, LANES), 0)
+        lane = lax.broadcasted_iota(jnp.int32, (self.rows, LANES), 1)
+        return (spot + self.rows - (lane % SLOTS) % self.rows) % self.rows, lane
+
+    def rearrange(self):
+        from_row, _ = self.from_row()
+        moved = jnp.zeros((self.rows, LANES), jnp.float32)
+        for r in range(self.rows):
+            moved = jnp.where(from_row == r, self.table[r : r + 1, :], moved)
+        self.table[...] = moved
+
+    def finish(self, load, assigned, info, good, tell):
+        devices, capacity, rows, keys = self.devices, self.capacity, self.rows, self.keys
+        own, sender = self.own()
+
+        def sweep(group, load):
+            return lax.fori_loop(
+                0, rows // group, lambda i, x: self.settle(self.two, group, False, x, i), load
+            )
+
+        def worst(load):
+            return jnp.max(jnp.where(own, 0.0, load))
+
+        def again(state):
+            count, _, load = state
+            load = lax.cond(count == 0, lambda x: sweep(4, x), lambda x: sweep(2, x), load)
+            return count + 1, worst(load), load
+
+        _, most, load = lax.while_loop(
+            lambda state: (state[0] < 6) & (state[1] > capacity), again, (0, worst(load), load)
         )
-
-    def worst(load):
-        return jnp.max(jnp.where(own, 0.0, load))
-
-    load = sweep(one, 4, True, jnp.zeros(square, jnp.float32))
-    spot = lax.broadcasted_iota(jnp.int32, (rows, LANES), 0)
-    lane = lax.broadcasted_iota(jnp.int32, (rows, LANES), 1)
-    from_row = (spot + rows - (lane % SLOTS) % rows) % rows
-    moved = jnp.zeros((rows, LANES), jnp.float32)
-    for r in range(rows):
-        moved = jnp.where(from_row == r, table[r : r + 1, :], moved)
-    table[...] = moved
-    load = sweep(two, 4, False, load)
-
-    def again(state):
-        count, _, load = state
-        load = lax.cond(
-            count == 0,
-            lambda x: sweep(two, 4, False, x),
-            lambda x: sweep(two, 2, False, x),
-            load,
-        )
-        return count + 1, worst(load), load
-
-    _, most, load = lax.while_loop(
-        lambda state: (state[0] < 6) & (state[1] > capacity), again, (0, worst(load), load)
-    )
-    ok = (most <= capacity) & (jnp.max(jnp.where(sender < devices, 0.0, load)) <= MOST_KEYS)
-    good[0] = ok.astype(jnp.int32)
-    tell = pltpu.make_async_copy(good, good_out, good_sem)
-    tell.start()
-    owner = (from_row + rows * (lane // SLOTS)).astype(jnp.float32)
-    final = jnp.where(ok, table[...], owner)
-    assigned[...] = final
-    me = device_number()
-
-    def found(device):
-        _, _, lane_row, _, row = key_parts(keys_of(keys, device), rows)
-        return handlers_of(final, lane_row, row)
-
-    place = lax.axis_index("dom")
-    column = lax.broadcasted_iota(jnp.int32, (1, keys.shape[1]), 1)
-    extra = jnp.full((1, keys.shape[1]), -1.0, jnp.float32)
-    for t, (offset, period) in enumerate(row_zero_uses(dom_count)):
-        there = has_use(place, offset, period, dom_count)
-        moved = found(jnp.where(there, me + offset, me))
-        moved = pltpu.roll(moved, 8 * t, 1) if t else moved
-        extra = jnp.where((column >= 8 * t) & (column < 8 * t + 8) & there, moved, extra)
-    size = jnp.where(ok, capacity, full)
-    write_places(info, found(me), extra, ok.astype(jnp.int32), me, devices, size)
-    tell.wait()
+        ok = (most <= capacity) & (jnp.max(jnp.where(sender < devices, 0.0, load)) <= MOST_KEYS)
+        good[0] = ok.astype(jnp.int32)
+        tell.start()
+        from_row, lane = self.from_row()
+        owner = (from_row + rows * (lane // SLOTS)).astype(jnp.float32)
+        final = jnp.where(ok, self.table[...], owner)
+        assigned[...] = final
+        me = device_number()
+
+        def found(device):
+            _, _, lane_row, _, row = key_parts(keys_of(keys, device), rows)
+            return handlers_of(final, lane_row, row)
+
+        dom_count = lax.axis_size("dom")
+        place = lax.axis_index("dom")
+        column = lax.broadcasted_iota(jnp.int32, (1, keys.shape[1]), 1)
+        extra = jnp.full((1, keys.shape[1]), -1.0, jnp.float32)
+        for t, (offset, period) in enumerate(row_zero_uses(dom_count)):
+            there = has_use(place, offset, period, dom_count)
+            moved = found(jnp.where(there, me + offset, me))
+            moved = pltpu.roll(moved, 8 * t, 1) if t else moved
+            extra = jnp.where((column >= 8 * t) & (column < 8 * t + 8) & there, moved, extra)
+        size = jnp.where(ok, capacity, self.full)
+        write_places(info, found(me), extra, ok.astype(jnp.int32), me, devices, size)
 
 
 def flat_rows(devices, capacity):
@@ -690,26 +735,60 @@
 
     balanced = capacity >= 8 and devices * SLOTS % LANES == 0 and devices <= 64
     info_shape = jax.ShapeDtypeStruct((8, blocks), jnp.int32)
+    slots = capacity // 2 if balanced else capacity
+    extras = 8 * len(row_zero_uses(dom_count)) if balanced else 0
+    row_shapes = (f32(rows * TILES, LANES), f32(TILES, LANES), f32(devices * slots, 8, LANES))
+    row_scratch = [
+        pltpu.VMEM((TILES + 2 * PAD, 24, LANES), jnp.float32),
+        pltpu.VMEM((TILES + 2 * PAD, 24, LANES), jnp.float32),
+        pltpu.VMEM((TILES, 24, LANES), jnp.float32),
+        pltpu.VMEM((TILES + 1, 16, LANES), jnp.float32),
+        pltpu.VMEM((TILES + 64, 16, LANES), jnp.float32),
+        pltpu.SMEM((8, blocks), jnp.int32),
+        pltpu.SMEM((1,), jnp.int32),
+        pltpu.SemaphoreType.DMA((3,)),
+    ]
+    row_call = functools.partial(
+        pl.pallas_call,
+        in_specs=[SM, SM, HBM, VM, VM, VM, VM, VM] + [VM] * 3 * balanced,
+        compiler_params=params(),
+        name="rows",
+        cost_estimate=SMALL,
+    )
     if balanced:
         key_rows = devices * SLOTS // LANES
-        assigned, info, good = pl.pallas_call(
-            functools.partial(
-                balance_kernel, devices=devices, capacity=capacity // 2, full=capacity
+        balance = dict(devices=devices, capacity=slots, full=capacity)
+        begun = pl.pallas_call(
+            functools.partial(first_rounds_kernel, **balance),
+            out_shape=(
+                f32(key_rows * (devices + 8), LANES),
+                f32(key_rows, LANES),
+                f32(devices, devices + 8),
             ),
-            out_shape=(f32(key_rows, LANES), info_shape, jax.ShapeDtypeStruct((1,), jnp.int32)),
             in_specs=[VM],
-            out_specs=(VM, VM, HBM),
-            scratch_shapes=[
-                pltpu.VMEM((key_rows * (devices + 8), LANES), jnp.float32),
-                pltpu.VMEM((key_rows * (devices + 8), LANES), jnp.float32),
-                pltpu.VMEM((key_rows, LANES), jnp.float32),
-                pltpu.SMEM((1,), jnp.int32),
-                pltpu.SemaphoreType.DMA,
-            ],
+            out_specs=(VM, VM, VM),
+            scratch_shapes=[pltpu.VMEM((key_rows * (devices + 8), LANES), jnp.float32)],
             compiler_params=params(),
-            name="balance",
+            name="first_rounds",
             cost_estimate=SMALL,
         )(keys)
+        low, high, *begun = lax.optimization_barrier((low, high, *begun))
+        blocks_in, lead, outgoing, assigned, info, good = row_call(
+            functools.partial(
+                rows_kernel,
+                extras=extras,
+                balance=balance,
+            ),
+            out_shape=row_shapes
+            + (f32(key_rows, LANES), info_shape, jax.ShapeDtypeStruct((1,), jnp.int32)),
+            out_specs=(VM, VM, VM, VM, VM, HBM),
+            scratch_shapes=row_scratch
+            + [
+                pltpu.VMEM((key_rows, LANES), jnp.float32),
+                pltpu.VMEM((devices, devices + 8), jnp.float32),
+                pltpu.SMEM((1,), jnp.int32),
+            ],
+        )(levels, velocity, grid_signs, keys, conc, dif, low, high, *begun)
     else:
         info = pl.pallas_call(
             functools.partial(owner_places_kernel, devices=devices, capacity=capacity),
@@ -718,35 +797,13 @@
             out_specs=VM,
             compiler_params=params(),
             name="places",
-            cost_estimate=SMALL,
         )(keys)
-
-    low, high, info = lax.optimization_barrier((low, high, info))
-    slots = capacity // 2 if balanced else capacity
-    extras = 8 * len(row_zero_uses(dom_count)) if balanced else 0
-    blocks_in, lead, outgoing = pl.pallas_call(
-        functools.partial(rows_kernel, extras=extras),
-        out_shape=(
-            f32(rows * TILES, LANES),
-            f32(TILES, LANES),
-            f32(devices * slots, 8, LANES),
-        ),
-        in_specs=[SM, SM, HBM, VM, VM, VM, VM, VM],
-        out_specs=(VM, VM, VM),
-        scratch_shapes=[
-            pltpu.VMEM((TILES + 2 * PAD, 24, LANES), jnp.float32),
-            pltpu.VMEM((TILES + 2 * PAD, 24, LANES), jnp.float32),
-            pltpu.VMEM((TILES, 24, LANES), jnp.float32),
-            pltpu.VMEM((TILES + 1, 16, LANES), jnp.float32),
-            pltpu.VMEM((TILES + 64, 16, LANES), jnp.float32),
-            pltpu.SMEM((8, blocks), jnp.int32),
-            pltpu.SMEM((1,), jnp.int32),
-            pltpu.SemaphoreType.DMA((2,)),
-        ],
-        compiler_params=params(),
-        name="rows",
-        cost_estimate=SMALL,
-    )(levels, velocity, grid_signs, info, conc, dif, low, high)
+        blocks_in, lead, outgoing = row_call(
+            functools.partial(rows_kernel, extras=extras, balance=None),
+            out_shape=row_shapes,
+            out_specs=(VM, VM, VM),
+            scratch_shapes=row_scratch,
+        )(levels, velocity, grid_signs, info, conc, dif, low, high)
 
     def fixed():
         coarse = None

time: 69.8 us -> 70 us (level)
  Pallas kernels: 18.4 us -> 16.9 us
  starting transfers between devices: 19.8 us -> 21.1 us
    pallas_call x2, Pallas kernels: 11.3 us -> 9.9 us  [the longest x1 7.77 us: body(): row_call(functools.partial(rows_kernel, extras=extras, balance=balance),...]
    all_to_all x2, starting transfers between devices: 7.45 us -> 8.69 us  [exchange(): lax.all_to_all(x.reshape(devices, slots * 8, LANES), ('grid', 'dom'), spl...]
  transfers between devices with their start and end apart: 5 -> 5, of which waited for: 3 -> 3; matrix products, arithmetic and copies ran while one was open for 0% -> 0% of each run, Pallas kernels for 11% -> 8%
where the time goes in v9:
time: 70 us; the launch traced here: 68.9 us
  waiting for transfers between devices  28 us (40%)
  starting transfers between devices  21.1 us (30%)
  Pallas kernels  16.9 us (24%)
  between operations  1.47 us (2%)
  local copies, waits for them, and re-layouts  0.8 us (1%)
    all_to_all x2, waiting for transfers between devices, exchange(): lax.all_to_all(x.reshape(devices, slots * 8, LANES), ('grid', 'dom'), spl...  26.8 us
    all_to_all x2, starting transfers between devices, exchange(): lax.all_to_all(x.reshape(devices, slots * 8, LANES), ('grid', 'dom'), spl...  8.69 us
    pallas_call x1, Pallas kernels, body(): row_call(functools.partial(rows_kernel, extras=extras, balance=balance),...  7.77 us
    all_to_all x1, starting transfers between devices, body(): lax.all_to_all(spread.reshape(devices, COPIES, blocks), ('grid', 'dom'),...  7.1 us
    ppermute x1, starting transfers between devices, body(): low = lax.ppermute(low_rows, 'dom', up)  3.99 us
    pallas_call x1, Pallas kernels, body(): pl.pallas_call(functools.partial(first_rounds_kernel, **balance), out_sha...  2.13 us
    pallas_call x1, Pallas kernels, route(): pl.pallas_call(sum_kernel, out_shape=(f32(devices * slots, 8, LANES), all...  1.88 us
    pallas_call x1, Pallas kernels, route(): pl.pallas_call(functools.partial(own_sum_kernel, arrive_rows=arrive_rows,...  1.5 us
  transfers between devices with their start and end apart: 5, of which 3 were waited for; matrix products, arithmetic and copies ran while one was open for 0% of the time, Pallas kernels for 8%

profile of v9, /device:TPU:1, one launch (start us, length us, event | category | flops | bytes accessed | tf_op | source)
XLA Modules:
  0.0 68.9 jit_solution(7130266055504899805)
XLA Ops:
  0.0 0.7 multiply_add_fusion.keys
  0.7 0.0 copy-start
  0.7 0.0 copy-start.1
  0.7 0.7 spread_keys.1
  1.3 0.0 copy-start.3
  1.3 0.0 copy-start.5
  1.3 7.1 %all-to-all-start.2 = ((s32[32,8,128]{2,1,0:T(8,128)}), s32[32,8,128]{2,1,0:T(8,128)S(1)}, u32[]{:S(2)}, u32[]{:S(2)}) async-start(s32[32,8,128]{2,1,0:T(8,128)} %bitcast.10), calls=%async_computation.2 | async-start | bytes 262144 | tf_op jit(solution)/shard_map/all_to_all | solution.py:715
  8.5 0.0 copy-done
  8.5 0.0 copy-done.1
  8.5 0.2 halo_rows.1
  8.7 1.3 %collective-permute-start.3 = (f32[5,64,128]{2,1,0:T(8,128)S(1)}, f32[5,64,128]{2,1,0:T(8,128)S(1)}, u32[]{:S(2)}, u32[]{:S(2)}) collective-permute-start(f32[5,64,128]{2,1,0:T(8,128)S(1)} %get-tuple-element.64), channel_id=1, source_target_pairs={{1,0},{2,1},{3,2},{5,4},{6,5},{7,6},{9,8},{10,9},{11,10},{13,12},{... | collective-permute-start | bytes 491528 | tf_op jit(solution)/shard_map/ppermute | solution.py:734
  10.0 4.0 %collective-permute-start.2 = (f32[3,64,128]{2,1,0:T(8,128)S(1)}, f32[3,64,128]{2,1,0:T(8,128)S(1)}, u32[]{:S(2)}, u32[]{:S(2)}) collective-permute-start(f32[3,64,128]{2,1,0:T(8,128)S(1)} %get-tuple-element.63), channel_id=1, source_target_pairs={{0,1},{1,2},{2,3},{4,5},{5,6},{6,7},{8,9},{9,10},{10,11},{12,13},{... | collective-permute-start | bytes 294920 | tf_op jit(solution)/shard_map/ppermute | solution.py:733
  14.6 1.2 %all-to-all-done.2 = s32[32,8,128]{2,1,0:T(8,128)S(1)} async-done(((s32[32,8,128]{2,1,0:T(8,128)}), s32[32,8,128]{2,1,0:T(8,128)S(1)}, u32[]{:S(2)}, u32[]{:S(2)}) %all-to-all-start.2) | async-done | bytes 131104 | tf_op jit(solution)/shard_map/all_to_all | solution.py:715
  15.8 2.1 %first_rounds.1 = (f32[640,128]{1,0:T(8,128)S(1)}, f32[16,128]{1,0:T(8,128)S(1)}, f32[32,40]{1,0:T(8,128)S(1)}) custom-call(s32[256,128]{1,0:T(8,128)S(1)} %bitcast.27), custom_call_target="tpu_custom_call" | custom-call | tf_op jit(solution)/shard_map/first_rounds/pallas_call | solution.py:761
  17.9 0.0 collective-permute-done.2.refs_6_
  17.9 0.0 collective-permute-done.3.refs_7_
  17.9 0.0 copy-done.3
  17.9 0.0 copy-done.5
  18.0 7.8 %rows.1 = (f32[1024,128]{1,0:T(8,128)S(1)}, f32[64,128]{1,0:T(8,128)S(1)}, f32[128,8,128]{2,1,0:T(8,128)}, f32[16,128]{1,0:T(8,128)S(1)}, s32[8,128]{1,0:T(8,128)S(1)}, /*index=5*/s32[1]{0:T(128)}) custom-call(s32[1,3]{1,0:T(1,128)S(1)} %copy-done.5, f32[4]{0:T(128)S(1)} %copy-done.3, s32[1]{0:T(128)S(6)} %copy.16.refs_2_, s32[256,128]{1,0:T(8,128)S(1)} %bitcast.28, ...), custom_call_target="tpu_custom_call" | custom-call | tf_op jit(solution)/shard_map/rows/pallas_call | solution.py:776
  25.7 5.5 %all-to-all-start.3 = ((f32[32,32,128]{2,1,0:T(8,128)}), f32[32,32,128]{2,1,0:T(8,128)S(1)}, u32[]{:S(2)}, u32[]{:S(2)}) async-start(f32[32,32,128]{2,1,0:T(8,128)} %bitcast.13), calls=%async_computation.3 | async-start | bytes 1048576 | tf_op jit(solution)/shard_map/all_to_all | solution.py:835
  31.2 0.9 %piece_table.3.table = s32[8,128]{1,0:T(8,128)S(1)} custom-call(s32[256,128]{1,0:T(8,128)S(1)} %bitcast.29, f32[16,128]{1,0:T(8,128)S(1)} %get-tuple-element.74.refs_1_), custom_call_target="tpu_custom_call" | custom-call | tf_op jit(solution)/shard_map/piece_table/pallas_call | solution.py:854
  32.1 1.5 %sum_own.3.pieces_in = f32[264,8,128]{2,1,0:T(8,128)S(1)} custom-call(s32[8,128]{1,0:T(8,128)S(1)} %piece_table.3.table, f32[128,8,128]{2,1,0:T(8,128)S(1)} %bitcast.32), custom_call_target="tpu_custom_call" | custom-call | tf_op jit(solution)/shard_map/sum_own/pallas_call | solution.py:871
  33.6 12.9 %all-to-all-done.3 = f32[32,32,128]{2,1,0:T(8,128)S(1)} async-done(((f32[32,32,128]{2,1,0:T(8,128)}), f32[32,32,128]{2,1,0:T(8,128)S(1)}, u32[]{:S(2)}, u32[]{:S(2)}) %all-to-all-start.3) | async-done | bytes 524320 | tf_op jit(solution)/shard_map/all_to_all | solution.py:835
  46.5 1.9 %sum_arrived.3 = (f32[128,8,128]{2,1,0:T(8,128)}, f32[264,8,128]{2,1,0:T(8,128)S(1)}) custom-call(s32[8,128]{1,0:T(8,128)S(1)} %piece_table.3.table, f32[128,8,128]{2,1,0:T(8,128)S(1)} %bitcast.25, f32[264,8,128]{2,1,0:T(8,128)S(1)} %sum_own.3.pieces_in), custom_call_target="tpu_custom_call", output_to_operand_aliasing={{1}: (2, {})} | custom-call | tf_op jit(solution)/shard_map/sum_arrived/pallas_call | solution.py:879
  48.4 3.2 %all-to-all-start.4 = ((f32[32,32,128]{2,1,0:T(8,128)}), f32[32,32,128]{2,1,0:T(8,128)S(1)}, u32[]{:S(2)}, u32[]{:S(2)}) async-start(f32[32,32,128]{2,1,0:T(8,128)} %bitcast.16), calls=%async_computation.4 | async-start | bytes 1048576 | tf_op jit(solution)/shard_map/all_to_all | solution.py:835
  52.3 0.7 %own_back.3 = f32[128,8,128]{2,1,0:T(8,128)S(1)} custom-call(s32[8,128]{1,0:T(8,128)S(1)} %piece_table.3.table, f32[264,8,128]{2,1,0:T(8,128)S(1)} %get-tuple-element.80.pieces), custom_call_target="tpu_custom_call" | custom-call | tf_op jit(solution)/shard_map/own_back/pallas_call | solution.py:888
  53.0 13.9 %all-to-all-done.4 = f32[32,32,128]{2,1,0:T(8,128)S(1)} async-done(((f32[32,32,128]{2,1,0:T(8,128)}), f32[32,32,128]{2,1,0:T(8,128)S(1)}, u32[]{:S(2)}, u32[]{:S(2)}) %all-to-all-start.4) | async-done | bytes 524320 | tf_op jit(solution)/shard_map/all_to_all | solution.py:835
  66.9 1.2 %conditional.1 = (f32[1,16,8192]{2,1,0:T(8,128)S(1)}) conditional(s32[]{:T(128)} %bitcast.12, (s32[256,128]{1,0:T(8,128)S(1)}, f32[16,128]{1,0:T(8,128)S(1)}, f32[64,128]{1,0:T(8,128)S(1)}, s32[1,3]{1,0:T(1,128)S(1)}, f32[1024,128]{1,0:T(8,128)S(1)}, /*index=5*/s32[8,128]{1,0:T(8,128)S(1)}) %tuple.25, (f32[32,32,128]{2,1,0:T(8,128)S(1)}, ...), branch_computations={%region_0.0_spmd, %region_1.0_spmd} | conditional | flops 8192 | bytes 10846388 | solution.py:915
  66.9 1.2 %unpack.3 = f32[16,8192]{1,0:T(8,128)S(1)} custom-call(s32[8,128]{1,0:T(8,128)S(1)} %get-tuple-element.36.info, f32[128,8,128]{2,1,0:T(8,128)S(1)} %bitcast.31, f32[128,8,128]{2,1,0:T(8,128)S(1)} %get-tuple-element.38.own), custom_call_target="tpu_custom_call" | custom-call | tf_op jit(solution)/shard_map/cond/branch_1_fun/unpack/pallas_call | solution.py:899
  68.1 0.0 copy-start.4
  68.1 0.8 %copy-done.4 = f32[1,16,8192]{2,1,0:T(8,128)} copy-done((f32[1,16,8192]{2,1,0:T(8,128)}, f32[1,16,8192]{2,1,0:T(8,128)S(1)}, u32[]{:S(2)}) %copy-start.4) | copy-done | bytes 524312
Async XLA Ops:
  0.7 7.8 %copy-start = (f32[1,16,8192]{2,1,0:T(8,128)S(1)}, f32[1,16,8192]{2,1,0:T(8,128)}, u32[]{:S(2)}) copy-start(f32[1,16,8192]{2,1,0:T(8,128)} %param.9) | copy-start | bytes 1572868
  0.7 7.8 %copy-start.1 = (f32[1,16,8192]{2,1,0:T(8,128)S(1)}, f32[1,16,8192]{2,1,0:T(8,128)}, u32[]{:S(2)}) copy-start(f32[1,16,8192]{2,1,0:T(8,128)} %param.10) | copy-start | bytes 1572868
  1.3 16.6 %copy-start.3 = (f32[4]{0:T(128)S(1)}, f32[4]{0:T(128)}, u32[]{:S(2)}) copy-start(f32[4]{0:T(128)} %refs_1_.1) | copy-start | bytes 52
  1.3 16.6 %copy-start.5 = (s32[1,3]{1,0:T(1,128)S(1)}, s32[1,3]{1,0:T(1,128)}, u32[]{:S(2)}) copy-start(s32[1,3]{1,0:T(1,128)} %refs_0_.1) | copy-start | bytes 40
  1.3 14.4 %all-to-all-start.2 = ((s32[32,8,128]{2,1,0:T(8,128)}), s32[32,8,128]{2,1,0:T(8,128)S(1)}, u32[]{:S(2)}, u32[]{:S(2)}) async-start(s32[32,8,128]{2,1,0:T(8,128)} %bitcast.10), calls=%async_computation.2 | async-start | bytes 262144 | tf_op jit(solution)/shard_map/all_to_all | solution.py:715
  8.7 9.3 %collective-permute-start.3 = (f32[5,64,128]{2,1,0:T(8,128)S(1)}, f32[5,64,128]{2,1,0:T(8,128)S(1)}, u32[]{:S(2)}, u32[]{:S(2)}) collective-permute-start(f32[5,64,128]{2,1,0:T(8,128)S(1)} %get-tuple-element.64), channel_id=1, source_target_pairs={{1,0},{2,1},{3,2},{5,4},{6,5},{7,6},{9,8},{10,9},{11,10},{13,12},{... | collective-permute-start | bytes 491528 | tf_op jit(solution)/shard_map/ppermute | solution.py:734
  10.0 7.9 %collective-permute-start.2 = (f32[3,64,128]{2,1,0:T(8,128)S(1)}, f32[3,64,128]{2,1,0:T(8,128)S(1)}, u32[]{:S(2)}, u32[]{:S(2)}) collective-permute-start(f32[3,64,128]{2,1,0:T(8,128)S(1)} %get-tuple-element.63), channel_id=1, source_target_pairs={{0,1},{1,2},{2,3},{4,5},{5,6},{6,7},{8,9},{9,10},{10,11},{12,13},{... | collective-permute-start | bytes 294920 | tf_op jit(solution)/shard_map/ppermute | solution.py:733
  25.7 20.8 %all-to-all-start.3 = ((f32[32,32,128]{2,1,0:T(8,128)}), f32[32,32,128]{2,1,0:T(8,128)S(1)}, u32[]{:S(2)}, u32[]{:S(2)}) async-start(f32[32,32,128]{2,1,0:T(8,128)} %bitcast.13), calls=%async_computation.3 | async-start | bytes 1048576 | tf_op jit(solution)/shard_map/all_to_all | solution.py:835
  48.4 18.5 %all-to-all-start.4 = ((f32[32,32,128]{2,1,0:T(8,128)}), f32[32,32,128]{2,1,0:T(8,128)S(1)}, u32[]{:S(2)}, u32[]{:S(2)}) async-start(f32[32,32,128]{2,1,0:T(8,128)} %bitcast.16), calls=%async_computation.4 | async-start | bytes 1048576 | tf_op jit(solution)/shard_map/all_to_all | solution.py:835
  68.1 0.8 %copy-start.4 = (f32[1,16,8192]{2,1,0:T(8,128)}, f32[1,16,8192]{2,1,0:T(8,128)S(1)}, u32[]{:S(2)}) copy-start(f32[1,16,8192]{2,1,0:T(8,128)S(1)} %get-tuple-element.95) | copy-start | bytes 1572868

commit v10 on v9

--- a/solution.py
+++ b/solution.py
@@ -74,7 +74,8 @@
         total = total + (ahead + before)
         drift = drift + weights[3] * (ahead - before)
         new = x + dif[j] * (total - 8.0 * x) - drift
-        dst[PAD + j] = jnp.where(valid, new, 0.0)
+        dst[PAD + j, 0:16] = new[0:16]
+        dst[PAD + j, 16:24] = jnp.where(valid, new[16:24], 0.0)
         return nxt, carry_two, carry_three
 
     def start(stride, in_lanes):
@@ -218,7 +219,8 @@
         dif[:, 16 + i] = 0.1 * high[3 + i]
     dif[:, 23] = 0.1 * low[2]
     row = lax.broadcasted_iota(jnp.int32, (24, LANES), 0)
-    valid = (row < 16) | ((row < 20) & (place < count - 1)) | ((row >= 20) & (place > 0))
+    halo_row = lax.broadcasted_iota(jnp.int32, (8, LANES), 0)
+    valid = ((halo_row < 4) & (place < count - 1)) | ((halo_row >= 4) & (place > 0))
     weights = [0.1 * velocity[d] for d in range(4)]
     first_bits = levels[0, 0]
     second_bits = levels[0, 1]
@@ -355,8 +357,10 @@
     )
 
 
-def mixed(handler, lane, row):
-    x = (handler * 40503 + lane * 30011 + row * 52711) & 0xFFFF
+def tie_breakers(devices):
+    handler = lax.broadcasted_iota(jnp.int32, (devices, LANES), 0)
+    lane = lax.broadcasted_iota(jnp.int32, (devices, LANES), 1)
+    x = (handler * 40503 + lane * 30011) & 0xFFFF
     x = ((x ^ (x >> 7)) * 9973) & 0xFFFF
     x = ((x ^ (x >> 5)) * 12347) & 0xFFFF
     return (x >> 8).astype(jnp.float32) * (1.0 / 256.0)
@@ -460,6 +464,7 @@
         self.devices, self.capacity, self.full = devices, capacity, full
         self.rows = devices * SLOTS // LANES
         self.deep = devices + 8
+        self.ties = 0.5 * tie_breakers(devices)
 
     def own(self):
         square = (self.devices, self.deep)
@@ -486,15 +491,19 @@
         )
         shape = (devices, group * LANES)
         handler = lax.broadcasted_iota(jnp.int32, shape, 0)
-        column = lax.broadcasted_iota(jnp.int32, shape, 1)
         handler_f = handler.astype(jnp.float32)
-        cost = dot_plain(self.price(load, 4.0 if first else 16.0), counts)
         was = None
-        if not first:
+        if first:
+            cost = dot_plain(self.price(load, 4.0), counts)
+        else:
             old = jnp.concatenate([table[pl.ds(base + i, 1), :] for i in range(group)], axis=1)
             was = handler_f == old
-            cost = jnp.where(was, dot_plain(self.price(load - 1.0, 16.0), counts) - 5.0, cost)
-        noise = 0.5 * mixed(handler, column % LANES, base + column // LANES)
+            prices = jnp.concatenate([self.price(load, 16.0), self.price(load - 1.0, 16.0)], axis=0)
+            costs = dot_plain(prices, counts)
+            cost = jnp.where(was, costs[devices:] - 5.0, costs[:devices])
+        noise = jnp.concatenate(
+            [pltpu.roll(self.ties, (base + i) * 37 % LANES, 1) for i in range(group)], axis=1
+        )
         ranked = jnp.floor((jnp.minimum(cost, 4000.0) + noise) * 64.0) * devices + handler_f
         least = jnp.min(ranked, axis=0, keepdims=True)
         chosen = least - jnp.floor(least * (1.0 / devices)) * devices
@@ -533,17 +542,18 @@
             )
 
         def worst(load):
-            return jnp.max(jnp.where(own, 0.0, load))
+            too_many = jnp.where((sender >= devices) & (load > MOST_KEYS), 1000.0, 0.0)
+            return jnp.max(jnp.where(own, too_many, load))
 
         def again(state):
             count, _, load = state
             load = lax.cond(count == 0, lambda x: sweep(4, x), lambda x: sweep(2, x), load)
             return count + 1, worst(load), load
 
-        _, most, load = lax.while_loop(
+        _, most, _ = lax.while_loop(
             lambda state: (state[0] < 6) & (state[1] > capacity), again, (0, worst(load), load)
         )
-        ok = (most <= capacity) & (jnp.max(jnp.where(sender < devices, 0.0, load)) <= MOST_KEYS)
+        ok = most <= capacity
         good[0] = ok.astype(jnp.int32)
         tell.start()
         from_row, lane = self.from_row()
@@ -659,13 +669,25 @@
         pieces[piece] = pieces[piece] - 0.5 * own[i % 8]
 
 
-def sum_kernel(table, arrived, pieces_in, out, pieces):
+def part_copies(src, dst, sems):
+    size = src.shape[0] // sems.shape[0]
+    parts = [pl.ds(k * size, size) for k in range(sems.shape[0])]
+    return [pltpu.make_async_copy(src.at[p], dst.at[p], sems.at[k]) for k, p in enumerate(parts)]
+
+
+def sum_kernel(table, arrived, pieces_in, out, pieces, held, sems):
     places = arrived.shape[0]
     for i in range(places):
         piece = table[i // LANES, i % LANES]
         pieces[piece] = pieces[piece] + arrived[i]
-    for i in range(places):
-        out[i] = pieces[table[i // LANES, i % LANES]]
+    copies = part_copies(held, out, sems)
+    size = places // len(copies)
+    for k, copy in enumerate(copies):
+        for i in range(k * size, (k + 1) * size):
+            held[i] = pieces[table[i // LANES, i % LANES]]
+        copy.start()
+    for copy in copies:
+        copy.wait()
 
 
 def own_back_kernel(table, pieces, out, *, arrive_rows):
@@ -880,8 +902,12 @@
             sum_kernel,
             out_shape=(f32(devices * slots, 8, LANES), all_pieces),
             in_specs=[SM, VM, VM],
-            out_specs=(VM, VM),
+            out_specs=(HBM, VM),
             input_output_aliases={2: 1},
+            scratch_shapes=[
+                pltpu.VMEM((devices * slots, 8, LANES), jnp.float32),
+                pltpu.SemaphoreType.DMA((4,)),
+            ],
             compiler_params=params(),
             name="sum_arrived",
         )(table, arrived, started)

time: 70 us -> 69.4 us (level)
  no operation moved by 1% of the time
where the time goes in v10:
time: 69.4 us; the launch traced here: 68.8 us
  waiting for transfers between devices  28 us (40%)
  starting transfers between devices  21 us (30%)
  Pallas kernels  16.9 us (24%)
  between operations  1.47 us (2%)
  local copies, waits for them, and re-layouts  0.8 us (1%)
    all_to_all x2, waiting for transfers between devices, exchange(): lax.all_to_all(x.reshape(devices, slots * 8, LANES), ('grid', 'dom'), spl...  26.8 us
    all_to_all x2, starting transfers between devices, exchange(): lax.all_to_all(x.reshape(devices, slots * 8, LANES), ('grid', 'dom'), spl...  8.63 us
    pallas_call x1, Pallas kernels, body(): row_call(functools.partial(rows_kernel, extras=extras, balance=balance),...  7.77 us
    all_to_all x1, starting transfers between devices, body(): lax.all_to_all(spread.reshape(devices, COPIES, blocks), ('grid', 'dom'),...  7.1 us
    ppermute x1, starting transfers between devices, body(): low = lax.ppermute(low_rows, 'dom', up)  3.99 us
    pallas_call x1, Pallas kernels, body(): pl.pallas_call(functools.partial(first_rounds_kernel, **balance), out_sha...  2.13 us
    pallas_call x1, Pallas kernels, route(): pl.pallas_call(sum_kernel, out_shape=(f32(devices * slots, 8, LANES), all...  1.9 us
    pallas_call x1, Pallas kernels, route(): pl.pallas_call(functools.partial(own_sum_kernel, arrive_rows=arrive_rows,...  1.5 us
  transfers between devices with their start and end apart: 5, of which 3 were waited for; matrix products, arithmetic and copies ran while one was open for 0% of the time, Pallas kernels for 8%

profile of v10, /device:TPU:1, one launch (start us, length us, event | category | flops | bytes accessed | tf_op | source)
XLA Modules:
  0.0 68.8 jit_solution(7139446122722245906)
XLA Ops:
  0.0 0.7 multiply_add_fusion.keys
  0.7 0.0 copy-start
  0.7 0.0 copy-start.1
  0.7 0.7 spread_keys.1
  1.3 0.0 copy-start.3
  1.3 0.0 copy-start.5
  1.3 7.1 %all-to-all-start.2 = ((s32[32,8,128]{2,1,0:T(8,128)}), s32[32,8,128]{2,1,0:T(8,128)S(1)}, u32[]{:S(2)}, u32[]{:S(2)}) async-start(s32[32,8,128]{2,1,0:T(8,128)} %bitcast.10), calls=%async_computation.2 | async-start | bytes 262144 | tf_op jit(solution)/shard_map/all_to_all | solution.py:737
  8.5 0.0 copy-done
  8.5 0.0 copy-done.1
  8.5 0.2 halo_rows.1
  8.7 1.3 %collective-permute-start.3 = (f32[5,64,128]{2,1,0:T(8,128)S(1)}, f32[5,64,128]{2,1,0:T(8,128)S(1)}, u32[]{:S(2)}, u32[]{:S(2)}) collective-permute-start(f32[5,64,128]{2,1,0:T(8,128)S(1)} %get-tuple-element.64), channel_id=1, source_target_pairs={{1,0},{2,1},{3,2},{5,4},{6,5},{7,6},{9,8},{10,9},{11,10},{13,12},{... | collective-permute-start | bytes 491528 | tf_op jit(solution)/shard_map/ppermute | solution.py:756
  10.0 4.0 %collective-permute-start.2 = (f32[3,64,128]{2,1,0:T(8,128)S(1)}, f32[3,64,128]{2,1,0:T(8,128)S(1)}, u32[]{:S(2)}, u32[]{:S(2)}) collective-permute-start(f32[3,64,128]{2,1,0:T(8,128)S(1)} %get-tuple-element.63), channel_id=1, source_target_pairs={{0,1},{1,2},{2,3},{4,5},{5,6},{6,7},{8,9},{9,10},{10,11},{12,13},{... | collective-permute-start | bytes 294920 | tf_op jit(solution)/shard_map/ppermute | solution.py:755
  14.6 1.2 %all-to-all-done.2 = s32[32,8,128]{2,1,0:T(8,128)S(1)} async-done(((s32[32,8,128]{2,1,0:T(8,128)}), s32[32,8,128]{2,1,0:T(8,128)S(1)}, u32[]{:S(2)}, u32[]{:S(2)}) %all-to-all-start.2) | async-done | bytes 131104 | tf_op jit(solution)/shard_map/all_to_all | solution.py:737
  15.8 2.1 %first_rounds.1 = (f32[640,128]{1,0:T(8,128)S(1)}, f32[16,128]{1,0:T(8,128)S(1)}, f32[32,40]{1,0:T(8,128)S(1)}) custom-call(s32[256,128]{1,0:T(8,128)S(1)} %bitcast.27), custom_call_target="tpu_custom_call" | custom-call | tf_op jit(solution)/shard_map/first_rounds/pallas_call | solution.py:783
  17.9 0.0 collective-permute-done.2.refs_6_
  17.9 0.0 collective-permute-done.3.refs_7_
  17.9 0.0 copy-done.3
  17.9 0.0 copy-done.5
  17.9 7.8 %rows.1 = (f32[1024,128]{1,0:T(8,128)S(1)}, f32[64,128]{1,0:T(8,128)S(1)}, f32[128,8,128]{2,1,0:T(8,128)}, f32[16,128]{1,0:T(8,128)S(1)}, s32[8,128]{1,0:T(8,128)S(1)}, /*index=5*/s32[1]{0:T(128)}) custom-call(s32[1,3]{1,0:T(1,128)S(1)} %copy-done.5, f32[4]{0:T(128)S(1)} %copy-done.3, s32[1]{0:T(128)S(6)} %copy.16.refs_2_, s32[256,128]{1,0:T(8,128)S(1)} %bitcast.28, ...), custom_call_target="tpu_custom_call" | custom-call | tf_op jit(solution)/shard_map/rows/pallas_call | solution.py:798
  25.7 5.5 %all-to-all-start.3 = ((f32[32,32,128]{2,1,0:T(8,128)}), f32[32,32,128]{2,1,0:T(8,128)S(1)}, u32[]{:S(2)}, u32[]{:S(2)}) async-start(f32[32,32,128]{2,1,0:T(8,128)} %bitcast.13), calls=%async_computation.3 | async-start | bytes 1048576 | tf_op jit(solution)/shard_map/all_to_all | solution.py:857
  31.2 0.9 %piece_table.3.table = s32[8,128]{1,0:T(8,128)S(1)} custom-call(s32[256,128]{1,0:T(8,128)S(1)} %bitcast.29, f32[16,128]{1,0:T(8,128)S(1)} %get-tuple-element.74.refs_1_), custom_call_target="tpu_custom_call" | custom-call | tf_op jit(solution)/shard_map/piece_table/pallas_call | solution.py:876
  32.1 1.5 %sum_own.3.pieces_in = f32[264,8,128]{2,1,0:T(8,128)S(1)} custom-call(s32[8,128]{1,0:T(8,128)S(1)} %piece_table.3.table, f32[128,8,128]{2,1,0:T(8,128)S(1)} %bitcast.32), custom_call_target="tpu_custom_call" | custom-call | tf_op jit(solution)/shard_map/sum_own/pallas_call | solution.py:893
  33.6 12.9 %all-to-all-done.3 = f32[32,32,128]{2,1,0:T(8,128)S(1)} async-done(((f32[32,32,128]{2,1,0:T(8,128)}), f32[32,32,128]{2,1,0:T(8,128)S(1)}, u32[]{:S(2)}, u32[]{:S(2)}) %all-to-all-start.3) | async-done | bytes 524320 | tf_op jit(solution)/shard_map/all_to_all | solution.py:857
  46.5 1.9 %sum_arrived.3 = (f32[128,8,128]{2,1,0:T(8,128)}, f32[264,8,128]{2,1,0:T(8,128)S(1)}) custom-call(s32[8,128]{1,0:T(8,128)S(1)} %piece_table.3.table, f32[128,8,128]{2,1,0:T(8,128)S(1)} %bitcast.25, f32[264,8,128]{2,1,0:T(8,128)S(1)} %sum_own.3.pieces_in), custom_call_target="tpu_custom_call", output_to_operand_aliasing={{1}: (2, {})} | custom-call | tf_op jit(solution)/shard_map/sum_arrived/pallas_call | solution.py:901
  48.4 3.1 %all-to-all-start.4 = ((f32[32,32,128]{2,1,0:T(8,128)}), f32[32,32,128]{2,1,0:T(8,128)S(1)}, u32[]{:S(2)}, u32[]{:S(2)}) async-start(f32[32,32,128]{2,1,0:T(8,128)} %bitcast.16), calls=%async_computation.4 | async-start | bytes 1048576 | tf_op jit(solution)/shard_map/all_to_all | solution.py:857
  52.2 0.7 %own_back.3 = f32[128,8,128]{2,1,0:T(8,128)S(1)} custom-call(s32[8,128]{1,0:T(8,128)S(1)} %piece_table.3.table, f32[264,8,128]{2,1,0:T(8,128)S(1)} %get-tuple-element.80.pieces), custom_call_target="tpu_custom_call" | custom-call | tf_op jit(solution)/shard_map/own_back/pallas_call | solution.py:914
  53.0 13.9 %all-to-all-done.4 = f32[32,32,128]{2,1,0:T(8,128)S(1)} async-done(((f32[32,32,128]{2,1,0:T(8,128)}), f32[32,32,128]{2,1,0:T(8,128)S(1)}, u32[]{:S(2)}, u32[]{:S(2)}) %all-to-all-start.4) | async-done | bytes 524320 | tf_op jit(solution)/shard_map/all_to_all | solution.py:857
  66.9 1.2 %conditional.1 = (f32[1,16,8192]{2,1,0:T(8,128)S(1)}) conditional(s32[]{:T(128)} %bitcast.12, (s32[256,128]{1,0:T(8,128)S(1)}, f32[16,128]{1,0:T(8,128)S(1)}, f32[64,128]{1,0:T(8,128)S(1)}, s32[1,3]{1,0:T(1,128)S(1)}, f32[1024,128]{1,0:T(8,128)S(1)}, /*index=5*/s32[8,128]{1,0:T(8,128)S(1)}) %tuple.25, (f32[32,32,128]{2,1,0:T(8,128)S(1)}, ...), branch_computations={%region_0.0_spmd, %region_1.0_spmd} | conditional | flops 8192 | bytes 10846388 | solution.py:941
  66.9 1.2 %unpack.3 = f32[16,8192]{1,0:T(8,128)S(1)} custom-call(s32[8,128]{1,0:T(8,128)S(1)} %get-tuple-element.36.info, f32[128,8,128]{2,1,0:T(8,128)S(1)} %bitcast.31, f32[128,8,128]{2,1,0:T(8,128)S(1)} %get-tuple-element.38.own), custom_call_target="tpu_custom_call" | custom-call | tf_op jit(solution)/shard_map/cond/branch_1_fun/unpack/pallas_call | solution.py:925
  68.0 0.0 copy-start.4
  68.1 0.8 %copy-done.4 = f32[1,16,8192]{2,1,0:T(8,128)} copy-done((f32[1,16,8192]{2,1,0:T(8,128)}, f32[1,16,8192]{2,1,0:T(8,128)S(1)}, u32[]{:S(2)}) %copy-start.4) | copy-done | bytes 524312
Async XLA Ops:
  0.7 7.8 %copy-start = (f32[1,16,8192]{2,1,0:T(8,128)S(1)}, f32[1,16,8192]{2,1,0:T(8,128)}, u32[]{:S(2)}) copy-start(f32[1,16,8192]{2,1,0:T(8,128)} %param.9) | copy-start | bytes 1572868
  0.7 7.8 %copy-start.1 = (f32[1,16,8192]{2,1,0:T(8,128)S(1)}, f32[1,16,8192]{2,1,0:T(8,128)}, u32[]{:S(2)}) copy-start(f32[1,16,8192]{2,1,0:T(8,128)} %param.10) | copy-start | bytes 1572868
  1.3 16.6 %copy-start.3 = (f32[4]{0:T(128)S(1)}, f32[4]{0:T(128)}, u32[]{:S(2)}) copy-start(f32[4]{0:T(128)} %refs_1_.1) | copy-start | bytes 52
  1.3 16.6 %copy-start.5 = (s32[1,3]{1,0:T(1,128)S(1)}, s32[1,3]{1,0:T(1,128)}, u32[]{:S(2)}) copy-start(s32[1,3]{1,0:T(1,128)} %refs_0_.1) | copy-start | bytes 40
  1.3 14.4 %all-to-all-start.2 = ((s32[32,8,128]{2,1,0:T(8,128)}), s32[32,8,128]{2,1,0:T(8,128)S(1)}, u32[]{:S(2)}, u32[]{:S(2)}) async-start(s32[32,8,128]{2,1,0:T(8,128)} %bitcast.10), calls=%async_computation.2 | async-start | bytes 262144 | tf_op jit(solution)/shard_map/all_to_all | solution.py:737
  8.7 9.3 %collective-permute-start.3 = (f32[5,64,128]{2,1,0:T(8,128)S(1)}, f32[5,64,128]{2,1,0:T(8,128)S(1)}, u32[]{:S(2)}, u32[]{:S(2)}) collective-permute-start(f32[5,64,128]{2,1,0:T(8,128)S(1)} %get-tuple-element.64), channel_id=1, source_target_pairs={{1,0},{2,1},{3,2},{5,4},{6,5},{7,6},{9,8},{10,9},{11,10},{13,12},{... | collective-permute-start | bytes 491528 | tf_op jit(solution)/shard_map/ppermute | solution.py:756
  10.0 7.9 %collective-permute-start.2 = (f32[3,64,128]{2,1,0:T(8,128)S(1)}, f32[3,64,128]{2,1,0:T(8,128)S(1)}, u32[]{:S(2)}, u32[]{:S(2)}) collective-permute-start(f32[3,64,128]{2,1,0:T(8,128)S(1)} %get-tuple-element.63), channel_id=1, source_target_pairs={{0,1},{1,2},{2,3},{4,5},{5,6},{6,7},{8,9},{9,10},{10,11},{12,13},{... | collective-permute-start | bytes 294920 | tf_op jit(solution)/shard_map/ppermute | solution.py:755
  25.7 20.8 %all-to-all-start.3 = ((f32[32,32,128]{2,1,0:T(8,128)}), f32[32,32,128]{2,1,0:T(8,128)S(1)}, u32[]{:S(2)}, u32[]{:S(2)}) async-start(f32[32,32,128]{2,1,0:T(8,128)} %bitcast.13), calls=%async_computation.3 | async-start | bytes 1048576 | tf_op jit(solution)/shard_map/all_to_all | solution.py:857
  48.4 18.4 %all-to-all-start.4 = ((f32[32,32,128]{2,1,0:T(8,128)}), f32[32,32,128]{2,1,0:T(8,128)S(1)}, u32[]{:S(2)}, u32[]{:S(2)}) async-start(f32[32,32,128]{2,1,0:T(8,128)} %bitcast.16), calls=%async_computation.4 | async-start | bytes 1048576 | tf_op jit(solution)/shard_map/all_to_all | solution.py:857
  68.0 0.8 %copy-start.4 = (f32[1,16,8192]{2,1,0:T(8,128)}, f32[1,16,8192]{2,1,0:T(8,128)S(1)}, u32[]{:S(2)}) copy-start(f32[1,16,8192]{2,1,0:T(8,128)S(1)} %get-tuple-element.95) | copy-start | bytes 1572868
